TPU v7x, 32 devices: a whole 2x2x4 slice. The times are simulated.
32 devices in a mesh: seq: 8 (over y, x, core), fsdp: 4 (over z).
Axes of the slice: x: 2, y: 2, z: 4, core: 2. Of those that a mesh axis runs over, the one named last changes fastest.
Arguments:
- tokens: bfloat16 [4, 2048, 1600], P('fsdp', 'seq'), may hold values from -6 to 6
- doc_ids: int32 [4, 2048], P('fsdp', 'seq'), may hold values from 0 to 1, never falling along the last dimension, each value on 1 to 1792 neighbouring positions
- in_weight: bfloat16 [1600, 8640], P('fsdp', 'seq'), may hold values from -0.15625 to 0.15625
- out_weight: bfloat16 [4800, 1600], P('fsdp', 'seq'), may hold values from -0.1875 to 0.1875
- gate_up: bfloat16 [1600, 11008], P('fsdp', 'seq'), may hold values from -0.15625 to 0.15625
- down_weight: bfloat16 [5504, 1600], P('fsdp', 'seq'), may hold values from -0.109375 to 0.109375
- select_weight: bfloat16 [132, 3200], P('fsdp', 'seq'), may hold values from -0.109375 to 0.109375
- step_weight: bfloat16 [100, 3200], P('fsdp', 'seq'), may hold values from -0.625 to 0.625
- first_gain: float32 [1600], replicated, may hold values from 0.25 to 1.75
- second_gain: float32 [1600], replicated, may hold values from 0.25 to 1.75
- attn_gain: float32 [1600], replicated, may hold values from 0.25 to 1.75
- mamba_gain: float32 [3200], replicated, may hold values from 0.25 to 1.75
- conv_weight: float32 [4, 3200], replicated, may hold values from -3 to 3
- conv_bias: float32 [3200], replicated, may hold values from -3 to 3
- step_bias: float32 [3200], replicated, may hold values from -7 to -2.5
- decay_log: float32 [16, 3200], replicated, may hold values from -3 to 2.5
- skip_gain: float32 [3200], replicated, may hold values from 0.5 to 1.5
- cotangent: bfloat16 [4, 2048, 1600], P('fsdp', 'seq'), may hold values from -6 to 6
Outputs:
- out_tokens: bfloat16 [4, 2048, 1600], P('fsdp', 'seq')
- tokens_grad: bfloat16 [4, 2048, 1600], P('fsdp', 'seq')
- in_grad: float32 [1600, 8640], P('fsdp', 'seq')
- out_grad: float32 [4800, 1600], P('fsdp', 'seq')
- gate_up_grad: float32 [1600, 11008], P('fsdp', 'seq')
- down_grad: float32 [5504, 1600], P('fsdp', 'seq')
- select_grad: float32 [132, 3200], P('fsdp', 'seq')
- step_weight_grad: float32 [100, 3200], P('fsdp', 'seq')
- first_gain_grad: float32 [1600], replicated
- second_gain_grad: float32 [1600], replicated
- attn_gain_grad: float32 [1600], replicated
- mamba_gain_grad: float32 [3200], replicated
- conv_weight_grad: float32 [4, 3200], replicated
- conv_bias_grad: float32 [3200], replicated
- step_bias_grad: float32 [3200], replicated
- decay_log_grad: float32 [16, 3200], replicated
- skip_gain_grad: float32 [3200], replicated
Inputs may be any that keep to these rules, and one draw needn't show every extreme that they name: Along each group doc_ids never falls and starts at 0; each value labels one run of 1 to 2048 - 256 * (1) tokens.
All inputs are finite; a program needn't handle non-finite values.
Results may differ from a plain program's by a relative error of at most 0.02.
Values may be sent and summed in bfloat16 or wider, within the bound.
A program may use at most 448 MiB of HBM per device.

v0:
```python
import math

import jax
import jax.numpy as jnp
from jax import lax
from jax.sharding import PartitionSpec as P

QUERY_HEADS = 25
KEY_VALUE_HEADS = 5
HEAD_SIZE = 64
DI = 3200
NS = 16
DTR = 100
KC = 4
F = 5504
WINDOW_TOKENS = 1024


norm_eps = 1e-05
masked_score = -1e30


def from_behind(block, axis, distance):
    devices = range(lax.axis_size(axis))
    route = [(i - distance, i) for i in devices if i - distance in devices]
    return lax.ppermute(block, axis, route)


def matmul(left, right):
    return jnp.dot(left, right, preferred_element_type=jnp.float32)


def dot_tn(left, right):
    return lax.dot_general(
        left, right, (((0,), (0,)), ((), ())), preferred_element_type=jnp.float32
    )


def dot_nt(left, right):
    return lax.dot_general(
        left, right, (((1,), (1,)), ((), ())), preferred_element_type=jnp.float32
    )


def rms_norm(value, gain):
    scale = lax.rsqrt(jnp.mean(value * value, axis=-1, keepdims=True) + norm_eps)
    return (value * scale * gain, scale)


def norm_back(value, scale, gain, upstream):
    weighted = upstream * gain
    gain_grad = jnp.sum(upstream * value * scale, 0)
    inner_mean = jnp.mean(weighted * value, axis=-1, keepdims=True)
    return (scale * weighted - value * (scale * scale * scale) * inner_mean, gain_grad)


def combine_pair(earlier, later):
    return (earlier[0] * later[0], later[0] * earlier[1] + later[1])


def block_states(step_blk, input_blk, b_blk, keep_blk, decay_rate, start_state):
    decays = jnp.exp(step_blk[:, None, :] * decay_rate[None]) * keep_blk[:, None, None]
    pushes = (step_blk * input_blk)[:, None, :] * b_blk[:, :, None]
    first_push = pushes[0] + decays[0] * start_state
    pushes = jnp.concatenate([first_push[None], pushes[1:]], 0)
    _, states = lax.associative_scan(combine_pair, (decays, pushes))
    return (decays, states)


def gather_weights(in_weight, out_weight, gate_up, down_weight, select_weight, step_weight):
    row_parts = (
        lax.all_gather(in_weight, "fsdp", axis=0, tiled=True),
        lax.all_gather(out_weight, "fsdp", axis=0, tiled=True),
        lax.all_gather(gate_up, "fsdp", axis=0, tiled=True),
        lax.all_gather(down_weight, "fsdp", axis=0, tiled=True),
        lax.all_gather(select_weight, "fsdp", axis=0, tiled=True),
        lax.all_gather(step_weight, "fsdp", axis=0, tiled=True),
    )
    return (
        lax.all_gather(row_parts[0], "seq", axis=1, tiled=True),
        lax.all_gather(row_parts[1], "seq", axis=1, tiled=True),
        lax.all_gather(row_parts[2], "seq", axis=1, tiled=True),
        lax.all_gather(row_parts[3], "seq", axis=1, tiled=True),
        lax.all_gather(row_parts[4], "seq", axis=1, tiled=True),
        lax.all_gather(row_parts[5], "seq", axis=1, tiled=True),
    )


def reduce_terms(first_term, second_term, third_term):
    col_parts = (
        lax.psum_scatter(
            first_term.astype(jnp.bfloat16), "seq", scatter_dimension=1, tiled=True
        ).astype(jnp.float32),
        lax.psum_scatter(
            second_term.astype(jnp.bfloat16), "seq", scatter_dimension=1, tiled=True
        ).astype(jnp.float32),
        lax.psum_scatter(
            third_term.astype(jnp.bfloat16), "seq", scatter_dimension=1, tiled=True
        ).astype(jnp.float32),
    )
    return (
        lax.psum_scatter(
            col_parts[0].astype(jnp.bfloat16), "fsdp", scatter_dimension=0, tiled=True
        ).astype(jnp.float32),
        lax.psum_scatter(
            col_parts[1].astype(jnp.bfloat16), "fsdp", scatter_dimension=0, tiled=True
        ).astype(jnp.float32),
        lax.psum_scatter(
            col_parts[2].astype(jnp.bfloat16), "fsdp", scatter_dimension=0, tiled=True
        ).astype(jnp.float32),
    )


def shards(
    tokens,
    doc_ids,
    in_weight,
    out_weight,
    gate_up,
    down_weight,
    select_weight,
    step_weight,
    first_gain,
    second_gain,
    attn_gain,
    mamba_gain,
    conv_weight,
    conv_bias,
    step_bias,
    decay_log,
    skip_gain,
    cotangent,
):
    gathered = gather_weights(
        in_weight, out_weight, gate_up, down_weight, select_weight, step_weight
    )
    full_in, full_out, full_gate_up, full_down, full_select, full_step = gathered
    seq_x = tokens[0].astype(jnp.float32)
    own_ids = doc_ids[0]
    token_length = seq_x.shape[0]
    query_w = QUERY_HEADS * HEAD_SIZE
    key_weight = KEY_VALUE_HEADS * HEAD_SIZE
    query_groups = QUERY_HEADS // KEY_VALUE_HEADS
    normed_one, scale_one = rms_norm(seq_x, first_gain)
    normed_one = normed_one.astype(jnp.bfloat16)
    projected = matmul(normed_one, full_in).astype(jnp.bfloat16)
    query_rows = projected[:, :query_w]
    key_vals = projected[:, query_w : query_w + 2 * key_weight]
    inputs_b = projected[:, query_w + 2 * key_weight : query_w + 2 * key_weight + DI]
    gate_z = projected[:, query_w + 2 * key_weight + DI :].astype(jnp.float32)
    reach_shards = (WINDOW_TOKENS + token_length - 2) // token_length
    near_kv, near_ids, near_tail = from_behind(
        (key_vals, own_ids, inputs_b[token_length - (KC - 1) :]), "seq", 1
    )
    kv_parts = [near_kv]
    id_parts = [near_ids]
    for back_index in range(2, reach_shards + 1):
        far_kv, far_ids = from_behind((key_vals, own_ids), "seq", back_index)
        kv_parts = [far_kv] + kv_parts
        id_parts = [far_ids] + id_parts
    every_key_value = jnp.concatenate(kv_parts + [key_vals], 0)
    all_ids = jnp.concatenate(id_parts + [own_ids], 0)
    count_of_keys = every_key_value.shape[0]
    base_pos = lax.axis_index("seq") * token_length
    query_pos = base_pos + jnp.arange(token_length, dtype=jnp.int32)
    key_pos = base_pos - reach_shards * token_length + jnp.arange(count_of_keys, dtype=jnp.int32)
    offset = query_pos[:, None] - key_pos[None, :]
    allowed = (
        (offset >= 0)
        & (offset < WINDOW_TOKENS)
        & (key_pos[None, :] >= 0)
        & (own_ids[:, None] == all_ids[None, :])
    )
    heads_of_queries = query_rows.reshape(token_length, KEY_VALUE_HEADS, query_groups, HEAD_SIZE)
    heads_of_keys = every_key_value[:, :key_weight].reshape(
        count_of_keys, KEY_VALUE_HEADS, HEAD_SIZE
    )
    heads_of_values = every_key_value[:, key_weight:].reshape(
        count_of_keys, KEY_VALUE_HEADS, HEAD_SIZE
    )
    score_scale = HEAD_SIZE ** (-0.5)

    def head_scores(index_of_head):
        raw_scores = (
            jnp.einsum(
                "qgd,kd->gqk",
                heads_of_queries[:, index_of_head],
                heads_of_keys[:, index_of_head],
                preferred_element_type=jnp.float32,
            )
            * score_scale
        )
        return jnp.where(allowed[None], raw_scores, masked_score)

    attn_parts = []
    lse_parts = []
    for index_of_head in range(KEY_VALUE_HEADS):
        scores = head_scores(index_of_head)
        row_max = jnp.max(scores, -1, keepdims=True)
        exp_scores = jnp.exp(scores - row_max)
        row_total = jnp.sum(exp_scores, -1, keepdims=True)
        lse_parts.append(row_max + jnp.log(row_total))
        head_probs = (exp_scores / row_total).astype(jnp.bfloat16)
        attn_parts.append(
            jnp.einsum(
                "gqk,kd->qgd",
                head_probs,
                heads_of_values[:, index_of_head],
                preferred_element_type=jnp.float32,
            )
        )
    attended = jnp.stack(attn_parts, 1).reshape(token_length, query_w)
    ext_inputs = jnp.concatenate([near_tail, inputs_b], 0).astype(jnp.float32)
    ext_ids = jnp.concatenate([near_ids[token_length - (KC - 1) :], own_ids], 0)
    conv_sum = jnp.zeros((token_length, DI), jnp.float32) + conv_bias
    same_masks = []
    for tap_index in range(KC):
        begin_row = KC - 1 - tap_index
        same_doc = (ext_ids[begin_row : begin_row + token_length] == own_ids).astype(jnp.float32)[
            :, None
        ]
        same_masks.append(same_doc)
        conv_sum = (
            conv_sum
            + conv_weight[tap_index] * ext_inputs[begin_row : begin_row + token_length] * same_doc
        )
    activated_b = jax.nn.silu(conv_sum).astype(jnp.bfloat16)
    activated = activated_b.astype(jnp.float32)
    selected = dot_nt(activated_b, full_select)
    step_raw = selected[:, :DTR].astype(jnp.bfloat16)
    b_in = selected[:, DTR : DTR + NS]
    c_out = selected[:, DTR + NS :]
    step_pre = matmul(step_raw, full_step) + step_bias
    step_size = jax.nn.softplus(step_pre)
    decay_rate = -jnp.exp(decay_log)
    previous_ids = jnp.concatenate([near_ids[token_length - 1 :], own_ids[:-1]], 0)
    keep_state = (own_ids == previous_ids).astype(jnp.float32)
    block_len = math.gcd(token_length, 32)
    block_count = token_length // block_len

    def split_blocks(value):
        return value.reshape((block_count, block_len) + value.shape[1:])

    def forward_block(carry_state, pieces):
        step_blk, input_blk, b_blk, c_blk, keep_blk = pieces
        _, states = block_states(step_blk, input_blk, b_blk, keep_blk, decay_rate, carry_state)
        return (states[-1], (jnp.sum(c_blk[:, :, None] * states, 1), carry_state))

    scan_pieces = (
        split_blocks(step_size),
        split_blocks(activated),
        split_blocks(b_in),
        split_blocks(c_out),
        split_blocks(keep_state),
    )
    zero_state = jnp.zeros((NS, DI), jnp.float32)
    local_end, (local_out, block_starts) = lax.scan(forward_block, zero_state, scan_pieces)
    step_total = jnp.cumsum(step_size, 0)
    reset_count = jnp.cumsum(1.0 - keep_state)
    alive_now = (reset_count == 0.0).astype(jnp.float32)
    alive_before = (reset_count == 1.0 - keep_state).astype(jnp.float32)
    total_decay = (
        jnp.exp(decay_rate * step_total[token_length - 1][None, :]) * alive_now[token_length - 1]
    )

    def relay_forward(turn, carried):
        return from_behind(total_decay * carried + local_end, "seq", 1)

    state_in = lax.fori_loop(0, lax.axis_size("seq") - 1, relay_forward, zero_state)

    def reach_decay(total_blk, alive_blk):
        return jnp.exp(total_blk[:, None, :] * decay_rate[None]) * alive_blk[:, None, None]

    def correct_block(pieces):
        total_blk, alive_blk, c_blk = pieces
        return jnp.sum(c_blk[:, :, None] * reach_decay(total_blk, alive_blk) * state_in[None], 1)

    correction = lax.map(
        correct_block, (split_blocks(step_total), split_blocks(alive_now), split_blocks(c_out))
    ).reshape(token_length, DI)
    mamba_pre = local_out.reshape(token_length, DI) + correction + skip_gain * activated
    gate_sig = jax.nn.sigmoid(gate_z)
    mamba_out = mamba_pre * gate_z * gate_sig
    attn_normed, attn_scale = rms_norm(attended, attn_gain)
    mamba_normed, mamba_scale = rms_norm(mamba_out, mamba_gain)
    joined = jnp.concatenate([attn_normed, mamba_normed], 1).astype(jnp.bfloat16)
    hidden = seq_x + 0.5 * matmul(joined, full_out)
    normed_two, scale_two = rms_norm(hidden, second_gain)
    normed_two = normed_two.astype(jnp.bfloat16)
    gate_up_out = matmul(normed_two, full_gate_up).astype(jnp.bfloat16)
    gate_part = gate_up_out[:, :F].astype(jnp.float32)
    up_part = gate_up_out[:, F:].astype(jnp.float32)
    gate_act = jax.nn.sigmoid(gate_part)
    inner = (gate_part * gate_act * up_part).astype(jnp.bfloat16)
    out_tokens = (hidden + matmul(inner, full_down)).astype(jnp.bfloat16)
    d_out = cotangent[0].astype(jnp.float32)
    d_ffn = d_out.astype(jnp.bfloat16)
    down_term = dot_tn(inner, d_ffn)
    d_inner = dot_nt(d_ffn, full_down)
    d_gate_up = jnp.concatenate(
        [
            d_inner * up_part * gate_act * (1.0 + gate_part * (1.0 - gate_act)),
            d_inner * gate_part * gate_act,
        ],
        1,
    ).astype(jnp.bfloat16)
    gate_up_term = dot_tn(normed_two, d_gate_up)
    d_hidden_part, second_grad = norm_back(
        hidden, scale_two, second_gain, dot_nt(d_gate_up, full_gate_up)
    )
    d_hidden = d_out + d_hidden_part
    d_mixed = d_hidden.astype(jnp.bfloat16)
    out_term = 0.5 * dot_tn(joined, d_mixed)
    down_sum, gate_up_sum, out_sum = reduce_terms(down_term, gate_up_term, out_term)
    d_joined = 0.5 * dot_nt(d_mixed, full_out)
    attended_gradient, attn_grad = norm_back(attended, attn_scale, attn_gain, d_joined[:, :query_w])
    d_mamba, mamba_grad = norm_back(mamba_out, mamba_scale, mamba_gain, d_joined[:, query_w:])
    heads_gradient = attended_gradient.astype(jnp.bfloat16).reshape(
        token_length, KEY_VALUE_HEADS, query_groups, HEAD_SIZE
    )
    query_grads = []
    key_grads = []
    value_grads = []
    for index_of_head in range(KEY_VALUE_HEADS):
        scores = head_scores(index_of_head)
        head_probs = jnp.exp(scores - lse_parts[index_of_head])
        head_out = heads_gradient[:, index_of_head]
        value_grads.append(
            jnp.einsum(
                "gqk,qgd->kd",
                head_probs.astype(jnp.bfloat16),
                head_out,
                preferred_element_type=jnp.float32,
            )
        )
        prob_grad = jnp.einsum(
            "qgd,kd->gqk",
            head_out,
            heads_of_values[:, index_of_head],
            preferred_element_type=jnp.float32,
        )
        score_grad = (
            head_probs * (prob_grad - jnp.sum(prob_grad * head_probs, -1, keepdims=True))
        ).astype(jnp.bfloat16)
        query_grads.append(
            jnp.einsum(
                "gqk,kd->qgd",
                score_grad,
                heads_of_keys[:, index_of_head],
                preferred_element_type=jnp.float32,
            )
            * score_scale
        )
        key_grads.append(
            jnp.einsum(
                "gqk,qgd->kd",
                score_grad,
                heads_of_queries[:, index_of_head],
                preferred_element_type=jnp.float32,
            )
            * score_scale
        )
    d_queries = jnp.stack(query_grads, 1).reshape(token_length, query_w)
    d_kv_all = jnp.concatenate(
        [
            jnp.stack(key_grads, 1).reshape(count_of_keys, key_weight),
            jnp.stack(value_grads, 1).reshape(count_of_keys, key_weight),
        ],
        1,
    )
    d_pre = d_mamba * gate_z * gate_sig
    d_gate = d_mamba * mamba_pre * gate_sig * (1.0 + gate_z * (1.0 - gate_sig))
    skip_grad = jnp.sum(d_pre * activated, 0)

    def grad_block(pieces):
        total_blk, alive_blk, c_blk, out_blk = pieces
        return jnp.sum(
            reach_decay(total_blk, alive_blk) * c_blk[:, :, None] * out_blk[:, None, :], 0
        )

    local_grad = jnp.sum(
        lax.map(
            grad_block,
            (
                split_blocks(step_total),
                split_blocks(alive_now),
                split_blocks(c_out),
                split_blocks(d_pre),
            ),
        ),
        0,
    )

    def relay_backward(turn, carried):
        return from_behind(local_grad + total_decay * carried, "seq", -1)

    cross_grad = lax.fori_loop(0, lax.axis_size("seq") - 1, relay_backward, zero_state)
    start_steps = split_blocks(step_total - step_size)[:, 0]
    start_alive = split_blocks(alive_before)[:, 0]
    full_starts = (
        block_starts
        + jnp.exp(start_steps[:, None, :] * decay_rate[None])
        * start_alive[:, None, None]
        * state_in[None]
    )

    def backward_block(carry_grad, pieces):
        step_blk, input_blk, b_blk, c_blk, keep_blk, out_blk, start_blk = pieces
        decays, states = block_states(step_blk, input_blk, b_blk, keep_blk, decay_rate, start_blk)
        prior = jnp.concatenate([start_blk[None], states[:-1]], 0)
        emits = c_blk[:, :, None] * out_blk[:, None, :]
        emits = jnp.concatenate([emits[:-1], (emits[-1] + carry_grad)[None]], 0)
        coefs = jnp.concatenate([decays[1:], jnp.ones((1, NS, DI), jnp.float32)], 0)
        _, flipped = lax.associative_scan(combine_pair, (coefs[::-1], emits[::-1]))
        grads = flipped[::-1]
        decay_grad = grads * prior * decays
        pushed = jnp.sum(grads * b_blk[:, :, None], 1)
        step_grad = jnp.sum(decay_grad * decay_rate[None], 1) + pushed * input_blk
        input_grad = pushed * step_blk
        b_grad = jnp.sum(grads * (step_blk * input_blk)[:, None, :], 2)
        c_grad = jnp.sum(out_blk[:, None, :] * states, 2)
        log_grad = jnp.sum(decay_grad * step_blk[:, None, :], 0) * decay_rate
        return (decays[0] * grads[0], (step_grad, input_grad, b_grad, c_grad, log_grad))

    _, (step_grads, input_grads, b_grads, c_grads, log_grads) = lax.scan(
        backward_block, cross_grad, scan_pieces + (split_blocks(d_pre), full_starts), reverse=True
    )
    decay_log_grad = jnp.sum(log_grads, 0)
    d_step_pre = step_grads.reshape(token_length, DI) * jax.nn.sigmoid(step_pre)
    step_bias_grad = jnp.sum(d_step_pre, 0)
    d_step_low = d_step_pre.astype(jnp.bfloat16)
    step_term = dot_tn(step_raw, d_step_low)
    d_selected = jnp.concatenate(
        [
            dot_nt(d_step_low, full_step),
            b_grads.reshape(token_length, NS),
            c_grads.reshape(token_length, NS),
        ],
        1,
    ).astype(jnp.bfloat16)
    select_term = dot_tn(d_selected, activated_b)
    d_activated = (
        d_pre * skip_gain + input_grads.reshape(token_length, DI) + matmul(d_selected, full_select)
    )
    conv_sig = jax.nn.sigmoid(conv_sum)
    d_conv = d_activated * conv_sig * (1.0 + conv_sum * (1.0 - conv_sig))
    conv_bias_grad = jnp.sum(d_conv, 0)
    ext_grad = jnp.zeros((token_length + KC - 1, DI), jnp.float32)
    conv_rows = []
    for tap_index in range(KC):
        begin_row = KC - 1 - tap_index
        masked_grad = d_conv * same_masks[tap_index]
        conv_rows.append(jnp.sum(masked_grad * ext_inputs[begin_row : begin_row + token_length], 0))
        ext_grad = ext_grad + jnp.pad(
            conv_weight[tap_index] * masked_grad, ((begin_row, tap_index), (0, 0))
        )
    conv_weight_grad = jnp.stack(conv_rows, 0)

    def kv_part(back_index):
        first_key = (reach_shards - back_index) * token_length
        return d_kv_all[first_key : first_key + token_length]

    recv_kv, recv_tail = (
        from_behind(kv_part(1).astype(jnp.bfloat16), "seq", -1).astype(jnp.float32),
        from_behind(ext_grad[: KC - 1].astype(jnp.bfloat16), "seq", -1).astype(jnp.float32),
    )
    d_kv_own = d_kv_all[reach_shards * token_length :] + recv_kv
    for back_index in range(2, reach_shards + 1):
        d_kv_own = d_kv_own + from_behind(
            kv_part(back_index).astype(jnp.bfloat16), "seq", -back_index
        ).astype(jnp.float32)
    d_inputs = ext_grad[KC - 1 :] + jnp.pad(recv_tail, ((token_length - (KC - 1), 0), (0, 0)))
    d_projected = jnp.concatenate([d_queries, d_kv_own, d_inputs, d_gate], 1).astype(jnp.bfloat16)
    in_term = dot_tn(normed_one, d_projected)
    d_x_part, first_grad = norm_back(seq_x, scale_one, first_gain, dot_nt(d_projected, full_in))
    tokens_grad = (d_hidden + d_x_part).astype(jnp.bfloat16)
    in_sum, select_sum, step_sum = reduce_terms(in_term, select_term, step_term)
    vector_sums = lax.psum(
        (
            first_grad,
            second_grad,
            attn_grad,
            mamba_grad,
            conv_weight_grad,
            conv_bias_grad,
            step_bias_grad,
            decay_log_grad,
            skip_grad,
        ),
        ("seq", "fsdp"),
    )
    return (
        out_tokens[None],
        tokens_grad[None],
        in_sum,
        out_sum,
        gate_up_sum,
        down_sum,
        select_sum,
        step_sum,
        vector_sums[0],
        vector_sums[1],
        vector_sums[2],
        vector_sums[3],
        vector_sums[4],
        vector_sums[5],
        vector_sums[6],
        vector_sums[7],
        vector_sums[8],
    )


def solution(mesh):
    placed = (
        P("fsdp", "seq", None),
        P("fsdp", "seq"),
        P("fsdp", "seq"),
        P("fsdp", "seq"),
        P("fsdp", "seq"),
        P("fsdp", "seq"),
        P("fsdp", "seq"),
        P("fsdp", "seq"),
        P(),
        P(),
        P(),
        P(),
        P(),
        P(),
        P(),
        P(),
        P(),
        P("fsdp", "seq", None),
    )
    return jax.shard_map(
        shards,
        mesh=mesh,
        in_specs=placed,
        out_specs=(
            P("fsdp", "seq", None),
            P("fsdp", "seq", None),
            P("fsdp", "seq"),
            P("fsdp", "seq"),
            P("fsdp", "seq"),
            P("fsdp", "seq"),
            P("fsdp", "seq"),
            P("fsdp", "seq"),
            P(),
            P(),
            P(),
            P(),
            P(),
            P(),
            P(),
            P(),
            P(),
        ),
        check_vma=False,
    )
```

profile of v0, /device:TPU:0, one launch (start us, length us, event | category | flops | bytes accessed | tf_op | source)
XLA Modules:
  0.0 4983.6 jit_solution(5396241482991929639)
XLA Ops:
  9.5 75.3 %all-gather.15.cloned.1.call-done = bf16[1600,1080]{1,0:T(8,128)(2,1)} async-done(((bf16[400,1080]{1,0:T(8,128)(2,1)}), bf16[1600,1080]{1,0:T(8,128)(2,1)}) %all-gather.15.cloned.1.call-update) | async-done | bytes 3456016 | tf_op jit(solution)/shard_map/all_gather | solution.py:72
  91.7 38.2 all-gather.25.cloned.1.call-done
  135.4 80.7 %all-gather.21.cloned.1.call-done = bf16[1600,1376]{1,0:T(8,128)(2,1)} async-done(((bf16[400,1376]{1,0:T(8,128)(2,1)}), bf16[1600,1376]{1,0:T(8,128)(2,1)}) %all-gather.21.cloned.1.call-update) | async-done | bytes 4403216 | tf_op jit(solution)/shard_map/all_gather | solution.py:74
  290.2 70.7 %all-gather.17.cloned.1.call-done = bf16[1600,8640]{0,1:T(8,128)(2,1)} async-done(((bf16[1600,1080]{0,1:T(8,128)(2,1)}), bf16[1600,8640]{0,1:T(8,128)(2,1)}) %all-gather.17.cloned.1.call-update) | async-done | bytes 27648016 | tf_op jit(solution)/shard_map/all_gather | solution.py:80
  381.7 29.3 all-gather.29.cloned.1.call-done
  499.5 794.5 %while.78 = (s32[]{:T(128)}, f32[16,3200]{1,0:T(8,128)S(1)}, f32[8,32,3200]{2,1,0:T(8,128)}, f32[8,16,3200]{2,1,0:T(8,128)}, f32[8,32,3200]{2,1,0:T(8,128)}, /*i...) while((s32[]{:T(128)}, f32[16,3200]{1,0:T(8,128)S(1)}, ...), condition=%wide.region_14.15_spmd, body=%wide.region_12.14_spmd.sunk | while | flops 23347200 | bytes 294926368 | solution.py:257
  1300.8 42.3 while.79
  1345.0 59.6 %while.80 = (s32[]{:T(128)}, f32[8,32,3200]{2,1,0:T(8,128)}, f32[8,32,16]{1,2,0:T(8,128)}, f32[8,32,3200]{2,1,0:T(8,128)}, f32[16,3200]{1,0:T(8,128)S(1)}, /*ind...) while((s32[]{:T(128)}, f32[8,32,3200]{2,1,0:T(8,128)}, f32[8,32,16]{1,2,0:T(8,128)}, ...), condition=%wide.region_23.24_spmd, body=%wide.region_21.23_spmd.sunk | while | flops 8089602 | bytes 2878433 | solution.py:278
  1453.9 46.0 copy.260
  1535.8 26.3 multiply_reduce_fusion.17
  1595.3 36.1 while.81
  1631.6 53.0 %while.82 = (s32[]{:T(128)}, f32[16,3200]{1,0:T(8,128)S(1)}, f32[16,3200]{1,0:T(8,128)S(1)}, f32[16,3200]{1,0:T(8,128)S(1)}, s32[]{:T(128)}) while((s32[]{:T(128)}, f32[16,3200]{1,0:T(8,128)S(1)}, f32[16,3200]{1,0:T(8,128)S(1)}, f32[16,3200]{1,0:T(8,128)S(1)}, s32[]{:T(128)}) %tuple.338), condition=%wide.region_39.40_spmd, body=%wide.region_38.39_spmd.sunk | while | flops 102402 | bytes 1638501 | solution.py:397
  1691.1 1700.6 %while.83 = (s32[]{:T(128)}, f32[16,3200]{1,0:T(8,128)S(1)}, f32[8,32,3200]{2,1,0:T(8,128)}, f32[8,32,3200]{2,1,0:T(8,128)}, bf16[8,32,16]{2,1,0:T(8,128)(2,1)},...) while((s32[]{:T(128)}, f32[16,3200]{1,0:T(8,128)S(1)}, ...), condition=%wide.region_46.47_spmd, body=%wide.region_40.46_spmd.sunk | while | flops 63179776 | bytes 760458816 | solution.py:425
  3444.0 47.3 copy.319
  3700.4 74.0 %reduce-scatter.48.cloned.1.call-done = bf16[5504,200]{0,1:T(8,128)(2,1)} async-done(((bf16[5504,1600]{0,1:T(8,128)(2,1)}), bf16[5504,200]{0,1:T(8,128)(2,1)}) %reduce-scatter.48.cloned.1.call-update) | async-done | bytes 2201616
  3778.8 298.1 %reduce-scatter.40.cloned.1.call-done = bf16[1376,1600]{1,0:T(8,128)(2,1)} async-done(((bf16[11008,1600]{1,0:T(8,128)(2,1)}), bf16[1376,1600]{1,0:T(8,128)(2,1)}) %reduce-scatter.40.cloned.1.call-update) | async-done | bytes 4403216
  4084.5 275.8 %reduce-scatter.46.cloned.1.call-done = bf16[1600,1080]{0,1:T(8,128)(2,1)} async-done(((bf16[1600,8640]{0,1:T(8,128)(2,1)}), bf16[1600,1080]{0,1:T(8,128)(2,1)}) %reduce-scatter.46.cloned.1.call-update) | async-done | bytes 3456016
  4387.2 21.6 fusion.164
  4441.2 49.2 reduce-scatter.38.cloned.1.call-done
  4492.7 54.6 %reduce-scatter.42.cloned.1.call-done = bf16[1376,200]{1,0:T(8,128)(2,1)} async-done(((bf16[5504,200]{1,0:T(8,128)(2,1)}), bf16[1376,200]{1,0:T(8,128)(2,1)}) %reduce-scatter.42.cloned.1.call-update) | async-done | bytes 550416
  4549.8 81.7 %reduce-scatter.32.cloned.1.call-done = bf16[400,1376]{1,0:T(8,128)(2,1)} async-done(((bf16[1600,1376]{1,0:T(8,128)(2,1)}), bf16[400,1376]{1,0:T(8,128)(2,1)}) %reduce-scatter.32.cloned.1.call-update) | async-done | bytes 1100816 | tf_op jit(solution)/shard_map/reduce_scatter | solution.py:105
  4634.2 68.9 %reduce-scatter.36.cloned.1.call-done = bf16[400,1080]{1,0:T(8,128)(2,1)} async-done(((bf16[1600,1080]{1,0:T(8,128)(2,1)}), bf16[400,1080]{1,0:T(8,128)(2,1)}) %reduce-scatter.36.cloned.1.call-update) | async-done | bytes 864016
  4706.7 125.8 %all-reduce.46.cloned.1.call-done = f32[16,3200]{1,0:T(8,128)} async-done(((f32[16,3200]{1,0:T(8,128)}), f32[16,3200]{1,0:T(8,128)}) %all-reduce.46.cloned.1.call-update) | async-done | bytes 204816 | tf_op jit(solution)/shard_map/psum | solution.py:478
  4832.5 131.9 %all-reduce.50.cloned.1.call-done = (f32[1600]{0:T(1024)}, f32[1600]{0:T(1024)}, f32[1600]{0:T(1024)}, f32[3200]{0:T(1024)}, f32[4,3200]{1,0:T(4,128)}, /*index=5*/f32[3200]{0:T(1024)}, f32[3200]{0:T(1024)}, f32[3200]{0:T(1024)}) async-done(((f32[1600]{0:T(1024)}, f32[1600]{0:T(1024)}, f32[1600]{0:T(1024)}, f32[3200]{0:T(1024)}, f32[4,3200]{1,0:T(4,128)}, /*index=5*/f32[3200]{0:T(1024)}, f32[3200]{0:T(1024)}, ...) | async-done | bytes 121616 | tf_op jit(solution)/shard_map/psum | solution.py:478
  (2671 shorter events, 3361.3 us)
Async XLA Ops:
  7.9 122.0 %all-gather.25.cloned.1.call-start = ((), (), s32[]{:S(2)}) async-start(), calls=%async_computation.19 | async-start | bytes 2560000 | tf_op jit(solution)/shard_map/all_gather | solution.py:73
  8.7 207.5 %all-gather.21.cloned.1.call-start = ((), (), s32[]{:S(2)}) async-start(), calls=%async_computation.13 | async-start | bytes 5632000 | tf_op jit(solution)/shard_map/all_gather | solution.py:74
  9.4 351.5 %all-gather.17.cloned.1.call-start = ((), (), s32[]{:S(2)}) async-start(), calls=%async_computation.11 | async-start | bytes 32348160 | tf_op jit(solution)/shard_map/all_gather | solution.py:80
  91.0 320.0 %all-gather.29.cloned.1.call-start = ((), (), s32[]{:S(2)}) async-start(), calls=%async_computation.21 | async-start | bytes 2816000 | tf_op jit(solution)/shard_map/all_gather | solution.py:75
  91.6 1353.8 %all-gather.19.cloned.1.call-start = ((), (), s32[]{:S(2)}) async-start(), calls=%async_computation.12 | async-start | bytes 17510400 | tf_op jit(solution)/shard_map/all_gather | solution.py:81
  135.4 1318.5 %all-gather.27.cloned.1.call-start = ((), (), s32[]{:S(2)}) async-start(), calls=%async_computation.20 | async-start | bytes 40550400 | tf_op jit(solution)/shard_map/all_gather | solution.py:82
  216.2 1302.9 %all-gather.23.cloned.1.call-start = ((), (), s32[]{:S(2)}) async-start(), calls=%async_computation.14 | async-start | bytes 19814400 | tf_op jit(solution)/shard_map/all_gather | solution.py:83
  416.8 3278.8 %reduce-scatter.34.cloned.1.call-start = ((), (), s32[]{:S(2)}) async-start(), calls=%async_computation.17 | async-start | bytes 921600 | tf_op jit(solution)/shard_map/reduce_scatter | solution.py:97
  418.7 1003.7 %collective-permute-start.2 = (bf16[256,640]{0,1:T(8,128)(2,1)}, bf16[256,640]{0,1:T(8,128)(2,1)}, u32[]{:S(2)}, u32[]{:S(2)}) collective-permute-start(bf16[256,640]{0,1:T(8,128)(2,1)} %slice.1205), channel_id=1, source_target_pairs={{0,16},{4,20},{8,24},{12,28},{1,17},{5,21},{9,25},{13,29},{2,18},{... | collective-permute-start | bytes 983048 | tf_op jit(solution)/shard_map/ppermute | solution.py:26
  422.8 1000.7 %collective-permute-start.3 = (bf16[256,640]{0,1:T(8,128)(2,1)}, bf16[256,640]{0,1:T(8,128)(2,1)}, u32[]{:S(2)}, u32[]{:S(2)}) collective-permute-start(bf16[256,640]{0,1:T(8,128)(2,1)} %slice.1205), channel_id=1, source_target_pairs={{0,12},{4,16},{8,20},{12,24},{16,28},{1,13},{5,17},{9,21},{13,25},... | collective-permute-start | bytes 983048 | tf_op jit(solution)/shard_map/ppermute | solution.py:26
  426.0 998.5 %collective-permute-start.4 = (bf16[256,640]{0,1:T(8,128)(2,1)}, bf16[256,640]{0,1:T(8,128)(2,1)}, u32[]{:S(2)}, u32[]{:S(2)}) collective-permute-start(bf16[256,640]{0,1:T(8,128)(2,1)} %slice.1205), channel_id=1, source_target_pairs={{0,8},{4,12},{8,16},{12,20},{16,24},{20,28},{1,9},{5,13},{9,17},{1... | collective-permute-start | bytes 983048 | tf_op jit(solution)/shard_map/ppermute | solution.py:26
  431.1 994.5 %collective-permute-start.5 = (bf16[256,640]{0,1:T(8,128)(2,1)}, bf16[256,640]{0,1:T(8,128)(2,1)}, u32[]{:S(2)}, u32[]{:S(2)}) collective-permute-start(bf16[256,640]{0,1:T(8,128)(2,1)} %slice.1205), channel_id=1, source_target_pairs={{0,4},{4,8},{8,12},{12,16},{16,20},{20,24},{24,28},{1,5},{5,9},{9,... | collective-permute-start | bytes 983048 | tf_op jit(solution)/shard_map/ppermute | solution.py:26
  3402.9 293.3 %reduce-scatter.30.cloned.1.call-start = ((), (), s32[]{:S(2)}) async-start(), calls=%async_computation.15 | async-start | bytes 17510400 | tf_op jit(solution)/shard_map/reduce_scatter | solution.py:97
  3411.8 362.6 %reduce-scatter.48.cloned.1.call-start = ((), (), s32[]{:S(2)}) async-start(), calls=%async_computation.29 | async-start | bytes 19814400
  3424.5 652.5 %reduce-scatter.40.cloned.1.call-start = ((), (), s32[]{:S(2)}) async-start(), calls=%async_computation.24 | async-start | bytes 41213952
  3491.4 868.9 %reduce-scatter.46.cloned.1.call-start = ((), (), s32[]{:S(2)}) async-start(), calls=%async_computation.28 | async-start | bytes 32348160
  3691.6 720.0 %reduce-scatter.44.cloned.1.call-start = ((), (), s32[]{:S(2)}) async-start(), calls=%async_computation.26 | async-start | bytes 1843200
  3695.5 743.1 %all-reduce.48.cloned.1.call-start = ((), (), s32[]{:S(2)}) async-start(), calls=%async_computation.27 | async-start | bytes 204800
  3696.1 794.3 %reduce-scatter.38.cloned.1.call-start = ((), (), s32[]{:S(2)}) async-start(), calls=%async_computation.23 | async-start | bytes 3072000
  3700.3 847.0 %reduce-scatter.42.cloned.1.call-start = ((), (), s32[]{:S(2)}) async-start(), calls=%async_computation.25 | async-start | bytes 3522560
  3778.8 852.7 %reduce-scatter.32.cloned.1.call-start = ((), (), s32[]{:S(2)}) async-start(), calls=%async_computation.16 | async-start | bytes 5632000 | tf_op jit(solution)/shard_map/reduce_scatter | solution.py:105
  4084.4 618.7 %reduce-scatter.36.cloned.1.call-start = ((), (), s32[]{:S(2)}) async-start(), calls=%async_computation.22 | async-start | bytes 4608000
  4366.5 465.9 %all-reduce.46.cloned.1.call-start = ((), (), s32[]{:S(2)}) async-start(), calls=%async_computation.18 | async-start | bytes 409600 | tf_op jit(solution)/shard_map/psum | solution.py:478
  4372.4 592.0 %all-reduce.50.cloned.1.call-start = ((), (), s32[]{:S(2)}) async-start(), calls=%async_computation.30 | async-start | bytes 282624 | tf_op jit(solution)/shard_map/psum | solution.py:478
  (644 other events, 5743.1 us)
Sparse Core Ops, SparseCore 0:
  9.6 75.0 all-gather.14
  86.3 43.5 all-gather.24
  131.5 84.6 all-gather.20
  217.9 142.9 all-gather.16
  362.3 48.7 all-gather.28
  412.8 105.6 all-gather.18
  520.4 172.4 all-gather.26
  695.3 93.3 all-gather.22
  3403.0 43.8 reduce-scatter.33
  3450.8 113.3 reduce-scatter.29
  3566.6 207.7 reduce-scatter.47
  3777.8 299.1 reduce-scatter.39
  4079.5 280.7 reduce-scatter.45
  4363.8 37.8 reduce-scatter.43
  4404.0 34.6 all-reduce.47
  4440.8 49.5 reduce-scatter.37
  4492.6 54.7 reduce-scatter.41
  4549.6 81.8 reduce-scatter.31
  4633.7 69.2 reduce-scatter.35
  4709.1 123.3 all-reduce.45
  4840.0 124.2 all-reduce.49
where the time goes:
time: 5020 us; the launch traced here: 4980 us
  local copies, waits for them, and re-layouts  1690 us (34%)
  waiting for transfers between devices  1540 us (31%)
  other arithmetic  1290 us (26%)
  matrix products  294 us (6%)
  starting transfers between devices  80.5 us (2%)
  blocking collectives  66.7 us (1%)
    unnamed x30, waiting for transfers between devices  834 us
    pad x128, local copies, waits for them, and re-layouts, block_states(): _, states = lax.associative_scan(combine_pair, (decays, pushes))  657 us
    pad x64, local copies, waits for them, and re-layouts, backward_block(): _, flipped = lax.associative_scan(combine_pair, (coefs[::-1], emits[::-1]))  369 us
    psum x2, waiting for transfers between devices, shards(): lax.psum((first_grad, second_grad, attn_grad, mamba_grad, conv_weight_gra...  258 us
    while x944, local copies, waits for them, and re-layouts  192 us
    add x72, other arithmetic, combine_pair(): return (earlier[0] * later[0], later[0] * earlier[1] + later[1])  184 us
    add x72, other arithmetic, block_states(): _, states = lax.associative_scan(combine_pair, (decays, pushes))  169 us
    mul x72, other arithmetic, combine_pair(): return (earlier[0] * later[0], later[0] * earlier[1] + later[1])  159 us
  transfers between devices with their start and end apart: 50, of which 31 were waited for; matrix products, arithmetic and copies ran while one was open for 28% of the time, Pallas kernels for 0%

commit v1 on v0

v1 whole, which is shorter than its diff:
```python
import functools

import jax
import jax.numpy as jnp
from jax import lax
from jax.experimental import pallas as pl
from jax.experimental.pallas import tpu as pltpu
from jax.sharding import PartitionSpec as P

QUERY_HEADS = 25
KEY_VALUE_HEADS = 5
HEAD_SIZE = 64
DI = 3200
NS = 16
DTR = 100
KC = 4
F = 5504
WINDOW_TOKENS = 1024

norm_eps = 1e-05
masked_score = -1e30
log2e = 1.4426950408889634
bf16 = jnp.bfloat16
f32 = jnp.float32


def matmul(left, right):
    return jnp.dot(left, right, preferred_element_type=f32)


def dot_tn(left, right):
    return lax.dot_general(left, right, (((0,), (0,)), ((), ())), preferred_element_type=f32)


def dot_nt(left, right):
    return lax.dot_general(left, right, (((1,), (1,)), ((), ())), preferred_element_type=f32)


def rms_norm(value, gain):
    scale = lax.rsqrt(jnp.mean(value * value, axis=-1, keepdims=True) + norm_eps)
    return (value * scale * gain, scale)


def norm_back(value, scale, gain, upstream):
    weighted = upstream * gain
    gain_grad = jnp.sum(upstream * value * scale, 0)
    inner_mean = jnp.mean(weighted * value, axis=-1, keepdims=True)
    return (scale * weighted - value * (scale * scale * scale) * inner_mean, gain_grad)


def park(part, j, value):
    for k, lane in enumerate(range(0, value.shape[1], 128)):
        end = min(lane + 128, value.shape[1])
        part[64 * k + 8 * j : 64 * k + 8 * j + 8, : end - lane] = value[:, lane:end]


def fold(part, out, t0):
    for k, lane in enumerate(range(0, out.shape[1], 128)):
        end = min(lane + 128, out.shape[1])
        total = part[pl.ds(64 * k, 8, stride=8), :]
        for s in range(1, 8):
            total = total + part[pl.ds(64 * k + s, 8, stride=8), :]
        out[pl.ds(t0, 8), lane:end] = total[:, : end - lane]


def scan_fwd_body(step_ref, push_ref, b_ref, c_ref, rate_ref, y_ref, st_ref, h_scr, part_scr):
    block = step_ref.shape[0]

    @pl.when(pl.program_id(0) == 0)
    def _():
        h_scr[...] = jnp.zeros_like(h_scr)

    rate = rate_ref[...]

    def group(index, state):
        t0 = pl.multiple_of(index * 8, 8)
        step8 = step_ref[pl.ds(t0, 8), :]
        push8 = push_ref[pl.ds(t0, 8), :]
        b_roll = pltpu.roll(b_ref[...], block - t0, 1)
        c_roll = pltpu.roll(c_ref[...], block - t0, 1)
        for j in range(8):
            decay = jnp.exp2(step8[j : j + 1, :] * rate)
            state = decay * state + push8[j : j + 1, :] * b_roll[:, j : j + 1]
            st_ref[t0 + j] = state
            out = c_roll[:, j : j + 1] * state
            park(part_scr, j, out[:8] + out[8:])
        fold(part_scr, y_ref, t0)
        return state

    h_scr[...] = lax.fori_loop(0, block // 8, group, h_scr[...])


def scan_bwd_body(
    step_ref, push_ref, dpre_ref, b_ref, c_ref, st_ref, prev_ref, rate_ref,
    pr_ref, pushed_ref, db_ref, dc_ref, log_ref, g_scr, log_scr, part1, part2,
):
    block = step_ref.shape[0]
    count = pl.num_programs(0)
    which = pl.program_id(0)

    @pl.when(which == 0)
    def _():
        g_scr[...] = jnp.zeros_like(g_scr)
        log_scr[...] = jnp.zeros_like(log_scr)

    lane_ids = lax.broadcasted_iota(jnp.int32, (NS, block), 1)
    before = prev_ref[0] * jnp.where(which == count - 1, 0.0, 1.0)

    def group(turn, carried):
        grad_in, state, db_acc, dc_acc = carried
        t0 = pl.multiple_of((block // 8 - 1 - turn) * 8, 8)
        step8 = step_ref[pl.ds(t0, 8), :]
        push8 = push_ref[pl.ds(t0, 8), :]
        dpre8 = dpre_ref[pl.ds(t0, 8), :]
        b_roll = pltpu.roll(b_ref[...], block - t0, 1)
        c_roll = pltpu.roll(c_ref[...], block - t0, 1)
        rate = rate_ref[...]
        log_acc = log_scr[...]
        for j in range(7, -1, -1):
            if j > 0:
                prior = st_ref[t0 + (j - 1)]
            else:
                prior = jnp.where(t0 > 0, st_ref[jnp.maximum(t0 - 1, 0)], before)
            step_row = step8[j : j + 1, :]
            dpre_row = dpre8[j : j + 1, :]
            grad = c_roll[:, j : j + 1] * dpre_row + grad_in
            grad_in = grad * jnp.exp2(step_row * (rate * log2e))
            flow = grad_in * prior
            by_rate = flow * rate
            park(part1, j, by_rate[:8] + by_rate[8:])
            by_b = grad * b_roll[:, j : j + 1]
            park(part2, j, by_b[:8] + by_b[8:])
            log_acc = log_acc + flow * step_row
            db = jnp.sum(grad * push8[j : j + 1, :], axis=1, keepdims=True)
            dc = jnp.sum(state * dpre_row, axis=1, keepdims=True)
            here = lane_ids == t0 + j
            db_acc = jnp.where(here, db, db_acc)
            dc_acc = jnp.where(here, dc, dc_acc)
            state = prior
        log_scr[...] = log_acc
        fold(part1, pr_ref, t0)
        fold(part2, pushed_ref, t0)
        return (grad_in, state, db_acc, dc_acc)

    zero = jnp.zeros((NS, block), f32)
    grad_in, _, db_acc, dc_acc = lax.fori_loop(
        0, block // 8, group, (g_scr[...], st_ref[block - 1], zero, zero)
    )
    g_scr[...] = grad_in
    db_ref[...] = db_acc
    dc_ref[...] = dc_acc

    @pl.when(which == count - 1)
    def _():
        log_ref[...] = log_scr[...] * rate_ref[...]


SCAN_BLOCK = 128


def scan_forward(step_keep, push, b_t, c_t, rate):
    tokens, width = step_keep.shape
    block = SCAN_BLOCK
    padded = (width + 127) // 128 * 128
    rows = pl.BlockSpec((block, width), lambda i: (i, 0))
    cols = pl.BlockSpec((NS, block), lambda i: (0, i))
    fixed = pl.BlockSpec((NS, width), lambda i: (0, 0))
    return pl.pallas_call(
        scan_fwd_body,
        grid=(tokens // block,),
        in_specs=[rows, rows, cols, cols, fixed],
        out_specs=[rows, pl.BlockSpec((block, NS, width), lambda i: (i, 0, 0))],
        out_shape=[
            jax.ShapeDtypeStruct((tokens, width), f32),
            jax.ShapeDtypeStruct((tokens, NS, width), f32),
        ],
        scratch_shapes=[pltpu.VMEM((NS, width), f32), pltpu.VMEM((padded // 2, 128), f32)],
        compiler_params=pltpu.CompilerParams(vmem_limit_bytes=40 << 20),
        cost_estimate=pl.CostEstimate(
            flops=tokens * width * NS * 8, bytes_accessed=tokens * width * NS * 4, transcendentals=tokens * width * NS
        ),
        name="scan_forward",
    )(step_keep, push, b_t, c_t, rate * log2e)


def scan_backward(step_keep, push, d_pre, b_t, c_t, states, rate):
    tokens, width = step_keep.shape
    block = SCAN_BLOCK
    padded = (width + 127) // 128 * 128
    last = tokens // block - 1
    rows = pl.BlockSpec((block, width), lambda i: (last - i, 0))
    cols = pl.BlockSpec((NS, block), lambda i: (0, last - i))
    fixed = pl.BlockSpec((NS, width), lambda i: (0, 0))
    return pl.pallas_call(
        scan_bwd_body,
        grid=(tokens // block,),
        in_specs=[
            rows, rows, rows, cols, cols,
            pl.BlockSpec((block, NS, width), lambda i: (last - i, 0, 0)),
            pl.BlockSpec((1, NS, width), lambda i: (jnp.maximum((last - i) * block - 1, 0), 0, 0)),
            fixed,
        ],
        out_specs=[rows, rows, cols, cols, fixed],
        out_shape=[
            jax.ShapeDtypeStruct((tokens, width), f32),
            jax.ShapeDtypeStruct((tokens, width), f32),
            jax.ShapeDtypeStruct((NS, tokens), f32),
            jax.ShapeDtypeStruct((NS, tokens), f32),
            jax.ShapeDtypeStruct((NS, width), f32),
        ],
        scratch_shapes=[
            pltpu.VMEM((NS, width), f32),
            pltpu.VMEM((NS, width), f32),
            pltpu.VMEM((padded // 2, 128), f32),
            pltpu.VMEM((padded // 2, 128), f32),
        ],
        compiler_params=pltpu.CompilerParams(vmem_limit_bytes=40 << 20),
        cost_estimate=pl.CostEstimate(
            flops=tokens * width * NS * 18, bytes_accessed=tokens * width * NS * 4, transcendentals=tokens * width * NS
        ),
        name="scan_backward",
    )(step_keep, push, d_pre, b_t, c_t, states, states, rate)


def attn_fwd_body(qt_ref, k_ref, vt_ref, bias_ref, out_ref, lse_ref):
    queries = bias_ref.shape[1]
    for head in range(qt_ref.shape[2] // queries):
        cols = slice(head * queries, (head + 1) * queries)
        scores = matmul(k_ref[0], qt_ref[0][:, cols]) + bias_ref[...]
        row_max = jnp.max(scores, 0, keepdims=True)
        exp_scores = jnp.exp(scores - row_max)
        row_total = jnp.sum(exp_scores, 0, keepdims=True)
        probs = (exp_scores * (1.0 / row_total)).astype(bf16)
        out_ref[0, :, cols] = matmul(vt_ref[0], probs)
        lse_ref[0, :, cols] = row_max + jnp.log(row_total)


def attn_bwd_body(
    q_ref, qt_ref, k_ref, kt_ref, v_ref, do_ref, dot_ref, lse_ref, bias_ref, dqt_ref, dk_ref, dv_ref
):
    queries = bias_ref.shape[1]
    dk = jnp.zeros(dk_ref.shape[1:], f32)
    dv = jnp.zeros(dv_ref.shape[1:], f32)
    for head in range(qt_ref.shape[2] // queries):
        cols = slice(head * queries, (head + 1) * queries)
        scores = matmul(k_ref[0], qt_ref[0][:, cols]) + bias_ref[...]
        probs = jnp.exp(scores - lse_ref[0][:, cols])
        d_probs = matmul(v_ref[0], dot_ref[0][:, cols])
        inner = jnp.sum(probs * d_probs, 0, keepdims=True)
        d_scores = (probs * (d_probs - inner)).astype(bf16)
        dqt_ref[0, :, cols] = matmul(kt_ref[0], d_scores) * (HEAD_SIZE**-0.5)
        dk = dk + matmul(d_scores, q_ref[0][cols])
        dv = dv + matmul(probs.astype(bf16), do_ref[0][cols])
    dk_ref[0] = dk
    dv_ref[0] = dv


def per_head(*dims):
    return pl.BlockSpec((1,) + dims, lambda h: (h, 0, 0))


def attention_forward(q_t, k, v_t, bias):
    heads, size, span = q_t.shape
    keys = k.shape[1]
    return pl.pallas_call(
        attn_fwd_body,
        grid=(heads,),
        in_specs=[per_head(size, span), per_head(keys, size), per_head(size, keys),
                  pl.BlockSpec(bias.shape, lambda h: (0, 0))],
        out_specs=[per_head(size, span), per_head(1, span)],
        out_shape=[
            jax.ShapeDtypeStruct((heads, size, span), f32),
            jax.ShapeDtypeStruct((heads, 1, span), f32),
        ],
        compiler_params=pltpu.CompilerParams(vmem_limit_bytes=40 << 20),
        cost_estimate=pl.CostEstimate(
            flops=heads * keys * span * 4 * 128, bytes_accessed=8 << 20, transcendentals=heads * keys * span
        ),
        name="attention_forward",
    )(q_t, k, v_t, bias)


def attention_backward(q, q_t, k, k_t, v, d_out, d_out_t, lse, bias):
    heads, size, span = q_t.shape
    keys = k.shape[1]
    return pl.pallas_call(
        attn_bwd_body,
        grid=(heads,),
        in_specs=[per_head(span, size), per_head(size, span), per_head(keys, size), per_head(size, keys),
                  per_head(keys, size), per_head(span, size), per_head(size, span), per_head(1, span),
                  pl.BlockSpec(bias.shape, lambda h: (0, 0))],
        out_specs=[per_head(size, span), per_head(keys, size), per_head(keys, size)],
        out_shape=[
            jax.ShapeDtypeStruct((heads, size, span), f32),
            jax.ShapeDtypeStruct((heads, keys, size), f32),
            jax.ShapeDtypeStruct((heads, keys, size), f32),
        ],
        compiler_params=pltpu.CompilerParams(vmem_limit_bytes=40 << 20),
        cost_estimate=pl.CostEstimate(
            flops=heads * keys * span * 10 * 128, bytes_accessed=16 << 20, transcendentals=heads * keys * span
        ),
        name="attention_backward",
    )(q, q_t, k, k_t, v, d_out, d_out_t, lse, bias)


def layer(
    n,
    m,
    tokens,
    doc_ids,
    in_weight,
    out_weight,
    gate_up,
    down_weight,
    select_weight,
    step_weight,
    first_gain,
    second_gain,
    attn_gain,
    mamba_gain,
    conv_weight,
    conv_bias,
    step_bias,
    decay_log,
    skip_gain,
    cotangent,
):
    me = lax.axis_index("seq")
    query_w = QUERY_HEADS * HEAD_SIZE
    key_w = KEY_VALUE_HEADS * HEAD_SIZE
    groups = QUERY_HEADS // KEY_VALUE_HEADS
    q_own, k_own, c_own, f_own = query_w // n, key_w // n, DI // n, F // n
    local = tokens.shape[1]
    length = local * n
    starts = (0, query_w, query_w + key_w, query_w + 2 * key_w, query_w + 2 * key_w + DI)
    widths = (q_own, k_own, k_own, c_own, c_own)

    def own_cols(value):
        return lax.dynamic_slice_in_dim(value, me * c_own, c_own, value.ndim - 1)

    in_cols = lax.all_gather(in_weight, "seq", axis=1, tiled=True)
    in_cols = jnp.concatenate(
        [lax.dynamic_slice_in_dim(in_cols, s + me * w, w, 1) for s, w in zip(starts, widths)], 1
    )
    in_full = lax.all_gather(in_cols, "fsdp", axis=0, tiled=True)
    select_own = lax.all_gather(select_weight, "fsdp", axis=0, tiled=True)
    step_own = lax.all_gather(step_weight, "fsdp", axis=0, tiled=True)

    half = n // 2
    route_a = [(d, 2 * d if d < half else 2 * (d - half) + 1) for d in range(n)]
    route_b = [(d, 2 * d + 1 if d < half else 2 * (d - half)) for d in range(n)]
    low_half = me < half
    even = me % 2 == 0
    piece0, piece1 = gate_up[:, :f_own], gate_up[:, f_own:]
    got_a = lax.ppermute(jnp.where(low_half, piece0, piece1), "seq", route_a)
    got_b = lax.ppermute(jnp.where(low_half, piece1, piece0), "seq", route_b)
    gu_cols = jnp.concatenate([jnp.where(even, got_a, got_b), jnp.where(even, got_b, got_a)], 1)
    gu_full = lax.all_gather(gu_cols, "fsdp", axis=0, tiled=True)

    out_rows = lax.all_gather(out_weight, "fsdp", axis=0, tiled=True)
    out_rows = jnp.concatenate(
        [out_rows[:query_w].reshape(n, q_own, -1), out_rows[query_w:].reshape(n, c_own, -1)], 1
    )
    out_full = lax.all_to_all(out_rows, "seq", 0, 0, tiled=False)
    out_full = out_full.transpose(1, 0, 2).reshape(q_own + c_own, -1)
    down_rows = lax.all_gather(down_weight, "fsdp", axis=0, tiled=True).reshape(n, f_own, -1)
    down_full = lax.all_to_all(down_rows, "seq", 0, 0, tiled=False)
    down_full = down_full.transpose(1, 0, 2).reshape(f_own, -1)

    seq_x = tokens[0].astype(f32)
    ids = lax.all_gather(doc_ids[0], "seq", axis=0, tiled=True)
    normed_one, scale_one = rms_norm(seq_x, first_gain)
    normed_one = lax.all_gather(normed_one.astype(bf16), "seq", axis=0, tiled=True)
    projected = matmul(normed_one, in_full).astype(bf16)
    edges = [0]
    for w in widths:
        edges.append(edges[-1] + w)
    queries_c = projected[:, : edges[1]]
    kv_c = projected[:, edges[1] : edges[3]]
    inputs = projected[:, edges[3] : edges[4]].astype(f32)
    gate_z = projected[:, edges[4] :].astype(f32)

    queries = lax.all_to_all(queries_c, "seq", 0, 1, tiled=True) * bf16(HEAD_SIZE**-0.5)
    kv_all = lax.all_gather(kv_c, "seq", axis=0, tiled=False)
    reach = (WINDOW_TOKENS + local - 2) // local
    span = min((reach + 1) * local, length)
    first_key = jnp.clip((me - reach) * local, 0, length - span)
    kv_win = lax.dynamic_slice_in_dim(kv_all, first_key, span, 1)
    keys = kv_win[:, :, :k_own].transpose(1, 0, 2).reshape(span, KEY_VALUE_HEADS, HEAD_SIZE)
    values = kv_win[:, :, k_own:].transpose(1, 0, 2).reshape(span, KEY_VALUE_HEADS, HEAD_SIZE)
    query_pos = me * local + jnp.arange(local, dtype=jnp.int32)
    key_pos = first_key + jnp.arange(span, dtype=jnp.int32)
    offset = query_pos[None, :] - key_pos[:, None]
    key_ids = lax.dynamic_slice_in_dim(ids, first_key, span, 0)
    allowed = (offset >= 0) & (offset < WINDOW_TOKENS) & (doc_ids[0][None, :] == key_ids[:, None])
    bias = jnp.where(allowed, 0.0, masked_score).astype(f32)
    q_heads = queries.reshape(local, KEY_VALUE_HEADS, groups, HEAD_SIZE)
    q_t = q_heads.transpose(1, 3, 2, 0).reshape(KEY_VALUE_HEADS, HEAD_SIZE, groups * local)
    q_rows = q_heads.transpose(1, 2, 0, 3).reshape(KEY_VALUE_HEADS, groups * local, HEAD_SIZE)
    k_rows, k_t = keys.transpose(1, 0, 2), keys.transpose(1, 2, 0)
    v_rows, v_t = values.transpose(1, 0, 2), values.transpose(1, 2, 0)
    attended_t, lse = attention_forward(q_t, k_rows, v_t, bias)

    def heads_to_rows(value):
        value = value.reshape(KEY_VALUE_HEADS, HEAD_SIZE, groups, local)
        return value.transpose(3, 0, 2, 1).reshape(local, query_w)

    attended = heads_to_rows(attended_t)
    attn_normed, attn_scale = rms_norm(attended, attn_gain)
    attn_c = lax.all_to_all(attn_normed.astype(bf16), "seq", 1, 0, tiled=True)

    conv_w, conv_b, step_b, decay_l, skip_g, mamba_g = (
        own_cols(v) for v in (conv_weight, conv_bias, step_bias, decay_log, skip_gain, mamba_gain)
    )
    padded_inputs = jnp.pad(inputs, ((KC - 1, 0), (0, 0)))
    padded_ids = jnp.pad(ids, (KC - 1, 0), constant_values=-1)
    conv_sum = conv_b + jnp.zeros_like(inputs)
    same_masks = []
    for tap in range(KC):
        begin = KC - 1 - tap
        same = (padded_ids[begin : begin + length] == ids).astype(f32)[:, None]
        same_masks.append(same)
        conv_sum = conv_sum + conv_w[tap] * padded_inputs[begin : begin + length] * same
    activated_b = jax.nn.silu(conv_sum).astype(bf16)
    activated = activated_b.astype(f32)
    selected = lax.psum(dot_nt(activated_b, select_own), "seq")
    step_raw = selected[:, :DTR].astype(bf16)
    b_t = selected[:, DTR : DTR + NS].T
    c_t = selected[:, DTR + NS :].T
    step_pre = matmul(step_raw, step_own) + step_b
    step_size = jax.nn.softplus(step_pre)
    rate = -jnp.exp(decay_l)
    changed = jnp.concatenate([jnp.zeros((1,), f32), (ids[1:] != ids[:-1]).astype(f32)])
    step_keep = step_size + 1e30 * changed[:, None]
    push = step_size * activated
    scan_out, states = scan_forward(step_keep, push, b_t, c_t, rate)
    mamba_pre = scan_out + skip_g * activated
    gate_sig = jax.nn.sigmoid(gate_z)
    mamba_out = mamba_pre * gate_z * gate_sig
    square_sum = lax.psum(jnp.sum(mamba_out * mamba_out, -1), "seq")
    mamba_scale = lax.rsqrt(square_sum / DI + norm_eps)[:, None]
    mamba_normed = mamba_out * mamba_scale * mamba_g
    joined = jnp.concatenate([attn_c, mamba_normed.astype(bf16)], 1)
    mixed = lax.psum_scatter(matmul(joined, out_full).astype(bf16), "seq", scatter_dimension=0, tiled=True)
    hidden = seq_x + 0.5 * mixed.astype(f32)
    normed_two, scale_two = rms_norm(hidden, second_gain)
    normed_two = lax.all_gather(normed_two.astype(bf16), "seq", axis=0, tiled=True)
    gate_up_out = matmul(normed_two, gu_full).astype(bf16)
    gate_part = gate_up_out[:, :f_own].astype(f32)
    up_part = gate_up_out[:, f_own:].astype(f32)
    gate_act = jax.nn.sigmoid(gate_part)
    inner = (gate_part * gate_act * up_part).astype(bf16)
    ffn = lax.psum_scatter(matmul(inner, down_full).astype(bf16), "seq", scatter_dimension=0, tiled=True)
    out_tokens = (hidden + ffn.astype(f32)).astype(bf16)

    d_ffn = lax.all_gather(cotangent[0], "seq", axis=0, tiled=True)
    down_term = dot_tn(inner, d_ffn).astype(bf16)
    d_inner = dot_nt(d_ffn, down_full)
    d_gate_up = jnp.concatenate(
        [
            d_inner * up_part * gate_act * (1.0 + gate_part * (1.0 - gate_act)),
            d_inner * gate_part * gate_act,
        ],
        1,
    ).astype(bf16)
    gate_up_term = dot_tn(normed_two, d_gate_up).astype(bf16)
    d_normed_two = lax.psum_scatter(
        dot_nt(d_gate_up, gu_full).astype(bf16), "seq", scatter_dimension=0, tiled=True
    ).astype(f32)
    d_hidden_part, second_grad = norm_back(hidden, scale_two, second_gain, d_normed_two)
    d_hidden = cotangent[0].astype(f32) + d_hidden_part
    d_mixed = lax.all_gather(d_hidden.astype(bf16), "seq", axis=0, tiled=True)
    out_term = (0.5 * dot_tn(joined, d_mixed)).astype(bf16)
    d_joined = 0.5 * dot_nt(d_mixed, out_full)

    d_attn = lax.all_to_all(d_joined[:, :q_own].astype(bf16), "seq", 0, 1, tiled=True).astype(f32)
    d_attended, attn_grad = norm_back(attended, attn_scale, attn_gain, d_attn)
    do_heads = d_attended.astype(bf16).reshape(local, KEY_VALUE_HEADS, groups, HEAD_SIZE)
    do_t = do_heads.transpose(1, 3, 2, 0).reshape(KEY_VALUE_HEADS, HEAD_SIZE, groups * local)
    do_rows = do_heads.transpose(1, 2, 0, 3).reshape(KEY_VALUE_HEADS, groups * local, HEAD_SIZE)
    dq_t, dk, dv = attention_backward(q_rows, q_t, k_rows, k_t, v_rows, do_rows, do_t, lse, bias)
    d_queries = lax.all_to_all(heads_to_rows(dq_t).astype(bf16), "seq", 1, 0, tiled=True)
    dk = dk.transpose(1, 0, 2).reshape(span, n, k_own)
    dv = dv.transpose(1, 0, 2).reshape(span, n, k_own)
    dkv = jnp.concatenate([dk, dv], 2).transpose(1, 0, 2).astype(bf16)
    dkv = lax.dynamic_update_slice_in_dim(jnp.zeros((n, length, 2 * k_own), bf16), dkv, first_key, 1)
    dkv = lax.psum_scatter(dkv, "seq", scatter_dimension=0, tiled=True)[0]

    u = d_joined[:, q_own:]
    weighted = u * mamba_g
    inner_mean = lax.psum(jnp.sum(weighted * mamba_out, -1), "seq")[:, None] / DI
    mamba_grad = jnp.sum(u * mamba_out * mamba_scale, 0)
    d_mamba = mamba_scale * weighted - mamba_out * (mamba_scale * mamba_scale * mamba_scale) * inner_mean
    d_pre = d_mamba * gate_z * gate_sig
    d_gate = d_mamba * mamba_pre * gate_sig * (1.0 + gate_z * (1.0 - gate_sig))
    skip_grad = jnp.sum(d_pre * activated, 0)
    by_rate, pushed, db_t, dc_t, decay_log_grad = scan_backward(
        step_keep, push, d_pre, b_t, c_t, states, rate
    )
    step_grads = by_rate + pushed * activated
    d_step_pre = step_grads * jax.nn.sigmoid(step_pre)
    step_bias_grad = jnp.sum(d_step_pre, 0)
    d_step_low = d_step_pre.astype(bf16)
    step_term = dot_tn(step_raw, d_step_low)
    d_selected = jnp.concatenate([dot_nt(d_step_low, step_own), db_t.T, dc_t.T], 1)
    d_selected = lax.psum(d_selected, "seq").astype(bf16)
    select_term = dot_tn(d_selected, activated_b)
    d_activated = d_pre * skip_g + pushed * step_size + matmul(d_selected, select_own)
    conv_sig = jax.nn.sigmoid(conv_sum)
    d_conv = d_activated * conv_sig * (1.0 + conv_sum * (1.0 - conv_sig))
    conv_bias_grad = jnp.sum(d_conv, 0)
    ext_grad = jnp.zeros((length + KC - 1, c_own), f32)
    conv_rows = []
    for tap in range(KC):
        begin = KC - 1 - tap
        masked_grad = d_conv * same_masks[tap]
        conv_rows.append(jnp.sum(masked_grad * padded_inputs[begin : begin + length], 0))
        ext_grad = ext_grad + jnp.pad(conv_w[tap] * masked_grad, ((begin, tap), (0, 0)))
    d_inputs = ext_grad[KC - 1 :]
    d_projected = jnp.concatenate([d_queries, dkv, d_inputs.astype(bf16), d_gate.astype(bf16)], 1)
    in_term = dot_tn(normed_one, d_projected).astype(bf16)
    d_normed_one = lax.psum_scatter(
        dot_nt(d_projected, in_full).astype(bf16), "seq", scatter_dimension=0, tiled=True
    ).astype(f32)
    d_x_part, first_grad = norm_back(seq_x, scale_one, first_gain, d_normed_one)
    tokens_grad = (d_hidden + d_x_part).astype(bf16)

    down_sum = lax.all_to_all(
        down_term.reshape(f_own, n, -1).transpose(1, 0, 2), "seq", 0, 0, tiled=False
    ).reshape(F, -1)
    down_sum = lax.psum_scatter(down_sum, "fsdp", scatter_dimension=0, tiled=True).astype(f32)
    out_sum = lax.all_to_all(
        out_term.reshape(q_own + c_own, n, -1).transpose(1, 0, 2), "seq", 0, 0, tiled=False
    )
    out_sum = jnp.concatenate(
        [out_sum[:, :q_own].reshape(query_w, -1), out_sum[:, q_own:].reshape(DI, -1)], 0
    )
    out_sum = lax.psum_scatter(out_sum, "fsdp", scatter_dimension=0, tiled=True).astype(f32)
    gu_sum = lax.psum_scatter(gate_up_term, "fsdp", scatter_dimension=0, tiled=True)
    gate_g, up_g = gu_sum[:, :f_own], gu_sum[:, f_own:]
    back_a = lax.ppermute(jnp.where(even, gate_g, up_g), "seq", [(t, s) for s, t in route_a])
    back_b = lax.ppermute(jnp.where(even, up_g, gate_g), "seq", [(t, s) for s, t in route_b])
    gu_sum = jnp.concatenate(
        [jnp.where(low_half, back_a, back_b), jnp.where(low_half, back_b, back_a)], 1
    ).astype(f32)
    in_part = lax.psum_scatter(in_term, "fsdp", scatter_dimension=0, tiled=True)
    in_sum = jnp.zeros((in_part.shape[0], sum(widths) * n), bf16)
    for s, w, e in zip(starts, widths, edges):
        in_sum = lax.dynamic_update_slice_in_dim(in_sum, in_part[:, e : e + w], s + me * w, 1)
    in_sum = lax.psum_scatter(in_sum, "seq", scatter_dimension=1, tiled=True).astype(f32)
    select_sum = lax.psum_scatter(select_term.astype(bf16), "fsdp", scatter_dimension=0, tiled=True).astype(f32)
    step_sum = lax.psum_scatter(step_term.astype(bf16), "fsdp", scatter_dimension=0, tiled=True).astype(f32)

    wide = jnp.stack([first_grad, second_grad, attn_grad])
    channel = jnp.concatenate(
        [
            mamba_grad[None], jnp.stack(conv_rows), conv_bias_grad[None], step_bias_grad[None],
            decay_log_grad, skip_grad[None],
        ],
        0,
    )
    wide = lax.psum(wide, ("seq", "fsdp"))
    channel = lax.all_gather(lax.psum(channel, "fsdp"), "seq", axis=1, tiled=True)
    return (
        out_tokens[None],
        tokens_grad[None],
        in_sum,
        out_sum,
        gu_sum,
        down_sum,
        select_sum,
        step_sum,
        wide[0],
        wide[1],
        wide[2],
        channel[0],
        channel[1 : 1 + KC],
        channel[1 + KC],
        channel[2 + KC],
        channel[3 + KC : 3 + KC + NS],
        channel[3 + KC + NS],
    )


def solution(mesh):
    split = P("fsdp", "seq")
    seq3 = P("fsdp", "seq", None)
    return jax.shard_map(
        functools.partial(layer, mesh.shape["seq"], mesh.shape["fsdp"]),
        mesh=mesh,
        in_specs=(seq3,) + (split,) * 7 + (P(),) * 9 + (seq3,),
        out_specs=(seq3, seq3) + (split,) * 6 + (P(),) * 9,
        check_vma=False,
    )
```

time: 5020 us -> 1800 us (0.36)
  local copies, waits for them, and re-layouts: 1690 us -> 247 us
  other arithmetic: 1290 us -> 118 us
  waiting for transfers between devices: 1540 us -> 670 us
  Pallas kernels: 0 us -> 230 us
  blocking collectives: 66.7 us -> 291 us
  matrix products: 294 us -> 175 us
    pad x192 -> x0, local copies, waits for them, and re-layouts: 1030 us -> none  [the longest x128 657 us: block_states(): _, states = lax.associative_scan(combine_pair, (decays, pushes))]
    unnamed x30 -> x26, waiting for transfers between devices: 834 us -> 101 us
    add x217 -> x2, other arithmetic: 509 us -> 0.01 us  [the longest x1 0.01 us: layer(): query_pos = me * local + jnp.arange(local, dtype=jnp.int32)]
    psum x2 -> x1, waiting for transfers between devices: 258 us -> 0.57 us  [layer(): selected = lax.psum(dot_nt(activated_b, select_own), 'seq')]
    pallas_call x0 -> x4, Pallas kernels: none -> 230 us  [the longest x1 117 us: scan_backward(): pl.pallas_call(scan_bwd_body, grid=(tokens // block,), in_specs=[rows, ro...]
    mul x131 -> x4, other arithmetic: 226 us -> 2.95 us  [the longest x1 1.49 us: scan_forward(): rate * log2e]
    reduce_sum x50 -> x4, other arithmetic: 230 us -> 26.7 us  [the longest x1 12.3 us: layer(): skip_grad = jnp.sum(d_pre * activated, 0)]
    while x947 -> x0, local copies, waits for them, and re-layouts: 194 us -> none
  transfers between devices with their start and end apart: 50 -> 33, of which waited for: 31 -> 17; matrix products, arithmetic and copies ran while one was open for 28% -> 22% of each run, Pallas kernels for 0% -> 11%
where the time goes in v1:
time: 1800 us; the launch traced here: 1790 us
  waiting for transfers between devices  670 us (37%)
  blocking collectives  291 us (16%)
  local copies, waits for them, and re-layouts  247 us (14%)
  Pallas kernels  230 us (13%)
  matrix products  175 us (10%)
  other arithmetic  118 us (7%)
  starting transfers between devices  42.7 us (2%)
    pallas_call x1, Pallas kernels, scan_backward(): pl.pallas_call(scan_bwd_body, grid=(tokens // block,), in_specs=[rows, ro...  117 us
    unnamed x26, waiting for transfers between devices  101 us
    unnamed x216, local copies, waits for them, and re-layouts  84.9 us
    all_gather x1, waiting for transfers between devices, layer(): in_full = lax.all_gather(in_cols, 'fsdp', axis=0, tiled=True)  74.6 us
    dot_general x6, matrix products, matmul(): return jnp.dot(left, right, preferred_element_type=f32)  74.3 us
    all_gather x1, waiting for transfers between devices, layer(): gu_full = lax.all_gather(gu_cols, 'fsdp', axis=0, tiled=True)  69.1 us
    reduce_scatter x1, waiting for transfers between devices, layer(): lax.psum_scatter(dot_nt(d_gate_up, gu_full).astype(bf16), 'seq', scatter_...  63 us
    psum x1, blocking collectives, layer(): d_selected = lax.psum(d_selected, 'seq').astype(bf16)  59.6 us
  transfers between devices with their start and end apart: 33, of which 17 were waited for; matrix products, arithmetic and copies ran while one was open for 22% of the time, Pallas kernels for 11%

profile of v1, /device:TPU:0, one launch (start us, length us, event | category | flops | bytes accessed | tf_op | source)
XLA Modules:
  0.0 1788.3 jit_solution(16231193538250389714)
XLA Ops:
  12.9 49.8 %all-gather.34.cloned.1.call-done = bf16[8,1080,400]{1,2,0:T(8,128)(2,1)} async-done(((bf16[1,1080,400]{1,2,0:T(8,128)(2,1)}), bf16[8,1080,400]{1,2,0:T(8,128)(2,1)}) %all-gather.34.cloned.1.call-update) | async-done | bytes 6912016 | tf_op jit(solution)/shard_map/all_gather | solution.py:341
  89.9 23.1 %all-gather.20.cloned.1.call-done = bf16[2048,1600]{0,1:T(8,128)(2,1)} async-done(((bf16[256,1600]{0,1:T(8,128)(2,1)}), bf16[2048,1600]{0,1:T(8,128)(2,1)}) %all-gather.20.cloned.1.call-update) | async-done | bytes 6553616 | tf_op jit(solution)/shard_map/all_gather | solution.py:373
  113.1 74.6 %all-gather.22.cloned.1.call-done = bf16[1600,1080]{1,0:T(8,128)(2,1)} async-done(((bf16[400,1080]{1,0:T(8,128)(2,1)}), bf16[1600,1080]{1,0:T(8,128)(2,1)}) %all-gather.22.cloned.1.call-update) | async-done | bytes 3456016 | tf_op jit(solution)/shard_map/all_gather | solution.py:345
  306.0 24.4 %attention_forward.1 = (f32[5,64,1280]{2,1,0:T(8,128)S(1)}, f32[5,1,1280]{2,1,0:T(1,128)S(1)}) custom-call(bf16[5,64,1280]{2,1,0:T(8,128)(2,1)S(1)} %bitcast.216, bf16[5,1280,64]{2,1,0:T(8,128)(2,1)S(1)} %copy.158.k_ref, bf16[5,64,1280]{2,1,0:T(8,128)(2,1)S(1)} %bitcast.211, f32[1280,256]{1,0:T(8,128)S(1)} %copy-done.12), custom_call_target="tpu_custom_call" | custom-call | flops 4194304000 | bytes 8388608 | tf_op jit(solution)/shard_map/attention_forward/pallas_call | solution.py:265
  352.6 57.3 %scan_forward.1 = (f32[2048,400]{1,0:T(8,128)S(1)}, f32[2048,16,400]{2,1,0:T(8,128)}) custom-call(f32[2048,400]{1,0:T(8,128)S(1)} %get-tuple-element.86.step_ref, f32[2048,400]{1,0:T(8,128)S(1)} %get-tuple-element.85.push_ref, f32[16,2048]{1,0:T(8,128)S(1)} %get-tuple-element.101.b_ref, f32[16,2048]{1,0:T(8,128)S(1)} %get-tuple-element.100.c_ref, ...), custom_call_target="tpu_custom_call" | custom-call | flops 104857600 | bytes 52428800 | tf_op jit(solution)/shard_map/scan_forward/pallas_call | solution.py:168
  426.0 27.4 %psum.43 = f32[2048]{0:T(1024)} all-reduce(f32[2048]{0:T(1024)S(1)} %get-tuple-element.69), channel_id=1, replica_groups=mesh['seq'=8,'fsdp'=4] {'seq'}, use_global_device_ids=true, to_apply=%region_4.5 | all-reduce | flops 2048 | bytes 16384 | tf_op jit(solution)/shard_map/psum | solution.py:440
  495.4 38.8 %reduce-scatter.21.cloned.1.call-done = bf16[256,1600]{0,1:T(8,128)(2,1)} async-done(((bf16[2048,1600]{0,1:T(8,128)(2,1)}), bf16[256,1600]{0,1:T(8,128)(2,1)}) %reduce-scatter.21.cloned.1.call-update) | async-done | bytes 819216 | tf_op jit(solution)/shard_map/reduce_scatter | solution.py:444
  540.5 44.1 %all-gather.38.cloned.1.call-done = bf16[4,1376,200]{1,2,0:T(8,128)(2,1)} async-done(((bf16[1,1376,200]{1,2,0:T(8,128)(2,1)}), bf16[4,1376,200]{1,2,0:T(8,128)(2,1)}) %all-gather.38.cloned.1.call-update) | async-done | bytes 2201616 | tf_op jit(solution)/shard_map/all_gather | solution.py:366
  602.5 69.1 %all-gather.26.cloned.1.call-done = bf16[1600,1376]{1,0:T(8,128)(2,1)} async-done(((bf16[400,1376]{1,0:T(8,128)(2,1)}), bf16[1600,1376]{1,0:T(8,128)(2,1)}) %all-gather.26.cloned.1.call-update) | async-done | bytes 4403216 | tf_op jit(solution)/shard_map/all_gather | solution.py:358
  671.6 48.8 %all-gather.24.cloned.1.call-done = bf16[2048,1600]{0,1:T(8,128)(2,1)} async-done(((bf16[256,1600]{0,1:T(8,128)(2,1)}), bf16[2048,1600]{0,1:T(8,128)(2,1)}) %all-gather.24.cloned.1.call-update) | async-done | bytes 6553616 | tf_op jit(solution)/shard_map/all_gather | solution.py:447
  735.9 34.4 %all-gather.32.cloned.1.call-done = bf16[1,2048,1600]{1,2,0:T(8,128)(2,1)} async-done(((bf16[1,256,1600]{1,2,0:T(8,128)(2,1)}), bf16[1,2048,1600]{1,2,0:T(8,128)(2,1)}) %all-gather.32.cloned.1.call-update) | async-done | bytes 6553616 | tf_op jit(solution)/shard_map/all_gather | solution.py:456
  797.0 63.0 %reduce-scatter.25.cloned.1.call-done = bf16[256,1600]{0,1:T(8,128)(2,1)} async-done(((bf16[2048,1600]{0,1:T(8,128)(2,1)}), bf16[256,1600]{0,1:T(8,128)(2,1)}) %reduce-scatter.25.cloned.1.call-update) | async-done | bytes 819216 | tf_op jit(solution)/shard_map/reduce_scatter | solution.py:467
  874.2 40.9 %all-gather.28.cloned.1.call-done = bf16[2048,1600]{0,1:T(8,128)(2,1)} async-done(((bf16[256,1600]{0,1:T(8,128)(2,1)}), bf16[2048,1600]{0,1:T(8,128)(2,1)}) %all-gather.28.cloned.1.call-update) | async-done | bytes 6553616 | tf_op jit(solution)/shard_map/all_gather | solution.py:472
  960.2 117.2 %scan_backward.1 = (f32[2048,400]{1,0:T(8,128)S(1)}, f32[2048,400]{1,0:T(8,128)S(1)}, f32[16,2048]{1,0:T(8,128)S(1)}, f32[16,2048]{1,0:T(8,128)S(1)}, f32[16,400]{1,0:T(8,128)S(1)}) custom-call(f32[2048,400]{1,0:T(8,128)S(1)} %copy-done.2, f32[2048,400]{1,0:T(8,128)} %copy-done, f32[2048,400]{1,0:T(8,128)} %get-tuple-element.66.dpre_ref, ...), custom_call_target="tpu_custom_call" | custom-call | flops 235929600 | bytes 52428800 | tf_op jit(solution)/shard_map/scan_backward/pallas_call | solution.py:194
  1104.7 30.8 %attention_backward.1 = (f32[5,64,1280]{2,1,0:T(8,128)S(1)}, f32[5,1280,64]{2,1,0:T(8,128)}, f32[5,1280,64]{2,1,0:T(8,128)}) custom-call(bf16[5,1280,64]{2,1,0:T(8,128)(2,1)S(1)} %bitcast.213, bf16[5,64,1280]{2,1,0:T(8,128)(2,1)S(1)} %bitcast.217, bf16[5,1280,64]{2,1,0:T(8,128)(2,1)S(1)} %copy.158.k_ref, bf16[5,64,1280]{2,1,0:T(8,128)(2,1)S(1)} %bitcast.210, ...), custom_call_target="tpu_custom_call" | custom-call | flops 10485760000 | bytes 16777216 | tf_op jit(solution)/shard_map/attention_backward/pallas_call | solution.py:286
  1178.7 59.6 %all-reduce.15 = bf16[2048,132]{0,1:T(8,128)(2,1)S(1)} all-reduce(f32[2048,132]{0,1:T(8,128)S(1)} %pad_maximum_fusion.9), channel_id=1, replica_groups=mesh['seq'=8,'fsdp'=4] {'seq'}, use_global_device_ids=true, to_apply=%region_14.15 | all-reduce | flops 270336 | bytes 1622016 | tf_op jit(solution)/shard_map/psum | solution.py:506
  1328.3 34.6 %all_to_all.78 = bf16[8,688,200]{1,2,0:T(8,128)(2,1)S(1)} all-to-all(bf16[8,688,200]{1,2,0:T(8,128)(2,1)} %bitcast.227), channel_id=1, replica_groups=mesh['seq'=8,'fsdp'=4] {'seq'}, dimensions={0} | all-to-all | bytes 4403200 | tf_op jit(solution)/shard_map/all_to_all | solution.py:528
  1377.4 29.6 %all_to_all.79 = bf16[8,600,200]{1,2,0:T(8,128)(2,1)S(1)} all-to-all(bf16[8,600,200]{1,2,0:T(8,128)(2,1)} %bitcast.228), channel_id=1, replica_groups=mesh['seq'=8,'fsdp'=4] {'seq'}, dimensions={0} | all-to-all | bytes 3840000 | tf_op jit(solution)/shard_map/all_to_all | solution.py:532
  1485.7 24.5 %reduce-scatter.39.cloned.1.call-done = bf16[1376,200]{1,0:T(8,128)(2,1)} async-done(((bf16[5504,200]{1,0:T(8,128)(2,1)}), bf16[1376,200]{1,0:T(8,128)(2,1)}) %reduce-scatter.39.cloned.1.call-update) | async-done | bytes 550416
  1516.5 19.6 %psum.47 = f32[24,400]{1,0:T(8,128)S(1)} all-reduce(f32[24,400]{1,0:T(8,128)S(1)} %concatenate.54), channel_id=1, replica_groups=mesh['seq'=8,'fsdp'=4] {'fsdp'}, use_global_device_ids=true, to_apply=%region_36.37 | all-reduce | flops 9600 | bytes 76800 | tf_op jit(solution)/shard_map/psum | solution.py:563
  1590.7 43.0 %reduce-scatter.29.cloned.1.call-done = bf16[256,1600]{0,1:T(8,128)(2,1)} async-done(((bf16[2048,1600]{0,1:T(8,128)(2,1)}), bf16[256,1600]{0,1:T(8,128)(2,1)}) %reduce-scatter.29.cloned.1.call-update) | async-done | bytes 819216 | tf_op jit(solution)/shard_map/reduce_scatter | solution.py:522
  1635.7 39.9 %psum.46 = f32[3,1600]{1,0:T(4,128)S(1)} all-reduce(f32[3,1600]{1,0:T(4,128)S(1)} %pad_maximum_fusion.10), channel_id=1, replica_groups=mesh['seq'=8,'fsdp'=4] {'seq','fsdp'}, use_global_device_ids=true, to_apply=%region_27.28 | all-reduce | flops 4800 | bytes 38400 | tf_op jit(solution)/shard_map/psum | solution.py:562
  1676.2 24.4 %reduce-scatter.23.cloned.1.call-done = bf16[256,1600]{0,1:T(8,128)(2,1)} async-done(((bf16[2048,1600]{0,1:T(8,128)(2,1)}), bf16[256,1600]{0,1:T(8,128)(2,1)}) %reduce-scatter.23.cloned.1.call-update) | async-done | bytes 819216 | tf_op jit(solution)/shard_map/reduce_scatter | solution.py:453
  1704.2 74.0 %reduce-scatter.35.cloned.1.call-done = bf16[1080,400]{1,0:T(8,128)(2,1)} async-done(((bf16[8640,400]{1,0:T(8,128)(2,1)}), bf16[1080,400]{1,0:T(8,128)(2,1)}) %reduce-scatter.35.cloned.1.call-update) | async-done | bytes 864016
  (449 shorter events, 678.9 us)
Async XLA Ops:
  7.2 55.6 %all-gather.34.cloned.1.call-start = ((), (), s32[]{:S(2)}) async-start(), calls=%async_computation.33 | async-start | bytes 8294400 | tf_op jit(solution)/shard_map/all_gather | solution.py:341
  7.9 105.1 %all-gather.20.cloned.1.call-start = ((), (), s32[]{:S(2)}) async-start(), calls=%async_computation.18 | async-start | bytes 7372800 | tf_op jit(solution)/shard_map/all_gather | solution.py:373
  12.9 174.8 %all-gather.22.cloned.1.call-start = ((), (), s32[]{:S(2)}) async-start(), calls=%async_computation.19 | async-start | bytes 4608000 | tf_op jit(solution)/shard_map/all_gather | solution.py:345
  89.3 165.3 %all-gather.36.cloned.1.call-start = ((), (), s32[]{:S(2)}) async-start(), calls=%async_computation.34 | async-start | bytes 2560000 | tf_op jit(solution)/shard_map/all_gather | solution.py:360
  89.9 202.2 %all-gather.30.cloned.1.call-start = ((), (), s32[]{:S(2)}) async-start(), calls=%async_computation.31 | async-start | bytes 4718592 | tf_op jit(solution)/shard_map/all_gather | solution.py:384
  277.3 67.5 %all-reduce.14.cloned.1.call-start = ((), (), s32[]{:S(2)}) async-start(), calls=%async_computation.20 | async-start | bytes 2228224 | tf_op jit(solution)/shard_map/psum | solution.py:426
  339.9 76.0 %all-to-all-start.1 = ((bf16[256,8,200]{0,2,1:T(8,128)(2,1)}), bf16[256,8,200]{0,2,1:T(8,128)(2,1)}, u32[]{:S(2)}, u32[]{:S(2)}) async-start(bf16[256,8,200]{0,2,1:T(8,128)(2,1)} %multiply_convert_fusion.4), calls=%async_computation.1 | async-start | bytes 1638400 | tf_op jit(solution)/shard_map/all_to_all | solution.py:410
  420.2 114.0 %reduce-scatter.21.cloned.1.call-start = ((), (), s32[]{:S(2)}) async-start(), calls=%async_computation.21 | async-start | bytes 7372800 | tf_op jit(solution)/shard_map/reduce_scatter | solution.py:444
  470.6 114.0 %all-gather.38.cloned.1.call-start = ((), (), s32[]{:S(2)}) async-start(), calls=%async_computation.35 | async-start | bytes 2816000 | tf_op jit(solution)/shard_map/all_gather | solution.py:366
  471.3 200.3 %all-gather.26.cloned.1.call-start = ((), (), s32[]{:S(2)}) async-start(), calls=%async_computation.23 | async-start | bytes 5632000 | tf_op jit(solution)/shard_map/all_gather | solution.py:358
  495.3 225.0 %all-gather.24.cloned.1.call-start = ((), (), s32[]{:S(2)}) async-start(), calls=%async_computation.22 | async-start | bytes 7372800 | tf_op jit(solution)/shard_map/all_gather | solution.py:447
  539.8 230.5 %all-gather.32.cloned.1.call-start = ((), (), s32[]{:S(2)}) async-start(), calls=%async_computation.32 | async-start | bytes 7372800 | tf_op jit(solution)/shard_map/all_gather | solution.py:456
  597.6 138.2 %all-to-all-start.3 = ((bf16[8,688,200]{1,2,0:T(8,128)(2,1)}), bf16[8,688,200]{1,2,0:T(8,128)(2,1)}, u32[]{:S(2)}, u32[]{:S(2)}) async-start(bf16[8,688,200]{1,2,0:T(8,128)(2,1)} %copy.166), calls=%async_computation.4 | async-start | bytes 4915200 | tf_op jit(solution)/shard_map/all_to_all | solution.py:367
  602.0 257.9 %reduce-scatter.25.cloned.1.call-start = ((), (), s32[]{:S(2)}) async-start(), calls=%async_computation.25 | async-start | bytes 7372800 | tf_op jit(solution)/shard_map/reduce_scatter | solution.py:467
  796.8 118.3 %all-gather.28.cloned.1.call-start = ((), (), s32[]{:S(2)}) async-start(), calls=%async_computation.26 | async-start | bytes 7372800 | tf_op jit(solution)/shard_map/all_gather | solution.py:472
  944.2 139.2 %all-to-all-start.4 = ((bf16[8,256,200]{1,2,0:T(8,128)(2,1)}), bf16[8,256,200]{1,2,0:T(8,128)(2,1)S(1)}, u32[]{:S(2)}, u32[]{:S(2)}) async-start(bf16[8,256,200]{1,2,0:T(8,128)(2,1)} %copy.170), calls=%async_computation.7 | async-start | bytes 1638400 | tf_op jit(solution)/shard_map/all_to_all | solution.py:476
  947.7 326.8 %reduce-scatter.27.cloned.1.call-start = ((), (), s32[]{:S(2)}) async-start(), calls=%async_computation.27 | async-start | bytes 4718592 | tf_op jit(solution)/shard_map/reduce_scatter | solution.py:487
  1244.5 198.8 %reduce-scatter.31.cloned.1.call-start = ((), (), s32[]{:S(2)}) async-start(), calls=%async_computation.29 | async-start | bytes 4608000 | tf_op jit(solution)/shard_map/reduce_scatter | solution.py:546
  1297.3 179.8 %reduce-scatter.33.cloned.1.call-start = ((), (), s32[]{:S(2)}) async-start(), calls=%async_computation.30 | async-start | bytes 5632000 | tf_op jit(solution)/shard_map/reduce_scatter | solution.py:539
  1312.3 198.0 %reduce-scatter.39.cloned.1.call-start = ((), (), s32[]{:S(2)}) async-start(), calls=%async_computation.38 | async-start | bytes 3522560
  1365.6 220.9 %reduce-scatter.37.cloned.1.call-start = ((), (), s32[]{:S(2)}) async-start(), calls=%async_computation.37 | async-start | bytes 3072000
  1419.1 214.6 %reduce-scatter.29.cloned.1.call-start = ((), (), s32[]{:S(2)}) async-start(), calls=%async_computation.28 | async-start | bytes 7372800 | tf_op jit(solution)/shard_map/reduce_scatter | solution.py:522
  1432.9 267.7 %reduce-scatter.23.cloned.1.call-start = ((), (), s32[]{:S(2)}) async-start(), calls=%async_computation.24 | async-start | bytes 7372800 | tf_op jit(solution)/shard_map/reduce_scatter | solution.py:453
  1443.2 335.0 %reduce-scatter.35.cloned.1.call-start = ((), (), s32[]{:S(2)}) async-start(), calls=%async_computation.36 | async-start | bytes 9953280
  (111 other events, 3211.8 us)
Sparse Core Ops, SparseCore 0:
  9.9 52.7 all-gather.33
  65.2 47.8 all-gather.19
  115.2 72.3 all-gather.21
  189.1 48.2 all-gather.35
  239.7 35.5 all-gather.29
  288.9 55.9 all-reduce.13
  470.7 63.4 reduce-scatter.20
  535.9 48.6 all-gather.37
  586.8 84.7 all-gather.25
  674.0 46.3 all-gather.23
  722.4 47.8 all-gather.31
  796.9 63.0 reduce-scatter.24
  867.2 47.8 all-gather.27
  1171.0 60.6 reduce-scatter.26
  1297.4 70.2 reduce-scatter.30
  1370.0 82.3 reduce-scatter.32
  1454.5 55.6 reduce-scatter.38
  1512.5 53.7 reduce-scatter.36
  1570.1 63.5 reduce-scatter.28
  1637.0 63.5 reduce-scatter.22
  1704.6 73.5 reduce-scatter.34

commit v2 on v1

v2 whole, which is shorter than its diff:
```python
import functools

import jax
import jax.numpy as jnp
from jax import lax
from jax.experimental import pallas as pl
from jax.experimental.pallas import tpu as pltpu
from jax.sharding import PartitionSpec as P

QUERY_HEADS = 25
KEY_VALUE_HEADS = 5
HEAD_SIZE = 64
DI = 3200
NS = 16
DTR = 100
KC = 4
F = 5504
WINDOW_TOKENS = 1024

norm_eps = 1e-05
masked_score = -1e30
log2e = 1.4426950408889634
bf16 = jnp.bfloat16
f32 = jnp.float32
MESH = pl.DeviceIdType.MESH


def matmul(left, right):
    return jnp.dot(left, right, preferred_element_type=f32)


def dot_tn(left, right):
    return lax.dot_general(left, right, (((0,), (0,)), ((), ())), preferred_element_type=f32)


def dot_nt(left, right):
    return lax.dot_general(left, right, (((1,), (1,)), ((), ())), preferred_element_type=f32)


def rms_norm(value, gain):
    scale = lax.rsqrt(jnp.mean(value * value, axis=-1, keepdims=True) + norm_eps)
    return (value * scale * gain, scale)


def norm_back(value, scale, gain, upstream):
    weighted = upstream * gain
    gain_grad = jnp.sum(upstream * value * scale, 0)
    inner_mean = jnp.mean(weighted * value, axis=-1, keepdims=True)
    return (scale * weighted - value * (scale * scale * scale) * inner_mean, gain_grad)


def park(part, j, value):
    for k, lane in enumerate(range(0, value.shape[1], 128)):
        end = min(lane + 128, value.shape[1])
        part[64 * k + 8 * j : 64 * k + 8 * j + 8, : end - lane] = value[:, lane:end]


def fold(part, out, t0):
    for k, lane in enumerate(range(0, out.shape[1], 128)):
        end = min(lane + 128, out.shape[1])
        total = part[pl.ds(64 * k, 8, stride=8), :]
        for s in range(1, 8):
            total = total + part[pl.ds(64 * k + s, 8, stride=8), :]
        out[pl.ds(t0, 8), lane:end] = total[:, : end - lane]


def scan_fwd_body(step_ref, push_ref, b_ref, c_ref, rate_ref, y_ref, st_ref, h_scr, part_scr):
    block = step_ref.shape[0]

    @pl.when(pl.program_id(0) == 0)
    def _():
        h_scr[...] = jnp.zeros_like(h_scr)

    rate = rate_ref[...]

    def group(index, state):
        t0 = pl.multiple_of(index * 8, 8)
        step8 = step_ref[pl.ds(t0, 8), :]
        push8 = push_ref[pl.ds(t0, 8), :]
        b_roll = pltpu.roll(b_ref[...], block - t0, 1)
        c_roll = pltpu.roll(c_ref[...], block - t0, 1)
        for j in range(8):
            decay = jnp.exp2(step8[j : j + 1, :] * rate)
            state = decay * state + push8[j : j + 1, :] * b_roll[:, j : j + 1]
            st_ref[t0 + j] = state
            out = c_roll[:, j : j + 1] * state
            park(part_scr, j, out[:8] + out[8:])
        fold(part_scr, y_ref, t0)
        return state

    h_scr[...] = lax.fori_loop(0, block // 8, group, h_scr[...])


def scan_bwd_body(
    step_ref, push_ref, dpre_ref, b_ref, c_ref, st_ref, prev_ref, rate_ref,
    pr_ref, pushed_ref, db_ref, dc_ref, log_ref, g_scr, log_scr, part1, part2,
):
    block = step_ref.shape[0]
    count = pl.num_programs(0)
    which = pl.program_id(0)

    @pl.when(which == 0)
    def _():
        g_scr[...] = jnp.zeros_like(g_scr)
        log_scr[...] = jnp.zeros_like(log_scr)

    lane_ids = lax.broadcasted_iota(jnp.int32, (NS, block), 1)
    before = prev_ref[0] * jnp.where(which == count - 1, 0.0, 1.0)

    def group(turn, carried):
        grad_in, state, db_acc, dc_acc = carried
        t0 = pl.multiple_of((block // 8 - 1 - turn) * 8, 8)
        step8 = step_ref[pl.ds(t0, 8), :]
        push8 = push_ref[pl.ds(t0, 8), :]
        dpre8 = dpre_ref[pl.ds(t0, 8), :]
        b_roll = pltpu.roll(b_ref[...], block - t0, 1)
        c_roll = pltpu.roll(c_ref[...], block - t0, 1)
        rate = rate_ref[...]
        log_acc = log_scr[...]
        for j in range(7, -1, -1):
            if j > 0:
                prior = st_ref[t0 + (j - 1)]
            else:
                prior = jnp.where(t0 > 0, st_ref[jnp.maximum(t0 - 1, 0)], before)
            step_row = step8[j : j + 1, :]
            dpre_row = dpre8[j : j + 1, :]
            grad = c_roll[:, j : j + 1] * dpre_row + grad_in
            grad_in = grad * jnp.exp2(step_row * (rate * log2e))
            flow = grad_in * prior
            by_rate = flow * rate
            park(part1, j, by_rate[:8] + by_rate[8:])
            by_b = grad * b_roll[:, j : j + 1]
            park(part2, j, by_b[:8] + by_b[8:])
            log_acc = log_acc + flow * step_row
            db = jnp.sum(grad * push8[j : j + 1, :], axis=1, keepdims=True)
            dc = jnp.sum(state * dpre_row, axis=1, keepdims=True)
            here = lane_ids == t0 + j
            db_acc = jnp.where(here, db, db_acc)
            dc_acc = jnp.where(here, dc, dc_acc)
            state = prior
        log_scr[...] = log_acc
        fold(part1, pr_ref, t0)
        fold(part2, pushed_ref, t0)
        return (grad_in, state, db_acc, dc_acc)

    zero = jnp.zeros((NS, block), f32)
    grad_in, _, db_acc, dc_acc = lax.fori_loop(
        0, block // 8, group, (g_scr[...], st_ref[block - 1], zero, zero)
    )
    g_scr[...] = grad_in
    db_ref[...] = db_acc
    dc_ref[...] = dc_acc

    @pl.when(which == count - 1)
    def _():
        log_ref[...] = log_scr[...] * rate_ref[...]


SCAN_BLOCK = 128


def scan_forward(step_keep, push, b_t, c_t, rate):
    tokens, width = step_keep.shape
    block = SCAN_BLOCK
    padded = (width + 127) // 128 * 128
    rows = pl.BlockSpec((block, width), lambda i: (i, 0))
    cols = pl.BlockSpec((NS, block), lambda i: (0, i))
    fixed = pl.BlockSpec((NS, width), lambda i: (0, 0))
    return pl.pallas_call(
        scan_fwd_body,
        grid=(tokens // block,),
        in_specs=[rows, rows, cols, cols, fixed],
        out_specs=[rows, pl.BlockSpec((block, NS, width), lambda i: (i, 0, 0))],
        out_shape=[
            jax.ShapeDtypeStruct((tokens, width), f32),
            jax.ShapeDtypeStruct((tokens, NS, width), f32),
        ],
        scratch_shapes=[pltpu.VMEM((NS, width), f32), pltpu.VMEM((padded // 2, 128), f32)],
        compiler_params=pltpu.CompilerParams(vmem_limit_bytes=40 << 20),
        cost_estimate=pl.CostEstimate(
            flops=tokens * width * NS * 8, bytes_accessed=tokens * width * NS * 4, transcendentals=tokens * width * NS
        ),
        name="scan_forward",
    )(step_keep, push, b_t, c_t, rate * log2e)


def scan_backward(step_keep, push, d_pre, b_t, c_t, states, rate):
    tokens, width = step_keep.shape
    block = SCAN_BLOCK
    padded = (width + 127) // 128 * 128
    last = tokens // block - 1
    rows = pl.BlockSpec((block, width), lambda i: (last - i, 0))
    cols = pl.BlockSpec((NS, block), lambda i: (0, last - i))
    fixed = pl.BlockSpec((NS, width), lambda i: (0, 0))
    return pl.pallas_call(
        scan_bwd_body,
        grid=(tokens // block,),
        in_specs=[
            rows, rows, rows, cols, cols,
            pl.BlockSpec((block, NS, width), lambda i: (last - i, 0, 0)),
            pl.BlockSpec((1, NS, width), lambda i: (jnp.maximum((last - i) * block - 1, 0), 0, 0)),
            fixed,
        ],
        out_specs=[rows, rows, cols, cols, fixed],
        out_shape=[
            jax.ShapeDtypeStruct((tokens, width), f32),
            jax.ShapeDtypeStruct((tokens, width), f32),
            jax.ShapeDtypeStruct((NS, tokens), f32),
            jax.ShapeDtypeStruct((NS, tokens), f32),
            jax.ShapeDtypeStruct((NS, width), f32),
        ],
        scratch_shapes=[
            pltpu.VMEM((NS, width), f32),
            pltpu.VMEM((NS, width), f32),
            pltpu.VMEM((padded // 2, 128), f32),
            pltpu.VMEM((padded // 2, 128), f32),
        ],
        compiler_params=pltpu.CompilerParams(vmem_limit_bytes=40 << 20),
        cost_estimate=pl.CostEstimate(
            flops=tokens * width * NS * 18, bytes_accessed=tokens * width * NS * 4, transcendentals=tokens * width * NS
        ),
        name="scan_backward",
    )(step_keep, push, d_pre, b_t, c_t, states, states, rate)


def places():
    me = lax.axis_index("seq")
    core, x, y = me % 2, (me // 2) % 2, me // 4
    sibling = me + 1 - 2 * core
    return me, core, sibling, 2 - 4 * x, 4 - 8 * y


def remote(src, dst, sems, k, to, axis="seq"):
    return pltpu.make_async_remote_copy(
        src_ref=src,
        dst_ref=dst,
        send_sem=sems.at[0, k],
        recv_sem=sems.at[1, k],
        device_id={axis: to},
        device_id_type=MESH,
    )


def greet(devices, axis="seq"):
    barrier = pltpu.get_barrier_semaphore()
    for d in devices:
        pl.semaphore_signal(barrier, inc=1, device_id={axis: d}, device_id_type=MESH)
    pl.semaphore_wait(barrier, len(devices))


def block_at(ref, d):
    if len(ref.shape) == 3:
        return ref.at[d]
    width = ref.shape[1] // 8
    return ref.at[:, pl.ds(pl.multiple_of(d * width, width), width)]


def halves(ref, tile):
    rows = ref.shape[0]
    top = (rows // 2 + tile - 1) // tile * tile
    return ref.at[pl.ds(0, top)], ref.at[pl.ds(top, rows - top)]


def gather_steps(out, sems, base, tile):
    me, core, sib, step_x, step_y = places()
    at_x, at_y = me + step_x, me + step_y
    diag = me + step_x + step_y

    def send(block, k, to):
        copy = remote(block, block, sems, base + k, to)
        copy.start()
        return copy

    mine, from_x, from_y, far = (block_at(out, d) for d in (me, at_x, at_y, diag))
    own_x, own_y, own_s = send(mine, 0, at_x), send(mine, 1, at_y), send(mine, 2, sib)
    own_x.wait_recv()
    on_y = send(halves(from_x, tile)[0], 3, at_y)
    pass_x = send(from_x, 5, sib)
    own_y.wait_recv()
    on_x = send(halves(from_y, tile)[1], 4, at_x)
    pass_y = send(from_y, 6, sib)
    on_y.wait_recv()
    pass_top = send(halves(far, tile)[0], 7, sib)
    on_x.wait_recv()
    pass_low = send(halves(far, tile)[1], 8, sib)
    for copy in (own_s, pass_x, pass_y, pass_top, pass_low):
        copy.wait()
    for copy in (own_x, own_y, on_x, on_y):
        copy.wait_send()


def gather_body(x_ref, out_ref, sems, local_sem):
    me, core, sib, step_x, step_y = places()
    mine = pltpu.make_async_copy(x_ref, out_ref.at[me], local_sem)
    mine.start()
    greet([sib, me + step_x, me + step_y])
    mine.wait()
    gather_steps(out_ref, sems, 0, 16)


def add_rows(out, parts, rows):
    def step(i, _):
        at = pl.ds(pl.multiple_of(i * rows, rows), rows)
        total = parts[0][at, :].astype(f32)
        for p in parts[1:]:
            total = total + p[at, :].astype(f32)
        out[at, :] = total.astype(out.dtype)
        return 0

    lax.fori_loop(0, out.shape[0] // rows, step, 0)


def scatter_steps(p_ref, out, from_sib, acc, got_x, got_y, last_x, last_y, sems, tile):
    me, core, sib, step_x, step_y = places()
    dests = (me + step_x + step_y, me + step_x, me + step_y, me)

    def send(src, dst, k, to):
        copy = remote(src, dst, sems, k, to)
        copy.start()
        return copy

    pairs = [send(block_at(p_ref, d + 1 - 2 * core), from_sib.at[k], k, sib) for k, d in enumerate(dests)]
    out_x, out_y = [], []
    for k, d in enumerate(dests):
        pairs[k].wait_recv()
        add_rows(acc.at[k], [block_at(p_ref, d), from_sib.at[k]], tile)
        top, low = halves(acc.at[k], tile)
        if k == 0:
            out_x.append(send(top, got_x.at[0], 4, me + step_x))
            out_y.append(send(low, got_y.at[0], 5, me + step_y))
        if k == 1:
            out_x.append(send(top, got_x.at[1], 6, me + step_x))
        if k == 2:
            out_y.append(send(low, got_y.at[1], 7, me + step_y))
    out_x[0].wait_recv()
    add_rows(got_x.at[0], [got_x.at[0], halves(acc.at[2], tile)[0]], tile)
    last_a = send(got_x.at[0], last_y, 8, me + step_y)
    out_y[0].wait_recv()
    add_rows(got_y.at[0], [got_y.at[0], halves(acc.at[1], tile)[1]], tile)
    last_b = send(got_y.at[0], last_x, 9, me + step_x)
    out_x[1].wait_recv()
    out_y[1].wait_recv()
    top, low = halves(acc.at[3], tile)
    out_top, out_low = halves(out, tile)
    last_a.wait_recv()
    add_rows(out_top, [got_x.at[1], top, last_y], tile)
    last_b.wait_recv()
    add_rows(out_low, [got_y.at[1], low, last_x], tile)
    for copy in pairs + out_x + out_y + [last_a, last_b]:
        copy.wait_send()


def scatter_body(p_ref, out_ref, from_sib, acc, got_x, got_y, last_x, last_y, sems):
    me, core, sib, step_x, step_y = places()
    greet([sib, me + step_x, me + step_y])
    scatter_steps(p_ref, out_ref, from_sib, acc, got_x, got_y, last_x, last_y, sems, 16)


def sum_body(p_ref, out_ref, from_sib, acc, got_x, got_y, last_x, last_y, sems):
    me, core, sib, step_x, step_y = places()
    greet([sib, me + step_x, me + step_y])
    scatter_steps(p_ref, block_at(out_ref, me), from_sib, acc, got_x, got_y, last_x, last_y, sems, 8)
    gather_steps(out_ref, sems, 10, 8)


def scatter_scratch(rows, width, dtype, tile):
    top = (rows // 2 + tile - 1) // tile * tile
    low = rows - top
    return [
        pltpu.VMEM((4, rows, width), dtype),
        pltpu.VMEM((4, rows, width), dtype),
        pltpu.VMEM((2, top, width), dtype),
        pltpu.VMEM((2, low, width), dtype),
        pltpu.VMEM((low, width), dtype),
        pltpu.VMEM((top, width), dtype),
    ]


def direct_body(axis, size, modes, *refs):
    count = len(modes)
    ins, outs, (sems, local_sems) = refs[:count], refs[count : 2 * count], refs[2 * count :]
    me = lax.axis_index(axis)
    own = []
    for a, (x, out, mode) in enumerate(zip(ins, outs, modes)):
        copy = pltpu.make_async_copy(x.at[me] if mode == "exchange" else x, out.at[me], local_sems.at[a])
        copy.start()
        own.append(copy)
    others = [(me + k) % size for k in range(1, size)]
    greet(others, axis)
    copies = []
    for a, (x, out, mode) in enumerate(zip(ins, outs, modes)):
        for k, to in enumerate(others):
            src = x.at[to] if mode == "exchange" else x
            copy = remote(src, out.at[me], sems, a * (size - 1) + k, to, axis)
            copy.start()
            copies.append(copy)
    for copy in own + copies:
        copy.wait()


any_space = pl.BlockSpec(memory_space=pl.ANY)
vmem_space = pl.BlockSpec(memory_space=pltpu.VMEM)


def comm_params(collective_id):
    return pltpu.CompilerParams(
        collective_id=collective_id, has_side_effects=True, vmem_limit_bytes=40 << 20
    )


def direct(axis, size, arrays, modes, collective_id):
    shapes = [x.shape if mode == "exchange" else (size,) + x.shape for x, mode in zip(arrays, modes)]
    return pl.pallas_call(
        functools.partial(direct_body, axis, size, modes),
        out_shape=[jax.ShapeDtypeStruct(s, x.dtype) for s, x in zip(shapes, arrays)],
        in_specs=[any_space] * len(arrays),
        out_specs=[any_space] * len(arrays),
        scratch_shapes=[
            pltpu.SemaphoreType.DMA((2, len(arrays) * (size - 1))),
            pltpu.SemaphoreType.DMA((len(arrays),)),
        ],
        compiler_params=comm_params(collective_id),
        name="direct_" + axis,
    )(*arrays)


def seq_gather(n, block, collective_id):
    if n != 8:
        return lax.all_gather(block, "seq", axis=0, tiled=False)
    return pl.pallas_call(
        gather_body,
        out_shape=jax.ShapeDtypeStruct((8,) + block.shape, block.dtype),
        in_specs=[any_space],
        out_specs=any_space,
        scratch_shapes=[pltpu.SemaphoreType.DMA((2, 9)), pltpu.SemaphoreType.DMA],
        compiler_params=comm_params(collective_id),
        name="seq_gather",
    )(block)


def seq_scatter(n, parts, collective_id):
    if n != 8:
        return lax.psum_scatter(parts, "seq", scatter_dimension=0, tiled=False).astype(f32)
    _, rows, width = parts.shape
    return pl.pallas_call(
        scatter_body,
        out_shape=jax.ShapeDtypeStruct((rows, width), f32),
        in_specs=[vmem_space],
        out_specs=vmem_space,
        scratch_shapes=scatter_scratch(rows, width, parts.dtype, 16) + [pltpu.SemaphoreType.DMA((2, 10))],
        compiler_params=comm_params(collective_id),
        name="seq_scatter",
    )(parts)


def seq_sum(n, parts, collective_id):
    if n != 8:
        return lax.psum(parts, "seq")
    rows, length = parts.shape
    return pl.pallas_call(
        sum_body,
        out_shape=jax.ShapeDtypeStruct(parts.shape, f32),
        in_specs=[vmem_space],
        out_specs=vmem_space,
        scratch_shapes=scatter_scratch(rows, length // 8, f32, 8) + [pltpu.SemaphoreType.DMA((2, 19))],
        compiler_params=comm_params(collective_id),
        name="seq_sum",
    )(parts)


def seq_token_sum(n, value, collective_id):
    if n != 8:
        return lax.psum(value, "seq")
    (got,) = direct("seq", n, [value.reshape(-1, 128)], ("gather",), collective_id)
    return jnp.sum(got, 0).reshape(-1)


def exchange(n, blocks, collective_id):
    if n != 8:
        return lax.all_to_all(blocks, "seq", 0, 0, tiled=False)
    return direct("seq", n, [blocks], ("exchange",), collective_id)[0]


def deal(total, parts, n):
    unit = 5 * n
    nat = jnp.arange(total, dtype=jnp.int32)
    start = jnp.zeros_like(nat)
    at = 0
    for w in parts[:-1]:
        at += w
        start = jnp.where(nat >= at, at, start)
    inside = nat - start
    owner = (inside % unit) // 5
    col = owner * (total // n) + start // n + (inside // unit) * 5 + inside % 5
    return (col[:, None] == nat[None, :]).astype(bf16)


def exact(left, right, contract, precision=None):
    return lax.dot_general(left, right, (contract, ((), ())), precision=precision, preferred_element_type=f32)


def attn_fwd_body(qt_ref, kt_ref, vt_ref, bias_ref, out_ref, lse_ref):
    keys = kt_ref[...].T
    for head in range(qt_ref.shape[0] // HEAD_SIZE):
        rows = slice(head * HEAD_SIZE, (head + 1) * HEAD_SIZE)
        scores = matmul(keys, qt_ref[rows, :]) + bias_ref[...]
        row_max = jnp.max(scores, 0, keepdims=True)
        exp_scores = jnp.exp(scores - row_max)
        row_total = jnp.sum(exp_scores, 0, keepdims=True)
        probs = (exp_scores * (1.0 / row_total)).astype(bf16)
        out_ref[rows, :] = matmul(vt_ref[...], probs)
        lse_ref[0, head : head + 1, :] = row_max + jnp.log(row_total)


def attn_bwd_body(qt_ref, kt_ref, vt_ref, dot_ref, lse_ref, bias_ref, dqt_ref, dkt_ref, dvt_ref):
    keys, values = kt_ref[...].T, vt_ref[...].T
    dk = jnp.zeros(keys.shape, f32)
    dv = jnp.zeros(values.shape, f32)
    for head in range(qt_ref.shape[0] // HEAD_SIZE):
        rows = slice(head * HEAD_SIZE, (head + 1) * HEAD_SIZE)
        q_t, do_t = qt_ref[rows, :], dot_ref[rows, :]
        scores = matmul(keys, q_t) + bias_ref[...]
        probs = jnp.exp(scores - lse_ref[0, head : head + 1, :])
        d_probs = matmul(values, do_t)
        inner = jnp.sum(probs * d_probs, 0, keepdims=True)
        d_scores = (probs * (d_probs - inner)).astype(bf16)
        dqt_ref[rows, :] = (matmul(kt_ref[...], d_scores) * (HEAD_SIZE**-0.5)).astype(bf16)
        dk = dk + matmul(d_scores, q_t.T)
        dv = dv + matmul(probs.astype(bf16), do_t.T)
    dkt_ref[...] = dk.T.astype(bf16)
    dvt_ref[...] = dv.T.astype(bf16)


def attn_specs(tokens, span, groups):
    heads = pl.BlockSpec((groups * HEAD_SIZE, tokens), lambda h: (h, 0))
    key = pl.BlockSpec((HEAD_SIZE, span), lambda h: (h, 0))
    value = pl.BlockSpec((HEAD_SIZE, span), lambda h: (KEY_VALUE_HEADS + h, 0))
    lse = pl.BlockSpec((1, 8, tokens), lambda h: (h, 0, 0))
    bias = pl.BlockSpec((span, tokens), lambda h: (0, 0))
    return heads, key, value, lse, bias


def attention_forward(q_t, kv_t, bias):
    span, tokens = bias.shape
    heads, key, value, lse, bias_spec = attn_specs(tokens, span, QUERY_HEADS // KEY_VALUE_HEADS)
    return pl.pallas_call(
        attn_fwd_body,
        grid=(KEY_VALUE_HEADS,),
        in_specs=[heads, key, value, bias_spec],
        out_specs=[heads, lse],
        out_shape=[
            jax.ShapeDtypeStruct(q_t.shape, f32),
            jax.ShapeDtypeStruct((KEY_VALUE_HEADS, 8, tokens), f32),
        ],
        compiler_params=pltpu.CompilerParams(vmem_limit_bytes=40 << 20),
        cost_estimate=pl.CostEstimate(
            flops=QUERY_HEADS * span * tokens * 512, bytes_accessed=8 << 20, transcendentals=QUERY_HEADS * span * tokens
        ),
        name="attention_forward",
    )(q_t, kv_t, kv_t, bias)


def attention_backward(q_t, kv_t, do_t, lse, bias):
    span, tokens = bias.shape
    heads, key, value, lse_spec, bias_spec = attn_specs(tokens, span, QUERY_HEADS // KEY_VALUE_HEADS)
    return pl.pallas_call(
        attn_bwd_body,
        grid=(KEY_VALUE_HEADS,),
        in_specs=[heads, key, value, heads, lse_spec, bias_spec],
        out_specs=[heads, key, key],
        out_shape=[
            jax.ShapeDtypeStruct(q_t.shape, bf16),
            jax.ShapeDtypeStruct((KEY_VALUE_HEADS * HEAD_SIZE, span), bf16),
            jax.ShapeDtypeStruct((KEY_VALUE_HEADS * HEAD_SIZE, span), bf16),
        ],
        compiler_params=pltpu.CompilerParams(vmem_limit_bytes=40 << 20),
        cost_estimate=pl.CostEstimate(
            flops=QUERY_HEADS * span * tokens * 1280, bytes_accessed=16 << 20, transcendentals=QUERY_HEADS * span * tokens
        ),
        name="attention_backward",
    )(q_t, kv_t, kv_t, do_t, lse, bias)


def layer(
    n,
    m,
    tokens,
    doc_ids,
    in_weight,
    out_weight,
    gate_up,
    down_weight,
    select_weight,
    step_weight,
    first_gain,
    second_gain,
    attn_gain,
    mamba_gain,
    conv_weight,
    conv_bias,
    step_bias,
    decay_log,
    skip_gain,
    cotangent,
):
    fast = n == 8
    me = lax.axis_index("seq")
    query_w = QUERY_HEADS * HEAD_SIZE
    key_w = KEY_VALUE_HEADS * HEAD_SIZE
    q_own, k_own, c_own, f_own = query_w // n, key_w // n, DI // n, F // n
    p_own = q_own + 2 * k_own + 2 * c_own
    kinds = (query_w, key_w, key_w, DI, DI)
    local, width = tokens.shape[1:]
    length = local * n
    z_rows = in_weight.shape[0]
    sel_rows = select_weight.shape[0]
    wide = p_own * n
    starts = (0, query_w, query_w + key_w, query_w + 2 * key_w, query_w + 2 * key_w + DI)
    widths = (q_own, k_own, k_own, c_own, c_own)
    highest = lax.Precision.HIGHEST

    small_w = jnp.concatenate([select_weight, step_weight], 0)
    if fast:
        deal_in, deal_small, deal_out = deal(p_own, (p_own,), n), deal(c_own, (c_own,), n), deal(out_weight.shape[0], (out_weight.shape[0],), n)
        in_blocks = exact(deal_in, in_weight, ((0,), (1,))).astype(bf16).reshape(n, p_own // n, z_rows)
        small_blocks = exact(deal_small, small_w, ((0,), (1,))).astype(bf16).reshape(n, c_own // n, -1)
        in_blocks, small_blocks, ids = direct(
            "seq", n, [in_blocks, small_blocks, doc_ids.reshape(-1, 128)], ("exchange", "exchange", "gather"), 0
        )
        ids = ids.reshape(-1)
        in_cols = in_blocks.reshape(p_own, z_rows).T
        small_cols = small_blocks.reshape(c_own, -1).T
        gu_blocks = gate_up.T.reshape(n, -1, z_rows)
        out_blocks = exact(deal_out, out_weight, ((0,), (0,))).astype(bf16).reshape(n, -1, out_weight.shape[1])
        down_blocks = down_weight.reshape(n, -1, down_weight.shape[1])
        gu_blocks, out_blocks, down_blocks = direct(
            "seq", n, [gu_blocks, out_blocks, down_blocks], ("exchange",) * 3, 1
        )
        gu_cols = gu_blocks.reshape(-1, z_rows).T
        out_rows = out_blocks.transpose(1, 0, 2).reshape(-1, width)
        down_rows = down_blocks.transpose(1, 0, 2).reshape(-1, width)
        (small_full,) = direct("fsdp", m, [small_cols], ("gather",), 2)
        out_full = lax.all_gather(out_rows, "fsdp", axis=0, tiled=True)
        down_full = lax.all_gather(down_rows, "fsdp", axis=0, tiled=True)
    else:
        ids = lax.all_gather(doc_ids[0], "seq", axis=0, tiled=True)
        in_cols = lax.all_gather(in_weight, "seq", axis=1, tiled=True)
        in_cols = jnp.concatenate(
            [lax.dynamic_slice_in_dim(in_cols, s + me * w, w, 1) for s, w in zip(starts, widths)], 1
        )
        small_full = lax.all_gather(small_w, "fsdp", axis=0, tiled=False)
        half = n // 2
        route_a = [(d, 2 * d if d < half else 2 * (d - half) + 1) for d in range(n)]
        route_b = [(d, 2 * d + 1 if d < half else 2 * (d - half)) for d in range(n)]
        low_half = me < half
        even = me % 2 == 0
        piece0, piece1 = gate_up[:, :f_own], gate_up[:, f_own:]
        got_a = lax.ppermute(jnp.where(low_half, piece0, piece1), "seq", route_a)
        got_b = lax.ppermute(jnp.where(low_half, piece1, piece0), "seq", route_b)
        gu_cols = jnp.concatenate([jnp.where(even, got_a, got_b), jnp.where(even, got_b, got_a)], 1)
        out_rows = lax.all_gather(out_weight, "fsdp", axis=0, tiled=True)
        out_rows = jnp.concatenate(
            [out_rows[:query_w].reshape(n, q_own, -1), out_rows[query_w:].reshape(n, c_own, -1)], 1
        )
        out_full = exchange(n, out_rows, None).transpose(1, 0, 2).reshape(q_own + c_own, -1)
        down_rows = lax.all_gather(down_weight, "fsdp", axis=0, tiled=True).reshape(n, f_own, -1)
        down_full = exchange(n, down_rows, None).transpose(1, 0, 2).reshape(f_own, -1)
    in_full = lax.all_gather(in_cols, "fsdp", axis=0, tiled=True)
    gu_full = lax.all_gather(gu_cols, "fsdp", axis=0, tiled=True)
    select_own = small_full[:, :sel_rows].reshape(-1, c_own)
    step_own = small_full[:, sel_rows:].reshape(-1, c_own)

    params = jnp.concatenate(
        [mamba_gain[None], conv_weight, conv_bias[None], step_bias[None], decay_log, skip_gain[None]], 0
    )
    if fast:
        params = params.reshape(-1, c_own)
        params = exact(params, deal(c_own, (c_own,), n), ((1,), (0,)), highest).reshape(-1, n, n, c_own // n)
        params = lax.dynamic_index_in_dim(params, me, 2, False).reshape(-1, c_own)
    else:
        params = lax.dynamic_slice_in_dim(params, me * c_own, c_own, 1)
    mamba_g, conv_w, conv_b, step_b = params[0], params[1 : 1 + KC], params[1 + KC], params[2 + KC]
    decay_l, skip_g = params[3 + KC : 3 + KC + NS], params[3 + KC + NS]

    def heads_in(blocks):
        blocks = blocks.reshape(query_w, local)
        return exact(deal(query_w, (query_w,), n), blocks, ((1,), (0,))).astype(bf16) if fast else blocks

    def heads_out(value):
        if fast:
            value = exact(deal(query_w, (query_w,), n), value, ((0,), (0,))).astype(bf16)
        return value.reshape(n, q_own, local)

    seq_x = tokens[0].astype(f32)
    normed_one, scale_one = rms_norm(seq_x, first_gain)
    normed_one = seq_gather(n, normed_one.astype(bf16), 3).reshape(length, width)
    qkv_w = q_own + 2 * k_own
    qkv_t = exact(in_full[:, :qkv_w], normed_one, ((0,), (1,))).astype(bf16)
    branch = matmul(normed_one, in_full[:, qkv_w:]).astype(bf16)
    inputs = branch[:, :c_own].astype(f32)
    gate_z = branch[:, c_own:].astype(f32)

    q_blocks = qkv_t[:q_own].reshape(q_own, n, local).transpose(1, 0, 2)
    q_t = heads_in(exchange(n, q_blocks, 4)) * bf16(HEAD_SIZE**-0.5)
    kv_all = seq_gather(n, qkv_t[q_own:], 5)
    reach = (WINDOW_TOKENS + local - 2) // local
    span = min((reach + 1) * local, length)
    first_key = jnp.clip((me - reach) * local, 0, length - span)
    kv_win = lax.dynamic_slice_in_dim(kv_all, first_key, span, 2)
    if fast:
        deal_kv = deal(2 * key_w, (key_w, key_w), n)
        kv_t = exact(deal_kv, kv_win.reshape(2 * key_w, span), ((1,), (0,))).astype(bf16)
    else:
        kv_t = jnp.concatenate(
            [kv_win[:, :k_own].reshape(key_w, span), kv_win[:, k_own:].reshape(key_w, span)], 0
        )
    query_pos = me * local + jnp.arange(local, dtype=jnp.int32)
    key_pos = first_key + jnp.arange(span, dtype=jnp.int32)
    offset = query_pos[None, :] - key_pos[:, None]
    key_ids = lax.dynamic_slice_in_dim(ids, first_key, span, 0)
    allowed = (offset >= 0) & (offset < WINDOW_TOKENS) & (doc_ids[0][None, :] == key_ids[:, None])
    bias = jnp.where(allowed, 0.0, masked_score).astype(f32)
    attended, lse = attention_forward(q_t, kv_t, bias)
    attn_scale = lax.rsqrt(jnp.mean(attended * attended, axis=0, keepdims=True) + norm_eps)
    attn_normed = (attended * attn_scale * attn_gain[:, None]).astype(bf16)
    attn_c = exchange(n, heads_out(attn_normed), 6).transpose(0, 2, 1).reshape(length, q_own)

    padded_inputs = jnp.pad(inputs, ((KC - 1, 0), (0, 0)))
    padded_ids = jnp.pad(ids, (KC - 1, 0), constant_values=-1)
    conv_sum = conv_b + jnp.zeros_like(inputs)
    same_masks = []
    for tap in range(KC):
        begin = KC - 1 - tap
        same = (padded_ids[begin : begin + length] == ids).astype(f32)[:, None]
        same_masks.append(same)
        conv_sum = conv_sum + conv_w[tap] * padded_inputs[begin : begin + length] * same
    activated_b = jax.nn.silu(conv_sum).astype(bf16)
    activated = activated_b.astype(f32)
    sel_pad = jnp.pad(select_own, ((0, (-select_own.shape[0]) % 8), (0, 0)))
    selected = seq_sum(n, dot_nt(sel_pad, activated_b), 7)
    step_raw = selected[:DTR].astype(bf16)
    b_t = selected[DTR : DTR + NS]
    c_t = selected[DTR + NS : DTR + 2 * NS]
    step_pre = dot_tn(step_raw, step_own) + step_b
    step_size = jax.nn.softplus(step_pre)
    rate = -jnp.exp(decay_l)
    changed = jnp.concatenate([jnp.zeros((1,), f32), (ids[1:] != ids[:-1]).astype(f32)])
    step_keep = step_size + 1e30 * changed[:, None]
    push = step_size * activated
    scan_out, states = scan_forward(step_keep, push, b_t, c_t, rate)
    mamba_pre = scan_out + skip_g * activated
    gate_sig = jax.nn.sigmoid(gate_z)
    mamba_out = mamba_pre * gate_z * gate_sig
    square_sum = seq_token_sum(n, jnp.sum(mamba_out * mamba_out, -1), 8)
    mamba_scale = lax.rsqrt(square_sum / DI + norm_eps)[:, None]
    mamba_normed = mamba_out * mamba_scale * mamba_g
    joined = jnp.concatenate([attn_c, mamba_normed.astype(bf16)], 1)
    mixed = seq_scatter(n, matmul(joined, out_full).astype(bf16).reshape(n, local, width), 9)
    hidden = seq_x + 0.5 * mixed
    normed_two, scale_two = rms_norm(hidden, second_gain)
    normed_two = seq_gather(n, normed_two.astype(bf16), 10).reshape(length, width)
    gate_up_out = matmul(normed_two, gu_full).astype(bf16)
    gate_part = gate_up_out[:, :f_own].astype(f32)
    up_part = gate_up_out[:, f_own:].astype(f32)
    gate_act = jax.nn.sigmoid(gate_part)
    inner = (gate_part * gate_act * up_part).astype(bf16)
    ffn = seq_scatter(n, matmul(inner, down_full).astype(bf16).reshape(n, local, width), 11)
    out_tokens = (hidden + ffn).astype(bf16)

    d_ffn = seq_gather(n, cotangent[0], 12).reshape(length, width)
    down_term = dot_tn(inner, d_ffn).astype(bf16)
    d_inner = dot_nt(d_ffn, down_full)
    d_gate_up = jnp.concatenate(
        [
            d_inner * up_part * gate_act * (1.0 + gate_part * (1.0 - gate_act)),
            d_inner * gate_part * gate_act,
        ],
        1,
    ).astype(bf16)
    gate_up_term = dot_tn(normed_two, d_gate_up).astype(bf16)
    d_normed_two = seq_scatter(n, dot_nt(d_gate_up, gu_full).astype(bf16).reshape(n, local, width), 13)
    d_hidden_part, second_grad = norm_back(hidden, scale_two, second_gain, d_normed_two)
    d_hidden = cotangent[0].astype(f32) + d_hidden_part
    d_mixed = seq_gather(n, d_hidden.astype(bf16), 14).reshape(length, width)
    out_term = (0.5 * dot_tn(joined, d_mixed)).astype(bf16)
    d_joined = 0.5 * dot_nt(d_mixed, out_full)

    d_attn = d_joined[:, :q_own].astype(bf16).reshape(n, local, q_own).transpose(0, 2, 1)
    d_attn = heads_in(exchange(n, d_attn, 15)).astype(f32)
    weighted_a = d_attn * attn_gain[:, None]
    attn_grad = jnp.sum(d_attn * attended * attn_scale, 1)
    mean_a = jnp.mean(weighted_a * attended, axis=0, keepdims=True)
    d_attended = attn_scale * weighted_a - attended * (attn_scale * attn_scale * attn_scale) * mean_a
    dq_t, dk_t, dv_t = attention_backward(q_t, kv_t, d_attended.astype(bf16), lse, bias)
    d_queries = exchange(n, heads_out(dq_t), 16).transpose(0, 2, 1).reshape(length, q_own)
    if fast:
        dkv = exact(deal_kv, jnp.concatenate([dk_t, dv_t], 0), ((0,), (0,))).astype(bf16).reshape(n, 2 * k_own, span)
    else:
        dkv = jnp.concatenate([dk_t.reshape(n, k_own, span), dv_t.reshape(n, k_own, span)], 1)
    dkv = lax.dynamic_update_slice_in_dim(jnp.zeros((n, 2 * k_own, length), bf16), dkv, first_key, 2)
    dkv = seq_scatter(n, dkv, 17).astype(bf16).T

    u = d_joined[:, q_own:]
    weighted = u * mamba_g
    inner_mean = seq_token_sum(n, jnp.sum(weighted * mamba_out, -1), 18)[:, None] / DI
    mamba_grad = jnp.sum(u * mamba_out * mamba_scale, 0)
    d_mamba = mamba_scale * weighted - mamba_out * (mamba_scale * mamba_scale * mamba_scale) * inner_mean
    d_pre = d_mamba * gate_z * gate_sig
    d_gate = d_mamba * mamba_pre * gate_sig * (1.0 + gate_z * (1.0 - gate_sig))
    skip_grad = jnp.sum(d_pre * activated, 0)
    by_rate, pushed, db_t, dc_t, decay_log_grad = scan_backward(
        step_keep, push, d_pre, b_t, c_t, states, rate
    )
    step_grads = by_rate + pushed * activated
    d_step_pre = step_grads * jax.nn.sigmoid(step_pre)
    step_bias_grad = jnp.sum(d_step_pre, 0)
    d_step_low = d_step_pre.astype(bf16)
    step_term = matmul(step_raw, d_step_low)
    d_selected = jnp.concatenate(
        [dot_nt(step_own, d_step_low), db_t, dc_t, jnp.zeros(((-DTR - 2 * NS) % 8, length), f32)], 0
    )
    d_selected = seq_sum(n, d_selected, 19)[: DTR + 2 * NS].astype(bf16)
    select_term = matmul(d_selected, activated_b)
    d_activated = d_pre * skip_g + pushed * step_size + dot_tn(d_selected, select_own)
    conv_sig = jax.nn.sigmoid(conv_sum)
    d_conv = d_activated * conv_sig * (1.0 + conv_sum * (1.0 - conv_sig))
    conv_bias_grad = jnp.sum(d_conv, 0)
    ext_grad = jnp.zeros((length + KC - 1, c_own), f32)
    conv_rows = []
    for tap in range(KC):
        begin = KC - 1 - tap
        masked_grad = d_conv * same_masks[tap]
        conv_rows.append(jnp.sum(masked_grad * padded_inputs[begin : begin + length], 0))
        ext_grad = ext_grad + jnp.pad(conv_w[tap] * masked_grad, ((begin, tap), (0, 0)))
    d_inputs = ext_grad[KC - 1 :]
    d_projected = jnp.concatenate([d_queries, dkv, d_inputs.astype(bf16), d_gate.astype(bf16)], 1)
    in_term = dot_tn(normed_one, d_projected).astype(bf16)
    d_normed_one = seq_scatter(n, dot_nt(d_projected, in_full).astype(bf16).reshape(n, local, width), 20)
    d_x_part, first_grad = norm_back(seq_x, scale_one, first_gain, d_normed_one)
    tokens_grad = (d_hidden + d_x_part).astype(bf16)

    gu_part = lax.psum_scatter(gate_up_term, "fsdp", scatter_dimension=0, tiled=True)
    in_part = lax.psum_scatter(in_term, "fsdp", scatter_dimension=0, tiled=True)
    small_term = jnp.concatenate(
        [select_term.reshape(m, sel_rows, c_own), step_term.reshape(m, -1, c_own)], 1
    ).astype(bf16)
    channel = jnp.concatenate(
        [
            mamba_grad[None], jnp.stack(conv_rows), conv_bias_grad[None], step_bias_grad[None],
            decay_log_grad, skip_grad[None],
        ],
        0,
    )
    wide_grads = jnp.stack([first_grad, second_grad, attn_grad])
    small_z, channel_z, wide_z = direct(
        "fsdp", m, [small_term, channel, wide_grads], ("exchange", "gather", "gather"), 21
    )
    small_part = jnp.sum(small_z.astype(f32), 0)
    channel, wide_grads = jnp.sum(channel_z, 0), jnp.sum(wide_z, 0)
    if fast:
        out_part = lax.psum_scatter(out_term.reshape(m, -1, width), "fsdp", scatter_dimension=0, tiled=False)
        down_part = lax.psum_scatter(down_term.reshape(m, -1, width), "fsdp", scatter_dimension=0, tiled=False)
        out_blocks = out_part.reshape(-1, n, width // n).transpose(1, 0, 2)
        down_blocks = down_part.reshape(-1, n, width // n).transpose(1, 0, 2)
        gu_blocks = gu_part.T.reshape(n, -1, z_rows)
        gu_blocks, out_blocks, down_blocks = direct(
            "seq", n, [gu_blocks, out_blocks, down_blocks], ("exchange",) * 3, 22
        )
        gu_sum = gu_blocks.reshape(-1, z_rows).T.astype(f32)
        out_sum = exact(deal_out, out_blocks.reshape(-1, width // n), ((1,), (0,)))
        down_sum = down_blocks.reshape(-1, width // n).astype(f32)
        small_blocks = small_part.astype(bf16).T.reshape(n, c_own // n, -1)
        small_blocks, channel_all, wide_all = direct(
            "seq", n, [small_blocks, channel, wide_grads], ("exchange", "gather", "gather"), 23
        )
        small_sum = exact(small_blocks.reshape(c_own, -1), deal_small, ((0,), (1,)))
        channel_rows = channel.shape[0]
        channel = channel_all.reshape(n, channel_rows, n, c_own // n).transpose(1, 2, 0, 3).reshape(-1, c_own)
        channel = exact(channel, deal_small, ((1,), (1,)), highest).reshape(channel_rows, DI)
        wide_grads = jnp.sum(wide_all, 0)
        (in_blocks,) = direct("seq", n, [in_part.T.reshape(n, -1, z_rows)], ("exchange",), 24)
        in_sum = exact(in_blocks.reshape(p_own, z_rows), deal_in, ((0,), (1,)))
    else:
        out_blocks = exchange(n, out_term.reshape(q_own + c_own, n, -1).transpose(1, 0, 2), None)
        out_sum = jnp.concatenate(
            [out_blocks[:, :q_own].reshape(query_w, -1), out_blocks[:, q_own:].reshape(DI, -1)], 0
        )
        out_sum = lax.psum_scatter(out_sum, "fsdp", scatter_dimension=0, tiled=True).astype(f32)
        down_sum = exchange(n, down_term.reshape(f_own, n, -1).transpose(1, 0, 2), None).reshape(F, -1)
        down_sum = lax.psum_scatter(down_sum, "fsdp", scatter_dimension=0, tiled=True).astype(f32)
        gate_g, up_g = gu_part[:, :f_own], gu_part[:, f_own:]
        back_a = lax.ppermute(jnp.where(even, gate_g, up_g), "seq", [(t, s) for s, t in route_a])
        back_b = lax.ppermute(jnp.where(even, up_g, gate_g), "seq", [(t, s) for s, t in route_b])
        gu_sum = jnp.concatenate(
            [jnp.where(low_half, back_a, back_b), jnp.where(low_half, back_b, back_a)], 1
        ).astype(f32)
        in_sum = jnp.zeros((z_rows, wide), bf16)
        at = 0
        for s, w in zip(starts, widths):
            in_sum = lax.dynamic_update_slice_in_dim(in_sum, in_part[:, at : at + w], s + me * w, 1)
            at += w
        in_sum = lax.psum_scatter(in_sum, "seq", scatter_dimension=1, tiled=True).astype(f32)
        small_sum = small_part
        channel = lax.all_gather(channel, "seq", axis=1, tiled=True)
        wide_grads = lax.psum(wide_grads, "seq")
    return (
        out_tokens[None],
        tokens_grad[None],
        in_sum,
        out_sum,
        gu_sum,
        down_sum,
        small_sum[:sel_rows],
        small_sum[sel_rows:],
        wide_grads[0],
        wide_grads[1],
        wide_grads[2],
        channel[0],
        channel[1 : 1 + KC],
        channel[1 + KC],
        channel[2 + KC],
        channel[3 + KC : 3 + KC + NS],
        channel[3 + KC + NS],
    )


def solution(mesh):
    split = P("fsdp", "seq")
    seq3 = P("fsdp", "seq", None)
    return jax.shard_map(
        functools.partial(layer, mesh.shape["seq"], mesh.shape["fsdp"]),
        mesh=mesh,
        in_specs=(seq3,) + (split,) * 7 + (P(),) * 9 + (seq3,),
        out_specs=(seq3, seq3) + (split,) * 6 + (P(),) * 9,
        check_vma=False,
    )
```

time: 1800 us -> 1310 us (0.73)
  waiting for transfers between devices: 670 us -> 36.5 us
  Pallas kernels: 230 us -> 789 us
  blocking collectives: 291 us -> 0 us
  other arithmetic: 118 us -> 56.9 us
  local copies, waits for them, and re-layouts: 247 us -> 204 us
  starting transfers between devices: 42.7 us -> 0.62 us
  matrix products: 175 us -> 194 us
    pallas_call x2 -> x27, Pallas kernels: 55.3 us -> 613 us  [the longest x13 213 us: direct(): pl.pallas_call(functools.partial(direct_body, axis, size, modes), out_sha...]
    all_gather x8 -> x2, waiting for transfers between devices: 241 us -> 0.02 us  [the longest x1 0.02 us: layer(): out_full = lax.all_gather(out_rows, 'fsdp', axis=0, tiled=True)]
    reduce_scatter x5 -> x1, waiting for transfers between devices: 169 us -> 0.01 us  [layer(): lax.psum_scatter(down_term.reshape(m, -1, width), 'fsdp', scatter_dimensi...]
    psum x5 -> x0, blocking collectives: 160 us -> none  [the longest x1 59.6 us: layer(): d_selected = lax.psum(d_selected, 'seq').astype(bf16)]
    unnamed x26 -> x9, waiting for transfers between devices: 101 us -> 0.14 us
    all_gather x1, waiting for transfers between devices: 69.1 us -> 0.01 us  [layer(): gu_full = lax.all_gather(gu_cols, 'fsdp', axis=0, tiled=True)]
    all_to_all x2 -> x0, blocking collectives: 64.1 us -> none  [the longest x1 34.6 us: layer(): lax.all_to_all(down_term.reshape(f_own, n, -1).transpose(1, 0, 2), 'seq',...]
    all_gather x4 -> x0, blocking collectives: 48.4 us -> none  [the longest x1 15 us: layer(): select_own = lax.all_gather(select_weight, 'fsdp', axis=0, tiled=True)]
  transfers between devices with their start and end apart: 33 -> 8, of which waited for: 17 -> 1; matrix products, arithmetic and copies ran while one was open for 22% -> 22% of each run, Pallas kernels for 11% -> 48%
where the time goes in v2:
time: 1310 us; the launch traced here: 1300 us
  Pallas kernels  789 us (60%)
  local copies, waits for them, and re-layouts  204 us (16%)
  matrix products  194 us (15%)
  other arithmetic  56.9 us (4%)
  waiting for transfers between devices  36.5 us (3%)
  between operations  16.7 us (1%)
    pallas_call x13, Pallas kernels, direct(): pl.pallas_call(functools.partial(direct_body, axis, size, modes), out_sha...  213 us
    pallas_call x5, Pallas kernels, seq_gather(): pl.pallas_call(gather_body, out_shape=jax.ShapeDtypeStruct((8,) + block.s...  156 us
    pallas_call x5, Pallas kernels, seq_scatter(): pl.pallas_call(scatter_body, out_shape=jax.ShapeDtypeStruct((rows, width)...  148 us
    pallas_call x1, Pallas kernels, scan_backward(): pl.pallas_call(scan_bwd_body, grid=(tokens // block,), in_specs=[rows, ro...  118 us
    dot_general x6, matrix products, dot_tn(): lax.dot_general(left, right, (((0,), (0,)), ((), ())), preferred_element_...  71.6 us
    pallas_call x1, Pallas kernels, scan_forward(): pl.pallas_call(scan_fwd_body, grid=(tokens // block,), in_specs=[rows, ro...  57.8 us
    unnamed x277, local copies, waits for them, and re-layouts  51.2 us
    dot_general x6, matrix products, matmul(): return jnp.dot(left, right, preferred_element_type=f32)  43.5 us
  transfers between devices with their start and end apart: 8, of which 1 were waited for; matrix products, arithmetic and copies ran while one was open for 22% of the time, Pallas kernels for 48%

profile of v2, /device:TPU:0, one launch (start us, length us, event | category | flops | bytes accessed | tf_op | source)
XLA Modules:
  0.0 1297.2 jit_solution(2379024512809568185)
XLA Ops:
  22.6 35.2 %direct_seq.15 = (bf16[8,172,400]{2,1,0:T(8,128)(2,1)S(1)}, bf16[8,150,200]{2,1,0:T(8,128)(2,1)S(1)}, bf16[8,172,200]{2,1,0:T(8,128)(2,1)S(1)}) custom-call(bf16[8,172,400]{2,1,0:T(8,128)(2,1)S(1)} %copy.146.refs_0_, bf16[8,150,200]{2,1,0:T(8,128)(2,1)S(1)} %copy-done.23, bf16[8,172,200]{2,1,0:T(8,128)(2,1)S(1)} %copy.147.refs_2_), custom_call_target="tpu_custom_call" | custom-call | tf_op jit(solution)/shard_map/direct_seq/pallas_call | solution.py:413
  71.0 18.4 %direct_seq.11 = (bf16[8,135,400]{2,1,0:T(8,128)(2,1)S(1)}, bf16[8,50,58]{2,1,0:T(8,128)(2,1)S(1)}, s32[8,2,128]{2,1,0:T(2,128)S(1)}) custom-call(bf16[8,135,400]{2,1,0:T(8,128)(2,1)S(1)} %reshape.546.refs_0_, bf16[8,50,58]{2,1,0:T(8,128)(2,1)S(1)} %copy-done.39, s32[2,128]{1,0:T(2,128)S(1)} %bitcast.213), custom_call_target="tpu_custom_call" | custom-call | tf_op jit(solution)/shard_map/direct_seq/pallas_call | solution.py:413
  117.4 34.3 %seq_gather.5 = bf16[8,256,1600]{2,1,0:T(8,128)(2,1)S(1)} custom-call(bf16[256,1600]{1,0:T(8,128)(2,1)S(1)} %fusion.50.x_ref), custom_call_target="tpu_custom_call" | custom-call | tf_op jit(solution)/shard_map/seq_gather/pallas_call | solution.py:430
  154.5 34.4 %seq_gather.8 = bf16[8,256,1600]{2,1,0:T(8,128)(2,1)S(1)} custom-call(bf16[256,1600]{1,0:T(8,128)(2,1)S(1)} %bitcast.181), custom_call_target="tpu_custom_call" | custom-call | tf_op jit(solution)/shard_map/seq_gather/pallas_call | solution.py:430
  200.3 36.3 %all-gather.7.cloned.1.call-done = bf16[1600,1080]{1,0:T(8,128)(2,1)} async-done(((bf16[400,1080]{1,0:T(8,128)(2,1)}), bf16[1600,1080]{1,0:T(8,128)(2,1)}) %all-gather.7.cloned.1.call-update) | async-done | bytes 3456016 | tf_op jit(solution)/shard_map/all_gather | solution.py:668
  255.1 19.5 %seq_gather.6 = bf16[8,80,2048]{2,1,0:T(8,128)(2,1)S(1)} custom-call(bf16[80,2048]{1,0:T(8,128)(2,1)S(1)} %slice.223.x_ref), custom_call_target="tpu_custom_call" | custom-call | tf_op jit(solution)/shard_map/seq_gather/pallas_call | solution.py:430
  279.3 25.5 %attention_forward.1 = (f32[1600,256]{1,0:T(8,128)S(1)}, f32[5,8,256]{2,1,0:T(8,128)S(1)}) custom-call(bf16[1600,256]{1,0:T(8,128)(2,1)S(1)} %fusion.45.qt_ref, bf16[640,1280]{1,0:T(8,128)(2,1)S(1)} %convolution_convert_fusion.10.kt_ref.vt_ref, bf16[640,1280]{1,0:T(8,128)(2,1)S(1)} %convolution_convert_fusion.10.kt_ref.vt_ref, f32[1280,256]{1,0:T(8,128)S(1)} %fusion.63.bias_ref), custom_call_target="tpu_custom_call" | custom-call | flops 4194304000 | bytes 8388608 | tf_op jit(solution)/shard_map/attention_forward/pallas_call | solution.py:546
  344.7 20.2 %seq_sum.2 = f32[136,2048]{1,0:T(8,128)S(1)} custom-call(f32[136,2048]{1,0:T(8,128)S(1)} %fusion.86.p_ref), custom_call_target="tpu_custom_call" | custom-call | tf_op jit(solution)/shard_map/seq_sum/pallas_call | solution.py:460
  369.5 57.8 %scan_forward.1 = (f32[2048,400]{1,0:T(8,128)S(1)}, f32[2048,16,400]{2,1,0:T(8,128)}) custom-call(f32[2048,400]{1,0:T(8,128)S(1)} %get-tuple-element.174.step_ref, f32[2048,400]{1,0:T(8,128)S(1)} %get-tuple-element.173.push_ref, f32[16,2048]{1,0:T(8,128)S(1)} %get-tuple-element.178.b_ref, f32[16,2048]{1,0:T(8,128)S(1)} %get-tuple-element.177.c_ref, ...), custom_call_target="tpu_custom_call" | custom-call | flops 104857600 | bytes 52428800 | tf_op jit(solution)/shard_map/scan_forward/pallas_call | solution.py:169
  461.6 33.5 %seq_scatter.5 = f32[256,1600]{1,0:T(8,128)S(1)} custom-call(bf16[8,256,1600]{2,1,0:T(8,128)(2,1)S(1)} %bitcast.177), custom_call_target="tpu_custom_call" | custom-call | tf_op jit(solution)/shard_map/seq_scatter/pallas_call | solution.py:445
  496.9 33.8 %seq_gather.7 = bf16[8,256,1600]{2,1,0:T(8,128)(2,1)S(1)} custom-call(bf16[256,1600]{1,0:T(8,128)(2,1)S(1)} %multiply_convert_fusion.3.x_ref), custom_call_target="tpu_custom_call" | custom-call | tf_op jit(solution)/shard_map/seq_gather/pallas_call | solution.py:430
  597.0 33.5 %seq_scatter.7 = f32[256,1600]{1,0:T(8,128)S(1)} custom-call(bf16[8,256,1600]{2,1,0:T(8,128)(2,1)S(1)} %bitcast.178), custom_call_target="tpu_custom_call" | custom-call | tf_op jit(solution)/shard_map/seq_scatter/pallas_call | solution.py:445
  644.3 33.0 %seq_scatter.6 = f32[256,1600]{1,0:T(8,128)S(1)} custom-call(bf16[8,256,1600]{2,1,0:T(8,128)(2,1)S(1)} %bitcast.179), custom_call_target="tpu_custom_call" | custom-call | tf_op jit(solution)/shard_map/seq_scatter/pallas_call | solution.py:445
  679.5 33.6 %seq_gather.9 = bf16[8,256,1600]{2,1,0:T(8,128)(2,1)S(1)} custom-call(bf16[256,1600]{1,0:T(8,128)(2,1)S(1)} %get-tuple-element.159.x_ref), custom_call_target="tpu_custom_call" | custom-call | tf_op jit(solution)/shard_map/seq_gather/pallas_call | solution.py:430
  751.5 118.4 %scan_backward.1 = (f32[2048,400]{1,0:T(8,128)S(1)}, f32[2048,400]{1,0:T(8,128)S(1)}, f32[16,2048]{1,0:T(8,128)S(1)}, f32[16,2048]{1,0:T(8,128)S(1)}, f32[16,400]{1,0:T(8,128)S(1)}) custom-call(f32[2048,400]{1,0:T(8,128)S(1)} %copy-done.8, f32[2048,400]{1,0:T(8,128)} %copy-done.6, f32[2048,400]{1,0:T(8,128)} %get-tuple-element.156.dpre_ref, ...), custom_call_target="tpu_custom_call" | custom-call | flops 235929600 | bytes 52428800 | tf_op jit(solution)/shard_map/scan_backward/pallas_call | solution.py:195
  892.5 20.3 %seq_sum.3 = f32[136,2048]{1,0:T(8,128)S(1)} custom-call(f32[136,2048]{1,0:T(8,128)S(1)} %maximum_maximum_fusion.p_ref), custom_call_target="tpu_custom_call" | custom-call | tf_op jit(solution)/shard_map/seq_sum/pallas_call | solution.py:460
  915.7 30.5 %attention_backward.1 = (bf16[1600,256]{1,0:T(8,128)(2,1)S(1)}, bf16[320,1280]{1,0:T(8,128)(2,1)S(1)}, bf16[320,1280]{1,0:T(8,128)(2,1)S(1)}) custom-call(bf16[1600,256]{1,0:T(8,128)(2,1)S(1)} %copy-done.46, bf16[640,1280]{1,0:T(8,128)(2,1)S(1)} %copy-done.44, bf16[640,1280]{1,0:T(8,128)(2,1)S(1)} %copy-done.44, ...), custom_call_target="tpu_custom_call" | custom-call | flops 10485760000 | bytes 16777216 | tf_op jit(solution)/shard_map/attention_backward/pallas_call | solution.py:566
  965.2 22.6 %dynamic_update_slice.3.p_ref = bf16[8,80,2048]{2,1,0:T(8,128)(2,1)S(1)} dynamic-update-slice(bf16[8,80,2048]{2,1,0:T(8,128)(2,1)S(1)} %broadcast_in_dim.32, bf16[8,80,1280]{2,1,0:T(8,128)(2,1)} %bitcast.223, s32[]{:T(128)} %constant.272.clone.1, s32[]{:T(128)} %constant.272.clone.1, s32[]{:T(128)S(6)} %min.4) | dynamic-update-slice | bytes 3276804 | tf_op jit(solution)/shard_map/dynamic_update_slice | solution.py:800
  987.9 16.7 %seq_scatter.8 = f32[80,2048]{1,0:T(8,128)S(1)} custom-call(bf16[8,80,2048]{2,1,0:T(8,128)(2,1)S(1)} %dynamic_update_slice.3.p_ref), custom_call_target="tpu_custom_call" | custom-call | tf_op jit(solution)/shard_map/seq_scatter/pallas_call | solution.py:445
  1005.1 20.5 %multiply_reduce_fusion = (f32[400]{0:T(512)S(1)}, f32[400]{0:T(512)S(1)}, f32[400]{0:T(512)S(1)}, f32[400]{0:T(512)S(1)}, f32[400]{0:T(512)S(1)}, /*index=5*/f3...) fusion(f32[2048,400]{1,0:T(8,128)} %slice_convert_fusion.1, ...), kind=kOutput, calls=%fused_computation.64 | convolution fusion | flops 245758000 | bytes 36880704 | tf_op jit(solution)/shard_map/dot_general | solution.py:33
  1057.9 17.4 %convolution_convert_fusion.6 = bf16[1600,1376]{1,0:T(8,128)(2,1)} fusion(bf16[2048,1600]{1,0:T(8,128)(2,1)} %bitcast.188, bf16[2048,688]{0,1:T(8,128)(2,1)} %get-tuple-element.169, bf16[2048,688]{0,1:T(8,128)(2,1)} %get-tuple-element.168), kind=kOutput, calls=%fused_computation.16 | convolution fusion | flops 9031227392 | bytes 16592896 | tf_op jit(solution)/shard_map/dot_general | solution.py:33
  1107.6 31.8 %seq_scatter.9 = f32[256,1600]{1,0:T(8,128)S(1)} custom-call(bf16[8,256,1600]{2,1,0:T(8,128)(2,1)S(1)} %bitcast.180), custom_call_target="tpu_custom_call" | custom-call | tf_op jit(solution)/shard_map/seq_scatter/pallas_call | solution.py:445
  1140.2 29.1 %direct_fsdp.3 = (bf16[4,58,400]{2,1,0:T(8,128)(2,1)S(1)}, f32[4,24,400]{2,1,0:T(8,128)S(1)}, f32[4,3,1600]{2,1,0:T(4,128)S(1)}) custom-call(bf16[4,58,400]{2,1,0:T(8,128)(2,1)S(1)} %pad_maximum_fusion.6.refs_0_, f32[24,400]{1,0:T(8,128)S(1)} %concatenate.65.refs_1_, f32[3,1600]{1,0:T(4,128)S(1)} %pad_maximum_fusion.7.refs_2_), custom_call_target="tpu_custom_call" | custom-call | tf_op jit(solution)/shard_map/direct_fsdp/pallas_call | solution.py:413
  1240.1 34.3 %direct_seq.20 = (bf16[8,172,400]{2,1,0:T(8,128)(2,1)S(1)}, bf16[8,150,200]{2,1,0:T(8,128)(2,1)S(1)}, bf16[8,172,200]{2,1,0:T(8,128)(2,1)S(1)}) custom-call(bf16[8,172,400]{2,1,0:T(8,128)(2,1)S(1)} %copy.164.refs_0_, bf16[8,150,200]{2,1,0:T(8,128)(2,1)S(1)} %bitcast.200, bf16[8,172,200]{2,1,0:T(8,128)(2,1)S(1)} %bitcast.199), custom_call_target="tpu_custom_call" | custom-call | tf_op jit(solution)/shard_map/direct_seq/pallas_call | solution.py:413
  (493 shorter events, 490.1 us)
Async XLA Ops:
  7.2 185.6 %all-gather.11.cloned.1.call-start = ((), (), s32[]{:S(2)}) async-start(), calls=%async_computation.9 | async-start | bytes 2529280 | tf_op jit(solution)/shard_map/all_gather | solution.py:643
  61.4 135.6 %all-gather.13.cloned.1.call-start = ((), (), s32[]{:S(2)}) async-start(), calls=%async_computation.10 | async-start | bytes 2928640 | tf_op jit(solution)/shard_map/all_gather | solution.py:644
  64.5 172.1 %all-gather.7.cloned.1.call-start = ((), (), s32[]{:S(2)}) async-start(), calls=%async_computation.4 | async-start | bytes 4608000 | tf_op jit(solution)/shard_map/all_gather | solution.py:668
  93.9 439.7 %all-gather.9.cloned.1.call-start = ((), (), s32[]{:S(2)}) async-start(), calls=%async_computation.5 | async-start | bytes 5632000 | tf_op jit(solution)/shard_map/all_gather | solution.py:669
  98.2 1107.0 %reduce-scatter.13.cloned.1.call-start = ((), (), s32[]{:S(2)}) async-start(), calls=%async_computation.11 | async-start | bytes 2529280
  98.3 179.4 %copy-start.115 = (s32[640]{0:T(1024)}, s32[640]{0:T(1024)S(1)}, u32[]{:S(2)}) copy-start(s32[640]{0:T(1024)S(1)} %fusion.187) | copy-start | bytes 7684
  98.3 218.6 %copy-start.102 = (s32[1600]{0:T(1024)}, s32[1600]{0:T(1024)S(1)}, u32[]{:S(2)}) copy-start(s32[1600]{0:T(1024)S(1)} %fusion.130) | copy-start | bytes 19204
  98.6 234.6 %copy-start.80 = (f32[2048]{0:T(1024)}, f32[2048]{0:T(1024)S(1)}, u32[]{:S(2)}) copy-start(f32[2048]{0:T(1024)S(1)} %get-tuple-element.191) | copy-start | bytes 24580
  98.6 234.6 %copy-start.82 = (f32[2048]{0:T(1024)}, f32[2048]{0:T(1024)S(1)}, u32[]{:S(2)}) copy-start(f32[2048]{0:T(1024)S(1)} %get-tuple-element.192) | copy-start | bytes 24580
  98.6 234.6 %copy-start.84 = (f32[2048]{0:T(1024)}, f32[2048]{0:T(1024)S(1)}, u32[]{:S(2)}) copy-start(f32[2048]{0:T(1024)S(1)} %get-tuple-element.193) | copy-start | bytes 24580
  113.5 251.4 %copy-start.86 = (f32[400]{0:T(512)}, f32[400]{0:T(512)S(1)}, u32[]{:S(2)}) copy-start(f32[400]{0:T(512)S(1)} %add.566) | copy-start | bytes 4804
  113.6 219.5 %copy-start.104 = (f32[400]{0:T(512)}, f32[400]{0:T(512)S(1)}, u32[]{:S(2)}) copy-start(f32[400]{0:T(512)S(1)} %mul.732) | copy-start | bytes 4804
  113.7 219.5 %copy-start.106 = (f32[400]{0:T(512)}, f32[400]{0:T(512)S(1)}, u32[]{:S(2)}) copy-start(f32[400]{0:T(512)S(1)} %mul.727) | copy-start | bytes 4804
  113.8 219.4 %copy-start.108 = (f32[400]{0:T(512)}, f32[400]{0:T(512)S(1)}, u32[]{:S(2)}) copy-start(f32[400]{0:T(512)S(1)} %mul.722) | copy-start | bytes 4804
  113.9 219.3 %copy-start.110 = (f32[400]{0:T(512)}, f32[400]{0:T(512)S(1)}, u32[]{:S(2)}) copy-start(f32[400]{0:T(512)S(1)} %mul.719) | copy-start | bytes 4804
  114.6 380.4 %copy-start.52 = (bf16[1,256,1600]{2,1,0:T(8,128)(2,1)}, bf16[1,256,1600]{2,1,0:T(8,128)(2,1)S(1)}, u32[]{:S(2)}) copy-start(bf16[1,256,1600]{2,1,0:T(8,128)(2,1)S(1)} %copy.136) | copy-start | bytes 2457604
  117.1 226.8 %copy-start.72 = (bf16[132,400]{1,0:T(8,128)(2,1)}, bf16[132,400]{1,0:T(8,128)(2,1)S(1)}, u32[]{:S(2)}) copy-start(bf16[132,400]{1,0:T(8,128)(2,1)S(1)} %reshape.558) | copy-start | bytes 316804
  117.1 247.8 %copy-start.68 = (bf16[100,400]{1,0:T(8,128)(2,1)}, bf16[100,400]{1,0:T(8,128)(2,1)S(1)}, u32[]{:S(2)}) copy-start(bf16[100,400]{1,0:T(8,128)(2,1)S(1)} %reshape.559) | copy-start | bytes 240004
  192.8 86.5 %copy-start.28 = (f32[1280,256]{1,0:T(8,128)}, f32[1280,256]{1,0:T(8,128)S(1)}, u32[]{:S(2)}) copy-start(f32[1280,256]{1,0:T(8,128)S(1)} %fusion.63.bias_ref) | copy-start | bytes 3932164
  734.7 473.6 %reduce-scatter.11.cloned.1.call-start = ((), (), s32[]{:S(2)}) async-start(), calls=%async_computation.8 | async-start | bytes 2928640 | tf_op jit(solution)/shard_map/reduce_scatter | solution.py:862
  751.5 118.4 %copy-start.59 = (f32[2048,400]{1,0:T(8,128)S(1)}, f32[2048,400]{1,0:T(8,128)}, u32[]{:S(2)}) copy-start(f32[2048,400]{1,0:T(8,128)} %get-tuple-element.200) | copy-start | bytes 9830404
  751.5 118.4 %copy-start.87 = (f32[400]{0:T(512)S(1)}, f32[400]{0:T(512)}, u32[]{:S(2)}) copy-start(f32[400]{0:T(512)} %copy-done.86) | copy-start | bytes 4804
  1005.0 205.8 %reduce-scatter.7.cloned.1.call-start = ((), (), s32[]{:S(2)}) async-start(), calls=%async_computation.6 | async-start | bytes 4608000 | tf_op jit(solution)/shard_map/reduce_scatter | solution.py:843
  1057.8 174.2 %reduce-scatter.9.cloned.1.call-start = ((), (), s32[]{:S(2)}) async-start(), calls=%async_computation.7 | async-start | bytes 5632000 | tf_op jit(solution)/shard_map/reduce_scatter | solution.py:842
  (116 other events, 1931.8 us)
Sparse Core Ops, SparseCore 0:
  61.5 51.0 all-gather.10
  114.8 48.3 all-gather.12
  165.4 71.1 all-gather.6
  238.6 84.4 all-gather.8
  734.8 39.5 reduce-scatter.12
  1005.1 45.4 reduce-scatter.10
  1058.0 66.3 reduce-scatter.6
  1126.6 91.4 reduce-scatter.8

commit v3 on v2

--- a/solution.py
+++ b/solution.py
@@ -1,4 +1,5 @@
 import functools
+import math
 
 import jax
 import jax.numpy as jnp
@@ -64,26 +65,43 @@
         out[pl.ds(t0, 8), lane:end] = total[:, : end - lane]
 
 
-def scan_fwd_body(step_ref, push_ref, b_ref, c_ref, rate_ref, y_ref, st_ref, h_scr, part_scr):
+def spread(split_ref, eye_ref, out_scr):
+    eye = eye_ref[...]
+    ones = jnp.ones((2 * NS, 128), bf16)
+    for first in range(0, split_ref.shape[0], 16):
+        split = split_ref[first : first + 16, :]
+        spaced = jnp.concatenate([split[j : j + 1, :] * eye for j in range(16)], 0).astype(bf16)
+        out_scr[first * NS : (first + 16) * NS, :] = matmul(spaced, ones)
+
+
+def widen(value, width):
+    return jnp.concatenate([value] * (width // 128) + ([value[:, : width % 128]] if width % 128 else []), 1)
+
+
+def scan_fwd_body(
+    step_ref, push_ref, b_ref, c_ref, rate_ref, eye_ref, y_ref, st_ref, h_scr, part_scr, b_scr, c_scr
+):
     block = step_ref.shape[0]
 
     @pl.when(pl.program_id(0) == 0)
     def _():
         h_scr[...] = jnp.zeros_like(h_scr)
 
+    spread(b_ref, eye_ref, b_scr)
+    spread(c_ref, eye_ref, c_scr)
     rate = rate_ref[...]
+    width = rate.shape[1]
 
     def group(index, state):
         t0 = pl.multiple_of(index * 8, 8)
         step8 = step_ref[pl.ds(t0, 8), :]
         push8 = push_ref[pl.ds(t0, 8), :]
-        b_roll = pltpu.roll(b_ref[...], block - t0, 1)
-        c_roll = pltpu.roll(c_ref[...], block - t0, 1)
         for j in range(8):
-            decay = jnp.exp2(step8[j : j + 1, :] * rate)
-            state = decay * state + push8[j : j + 1, :] * b_roll[:, j : j + 1]
-            st_ref[t0 + j] = state
-            out = c_roll[:, j : j + 1] * state
+            at = pl.ds(pl.multiple_of((t0 + j) * NS, NS), NS)
+            decay = jnp.exp(step8[j : j + 1, :] * rate)
+            state = decay * state + push8[j : j + 1, :] * widen(b_scr[at, :], width)
+            st_ref[t0 + j] = state.astype(bf16)
+            out = widen(c_scr[at, :], width) * state
             park(part_scr, j, out[:8] + out[8:])
         fold(part_scr, y_ref, t0)
         return state
@@ -92,9 +110,10 @@
 
 
 def scan_bwd_body(
-    step_ref, push_ref, dpre_ref, b_ref, c_ref, st_ref, prev_ref, rate_ref,
-    pr_ref, pushed_ref, db_ref, dc_ref, log_ref, g_scr, log_scr, part1, part2,
+    step_ref, push_ref, dpre_ref, b_ref, c_ref, st_ref, prev_ref, rate_ref, eye_ref, *refs
 ):
+    pr_ref, pushed_ref, db_ref, dc_ref, log_ref = refs[-12:-7]
+    g_scr, log_scr, part1, part2, b_scr, c_scr, grad_scr = refs[-7:]
     block = step_ref.shape[0]
     count = pl.num_programs(0)
     which = pl.program_id(0)
@@ -104,52 +123,59 @@
         g_scr[...] = jnp.zeros_like(g_scr)
         log_scr[...] = jnp.zeros_like(log_scr)
 
-    lane_ids = lax.broadcasted_iota(jnp.int32, (NS, block), 1)
-    before = prev_ref[0] * jnp.where(which == count - 1, 0.0, 1.0)
-
-    def group(turn, carried):
-        grad_in, state, db_acc, dc_acc = carried
+    spread(b_ref, eye_ref, b_scr)
+    spread(c_ref, eye_ref, c_scr)
+    width = rate_ref.shape[1]
+    before = prev_ref[0].astype(f32) * jnp.where(which == count - 1, 0.0, 1.0)
+
+    def group(turn, grad_in):
         t0 = pl.multiple_of((block // 8 - 1 - turn) * 8, 8)
         step8 = step_ref[pl.ds(t0, 8), :]
-        push8 = push_ref[pl.ds(t0, 8), :]
         dpre8 = dpre_ref[pl.ds(t0, 8), :]
-        b_roll = pltpu.roll(b_ref[...], block - t0, 1)
-        c_roll = pltpu.roll(c_ref[...], block - t0, 1)
         rate = rate_ref[...]
         log_acc = log_scr[...]
         for j in range(7, -1, -1):
+            at = pl.ds(pl.multiple_of((t0 + j) * NS, NS), NS)
             if j > 0:
-                prior = st_ref[t0 + (j - 1)]
+                prior = st_ref[t0 + (j - 1)].astype(f32)
             else:
-                prior = jnp.where(t0 > 0, st_ref[jnp.maximum(t0 - 1, 0)], before)
+                prior = jnp.where(t0 > 0, st_ref[jnp.maximum(t0 - 1, 0)].astype(f32), before)
             step_row = step8[j : j + 1, :]
-            dpre_row = dpre8[j : j + 1, :]
-            grad = c_roll[:, j : j + 1] * dpre_row + grad_in
-            grad_in = grad * jnp.exp2(step_row * (rate * log2e))
+            grad = widen(c_scr[at, :], width) * dpre8[j : j + 1, :] + grad_in
+            grad_scr[at, :] = grad.astype(bf16)
+            grad_in = grad * jnp.exp(step_row * rate)
             flow = grad_in * prior
             by_rate = flow * rate
             park(part1, j, by_rate[:8] + by_rate[8:])
-            by_b = grad * b_roll[:, j : j + 1]
+            by_b = grad * widen(b_scr[at, :], width)
             park(part2, j, by_b[:8] + by_b[8:])
             log_acc = log_acc + flow * step_row
-            db = jnp.sum(grad * push8[j : j + 1, :], axis=1, keepdims=True)
-            dc = jnp.sum(state * dpre_row, axis=1, keepdims=True)
-            here = lane_ids == t0 + j
-            db_acc = jnp.where(here, db, db_acc)
-            dc_acc = jnp.where(here, dc, dc_acc)
-            state = prior
         log_scr[...] = log_acc
         fold(part1, pr_ref, t0)
         fold(part2, pushed_ref, t0)
-        return (grad_in, state, db_acc, dc_acc)
-
-    zero = jnp.zeros((NS, block), f32)
-    grad_in, _, db_acc, dc_acc = lax.fori_loop(
-        0, block // 8, group, (g_scr[...], st_ref[block - 1], zero, zero)
-    )
-    g_scr[...] = grad_in
-    db_ref[...] = db_acc
-    dc_ref[...] = dc_acc
+        return grad_in
+
+    g_scr[...] = lax.fori_loop(0, block // 8, group, g_scr[...])
+
+    lanes = lax.broadcasted_iota(jnp.int32, (NS, block), 1)
+
+    def own_token(left, right_ref, out_ref):
+        right = right_ref[...].astype(bf16)
+
+        totals = []
+        for i in range(block // 16):
+            pairs = dot_nt(left(i), right)
+            total = pairs[:NS]
+            for j in range(1, 16):
+                total = jnp.where(lanes == i * 16 + j, pairs[j * NS : (j + 1) * NS], total)
+            totals.append(total)
+        total = totals[0]
+        for i in range(1, block // 16):
+            total = jnp.where(lanes >= i * 16, totals[i], total)
+        out_ref[...] = total
+
+    own_token(lambda i: grad_scr[i * 16 * NS : (i + 1) * 16 * NS, :], push_ref, db_ref)
+    own_token(lambda i: st_ref[i * 16 : (i + 1) * 16].reshape(16 * NS, width), dpre_ref, dc_ref)
 
     @pl.when(which == count - 1)
     def _():
@@ -157,6 +183,12 @@
 
 
 SCAN_BLOCK = 128
+
+
+def split_halves(value):
+    high = lax.reduce_precision(value, 8, 7)
+    low = lax.reduce_precision(value - high, 8, 7)
+    return jnp.concatenate([high, low], 0).T
 
 
 def scan_forward(step_keep, push, b_t, c_t, rate):
@@ -164,43 +196,51 @@
     block = SCAN_BLOCK
     padded = (width + 127) // 128 * 128
     rows = pl.BlockSpec((block, width), lambda i: (i, 0))
-    cols = pl.BlockSpec((NS, block), lambda i: (0, i))
+    halves_spec = pl.BlockSpec((block, 2 * NS), lambda i: (i, 0))
     fixed = pl.BlockSpec((NS, width), lambda i: (0, 0))
+    eye = jnp.concatenate([jnp.eye(NS, dtype=f32)] * 2, 1)
     return pl.pallas_call(
         scan_fwd_body,
         grid=(tokens // block,),
-        in_specs=[rows, rows, cols, cols, fixed],
+        in_specs=[rows, rows, halves_spec, halves_spec, fixed, pl.BlockSpec(eye.shape, lambda i: (0, 0))],
         out_specs=[rows, pl.BlockSpec((block, NS, width), lambda i: (i, 0, 0))],
         out_shape=[
             jax.ShapeDtypeStruct((tokens, width), f32),
-            jax.ShapeDtypeStruct((tokens, NS, width), f32),
+            jax.ShapeDtypeStruct((tokens, NS, width), bf16),
         ],
-        scratch_shapes=[pltpu.VMEM((NS, width), f32), pltpu.VMEM((padded // 2, 128), f32)],
+        scratch_shapes=[
+            pltpu.VMEM((NS, width), f32),
+            pltpu.VMEM((padded // 2, 128), f32),
+            pltpu.VMEM((block * NS, 128), f32),
+            pltpu.VMEM((block * NS, 128), f32),
+        ],
         compiler_params=pltpu.CompilerParams(vmem_limit_bytes=40 << 20),
         cost_estimate=pl.CostEstimate(
             flops=tokens * width * NS * 8, bytes_accessed=tokens * width * NS * 4, transcendentals=tokens * width * NS
         ),
         name="scan_forward",
-    )(step_keep, push, b_t, c_t, rate * log2e)
-
-
-def scan_backward(step_keep, push, d_pre, b_t, c_t, states, rate):
+    )(step_keep, push, split_halves(b_t), split_halves(c_t), rate, eye)
+
+
+def scan_backward(step_keep, push, d_pre, b_t, c_t, states, rate, after=()):
     tokens, width = step_keep.shape
     block = SCAN_BLOCK
     padded = (width + 127) // 128 * 128
     last = tokens // block - 1
     rows = pl.BlockSpec((block, width), lambda i: (last - i, 0))
     cols = pl.BlockSpec((NS, block), lambda i: (0, last - i))
+    halves_spec = pl.BlockSpec((block, 2 * NS), lambda i: (last - i, 0))
     fixed = pl.BlockSpec((NS, width), lambda i: (0, 0))
+    eye = jnp.concatenate([jnp.eye(NS, dtype=f32)] * 2, 1)
     return pl.pallas_call(
         scan_bwd_body,
         grid=(tokens // block,),
         in_specs=[
-            rows, rows, rows, cols, cols,
+            rows, rows, rows, halves_spec, halves_spec,
             pl.BlockSpec((block, NS, width), lambda i: (last - i, 0, 0)),
             pl.BlockSpec((1, NS, width), lambda i: (jnp.maximum((last - i) * block - 1, 0), 0, 0)),
-            fixed,
-        ],
+            fixed, pl.BlockSpec(eye.shape, lambda i: (0, 0)),
+        ] + [pl.BlockSpec(memory_space=pl.ANY)] * len(after),
         out_specs=[rows, rows, cols, cols, fixed],
         out_shape=[
             jax.ShapeDtypeStruct((tokens, width), f32),
@@ -214,13 +254,16 @@
             pltpu.VMEM((NS, width), f32),
             pltpu.VMEM((padded // 2, 128), f32),
             pltpu.VMEM((padded // 2, 128), f32),
+            pltpu.VMEM((block * NS, 128), f32),
+            pltpu.VMEM((block * NS, 128), f32),
+            pltpu.VMEM((block * NS, width), bf16),
         ],
         compiler_params=pltpu.CompilerParams(vmem_limit_bytes=40 << 20),
         cost_estimate=pl.CostEstimate(
             flops=tokens * width * NS * 18, bytes_accessed=tokens * width * NS * 4, transcendentals=tokens * width * NS
         ),
         name="scan_backward",
-    )(step_keep, push, d_pre, b_t, c_t, states, states, rate)
+    )(step_keep, push, d_pre, split_halves(b_t), split_halves(c_t), states, states, rate, eye, *after)
 
 
 def places():
@@ -289,7 +332,8 @@
         copy.wait_send()
 
 
-def gather_body(x_ref, out_ref, sems, local_sem):
+def gather_body(x_ref, *refs):
+    out_ref, sems, local_sem = refs[-3:]
     me, core, sib, step_x, step_y = places()
     mine = pltpu.make_async_copy(x_ref, out_ref.at[me], local_sem)
     mine.start()
@@ -350,7 +394,81 @@
         copy.wait_send()
 
 
-def scatter_body(p_ref, out_ref, from_sib, acc, got_x, got_y, last_x, last_y, sems):
+def product_scatter_body(transposed, a_ref, w_ref, *refs):
+    out_ref, stage, from_sib, acc, got_x, got_y, last_x, last_y, sems = refs[-9:]
+    me, core, sib, step_x, step_y = places()
+    rows, width = out_ref.shape
+    greet([sib, me + step_x, me + step_y])
+    dests = (me + step_x + step_y, me + step_x, me + step_y, me)
+
+    def multiply(d, store):
+        left = a_ref[pl.ds(pl.multiple_of(d * rows, rows), rows), :]
+
+        def part(cols):
+            if transposed:
+                return dot_nt(left, w_ref[cols, :])
+            return matmul(left, w_ref[:, cols])
+
+        def step(i, _):
+            cols = pl.ds(pl.multiple_of(i * 512, 512), 512)
+            store(cols, part(cols))
+            return 0
+
+        lax.fori_loop(0, width // 512, step, 0, unroll=True)
+        if width % 512:
+            cols = pl.ds(width // 512 * 512, width % 512)
+            store(cols, part(cols))
+
+    def send(src, dst, k, to):
+        copy = remote(src, dst, sems, k, to)
+        copy.start()
+        return copy
+
+    def for_sibling(k):
+        def store(cols, value):
+            stage[k, :, cols] = value.astype(bf16)
+
+        multiply(dests[k] + 1 - 2 * core, store)
+        return send(stage.at[k], from_sib.at[k], k, sib)
+
+    def for_chip(k):
+        def store(cols, value):
+            acc[k, :, cols] = (value + from_sib[k, :, cols].astype(f32)).astype(bf16)
+
+        pairs[k].wait_recv()
+        multiply(dests[k], store)
+        return halves(acc.at[k], 16)
+
+    pairs = [for_sibling(0), for_sibling(1)]
+    top, low = for_chip(0)
+    out_x = [send(top, got_x.at[0], 4, me + step_x)]
+    out_y = [send(low, got_y.at[0], 5, me + step_y)]
+    pairs.append(for_sibling(2))
+    top, low = for_chip(1)
+    out_x.append(send(top, got_x.at[1], 6, me + step_x))
+    pairs.append(for_sibling(3))
+    top, low = for_chip(2)
+    out_y.append(send(low, got_y.at[1], 7, me + step_y))
+    out_x[0].wait_recv()
+    add_rows(got_x.at[0], [got_x.at[0], halves(acc.at[2], 16)[0]], 16)
+    last_a = send(got_x.at[0], last_y, 8, me + step_y)
+    out_y[0].wait_recv()
+    add_rows(got_y.at[0], [got_y.at[0], halves(acc.at[1], 16)[1]], 16)
+    last_b = send(got_y.at[0], last_x, 9, me + step_x)
+    top, low = for_chip(3)
+    out_x[1].wait_recv()
+    out_y[1].wait_recv()
+    out_top, out_low = halves(out_ref, 16)
+    last_a.wait_recv()
+    add_rows(out_top, [got_x.at[1], top, last_y], 16)
+    last_b.wait_recv()
+    add_rows(out_low, [got_y.at[1], low, last_x], 16)
+    for copy in pairs + out_x + out_y + [last_a, last_b]:
+        copy.wait_send()
+
+
+def scatter_body(p_ref, *refs):
+    out_ref, from_sib, acc, got_x, got_y, last_x, last_y, sems = refs[-8:]
     me, core, sib, step_x, step_y = places()
     greet([sib, me + step_x, me + step_y])
     scatter_steps(p_ref, out_ref, from_sib, acc, got_x, got_y, last_x, last_y, sems, 16)
@@ -376,26 +494,50 @@
     ]
 
 
-def direct_body(axis, size, modes, *refs):
+def direct_copies(sizes, axes, modes, ins, outs, sems, local_sems):
+    me = {axis: lax.axis_index(axis) for axis in sizes}
+    others = {axis: [(me[axis] + k) % size for k in range(1, size)] for axis, size in sizes.items()}
+    own, copies = [], []
+    for a, (x, out, axis, mode) in enumerate(zip(ins, outs, axes, modes)):
+        at = me[axis]
+        own.append(pltpu.make_async_copy(x.at[at] if mode == "exchange" else x, out.at[at], local_sems.at[a]))
+        for to in others[axis]:
+            src = x.at[to] if mode == "exchange" else x
+            copies.append(remote(src, out.at[at], sems, len(copies), to, axis))
+    return others, own, copies
+
+
+def direct_start(plan):
+    others, own, copies = plan
+    for copy in own:
+        copy.start()
+    barrier = pltpu.get_barrier_semaphore()
+    for axis, devices in others.items():
+        for d in devices:
+            pl.semaphore_signal(barrier, inc=1, device_id={axis: d}, device_id_type=MESH)
+    pl.semaphore_wait(barrier, sum(len(devices) for devices in others.values()))
+    for copy in copies:
+        copy.start()
+
+
+def direct_wait(plan):
+    for copy in plan[1] + plan[2]:
+        copy.wait()
+
+
+def direct_scratch(sizes, axes):
+    return [
+        pltpu.SemaphoreType.DMA((2, sum(sizes[axis] - 1 for axis in axes))),
+        pltpu.SemaphoreType.DMA((len(axes),)),
+    ]
+
+
+def direct_body(sizes, axes, modes, unused, *refs):
     count = len(modes)
-    ins, outs, (sems, local_sems) = refs[:count], refs[count : 2 * count], refs[2 * count :]
-    me = lax.axis_index(axis)
-    own = []
-    for a, (x, out, mode) in enumerate(zip(ins, outs, modes)):
-        copy = pltpu.make_async_copy(x.at[me] if mode == "exchange" else x, out.at[me], local_sems.at[a])
-        copy.start()
-        own.append(copy)
-    others = [(me + k) % size for k in range(1, size)]
-    greet(others, axis)
-    copies = []
-    for a, (x, out, mode) in enumerate(zip(ins, outs, modes)):
-        for k, to in enumerate(others):
-            src = x.at[to] if mode == "exchange" else x
-            copy = remote(src, out.at[me], sems, a * (size - 1) + k, to, axis)
-            copy.start()
-            copies.append(copy)
-    for copy in own + copies:
-        copy.wait()
+    ins, refs = refs[:count], refs[count + unused :]
+    plan = direct_copies(sizes, axes, modes, ins, refs[:count], *refs[count:])
+    direct_start(plan)
+    direct_wait(plan)
 
 
 any_space = pl.BlockSpec(memory_space=pl.ANY)
@@ -404,53 +546,75 @@
 
 def comm_params(collective_id):
     return pltpu.CompilerParams(
-        collective_id=collective_id, has_side_effects=True, vmem_limit_bytes=40 << 20
-    )
-
-
-def direct(axis, size, arrays, modes, collective_id):
-    shapes = [x.shape if mode == "exchange" else (size,) + x.shape for x, mode in zip(arrays, modes)]
+        collective_id=collective_id, has_side_effects=True, vmem_limit_bytes=48 << 20
+    )
+
+
+def direct(sizes, arrays, collective_id, after=()):
+    values = [x for x, _, _ in arrays]
+    axes = [axis for _, axis, _ in arrays]
+    modes = [mode for _, _, mode in arrays]
+    sizes = {axis: sizes[axis] for axis in sorted(set(axes))}
+    shapes = [x.shape if mode == "exchange" else (sizes[axis],) + x.shape for x, axis, mode in arrays]
     return pl.pallas_call(
-        functools.partial(direct_body, axis, size, modes),
-        out_shape=[jax.ShapeDtypeStruct(s, x.dtype) for s, x in zip(shapes, arrays)],
-        in_specs=[any_space] * len(arrays),
-        out_specs=[any_space] * len(arrays),
-        scratch_shapes=[
-            pltpu.SemaphoreType.DMA((2, len(arrays) * (size - 1))),
-            pltpu.SemaphoreType.DMA((len(arrays),)),
-        ],
+        functools.partial(direct_body, sizes, axes, modes, len(after)),
+        out_shape=[jax.ShapeDtypeStruct(s, x.dtype) for s, x in zip(shapes, values)],
+        in_specs=[any_space] * (len(values) + len(after)),
+        out_specs=[any_space] * len(values),
+        scratch_shapes=direct_scratch(sizes, axes),
         compiler_params=comm_params(collective_id),
-        name="direct_" + axis,
-    )(*arrays)
-
-
-def seq_gather(n, block, collective_id):
+        name="direct",
+    )(*values, *after)
+
+
+def seq_gather(n, block, collective_id, after=()):
     if n != 8:
         return lax.all_gather(block, "seq", axis=0, tiled=False)
     return pl.pallas_call(
         gather_body,
         out_shape=jax.ShapeDtypeStruct((8,) + block.shape, block.dtype),
-        in_specs=[any_space],
+        in_specs=[any_space] * (1 + len(after)),
         out_specs=any_space,
         scratch_shapes=[pltpu.SemaphoreType.DMA((2, 9)), pltpu.SemaphoreType.DMA],
         compiler_params=comm_params(collective_id),
         name="seq_gather",
-    )(block)
-
-
-def seq_scatter(n, parts, collective_id):
+    )(block, *after)
+
+
+def seq_scatter(n, parts, collective_id, after=()):
     if n != 8:
         return lax.psum_scatter(parts, "seq", scatter_dimension=0, tiled=False).astype(f32)
     _, rows, width = parts.shape
     return pl.pallas_call(
         scatter_body,
         out_shape=jax.ShapeDtypeStruct((rows, width), f32),
-        in_specs=[vmem_space],
+        in_specs=[vmem_space] + [any_space] * len(after),
         out_specs=vmem_space,
         scratch_shapes=scatter_scratch(rows, width, parts.dtype, 16) + [pltpu.SemaphoreType.DMA((2, 10))],
         compiler_params=comm_params(collective_id),
         name="seq_scatter",
-    )(parts)
+    )(parts, *after)
+
+
+def product_scatter(n, a, w, transposed, collective_id, after=()):
+    if n != 8:
+        product = (dot_nt if transposed else matmul)(a, w).astype(bf16)
+        return lax.psum_scatter(product, "seq", scatter_dimension=0, tiled=True).astype(f32)
+    rows, width = a.shape[0] // 8, w.shape[0 if transposed else 1]
+    return pl.pallas_call(
+        functools.partial(product_scatter_body, transposed),
+        out_shape=jax.ShapeDtypeStruct((rows, width), f32),
+        in_specs=[vmem_space, vmem_space] + [any_space] * len(after),
+        out_specs=vmem_space,
+        scratch_shapes=[pltpu.VMEM((4, rows, width), bf16)]
+        + scatter_scratch(rows, width, bf16, 16)
+        + [pltpu.SemaphoreType.DMA((2, 10))],
+        compiler_params=comm_params(collective_id),
+        cost_estimate=pl.CostEstimate(
+            flops=2 * a.shape[0] * a.shape[1] * width, bytes_accessed=100 << 20, transcendentals=0
+        ),
+        name="product_scatter",
+    )(a, w, *after)
 
 
 def seq_sum(n, parts, collective_id):
@@ -471,14 +635,14 @@
 def seq_token_sum(n, value, collective_id):
     if n != 8:
         return lax.psum(value, "seq")
-    (got,) = direct("seq", n, [value.reshape(-1, 128)], ("gather",), collective_id)
+    (got,) = direct({"seq": n}, [(value.reshape(-1, 128), "seq", "gather")], collective_id)
     return jnp.sum(got, 0).reshape(-1)
 
 
-def exchange(n, blocks, collective_id):
+def exchange(n, blocks, collective_id, after=()):
     if n != 8:
         return lax.all_to_all(blocks, "seq", 0, 0, tiled=False)
-    return direct("seq", n, [blocks], ("exchange",), collective_id)[0]
+    return direct({"seq": n}, [(blocks, "seq", "exchange")], collective_id, after)[0]
 
 
 def deal(total, parts, n):
@@ -499,8 +663,43 @@
     return lax.dot_general(left, right, (contract, ((), ())), precision=precision, preferred_element_type=f32)
 
 
+def window_start(tokens, span, length):
+    me = lax.axis_index("seq")
+    reach = (WINDOW_TOKENS + tokens - 2) // tokens
+    if length == 2 * reach * tokens:
+        first = me // reach * (me - reach) * tokens
+    else:
+        first = jnp.minimum(jnp.maximum(me - reach, 0) * tokens, length - span)
+    return pl.ds(pl.multiple_of(first, math.gcd(tokens, length - span)), span)
+
+
+def with_exchange(body, count, ins, outs):
+    def whole(*refs):
+        given, moved = refs[:ins], refs[ins : ins + count]
+        refs = refs[ins + count :]
+        made, arrived, sems = refs[:outs], refs[outs : outs + count], refs[outs + count :]
+        if count:
+            plan = direct_copies({"seq": 8}, ("seq",) * count, ("exchange",) * count, moved, arrived, *sems)
+
+            @pl.when(pl.program_id(0) == 0)
+            def _():
+                direct_start(plan)
+
+        body(*given, *made)
+        if count:
+
+            @pl.when(pl.program_id(0) == KEY_VALUE_HEADS - 1)
+            def _():
+                direct_wait(plan)
+
+    return whole
+
+
 def attn_fwd_body(qt_ref, kt_ref, vt_ref, bias_ref, out_ref, lse_ref):
-    keys = kt_ref[...].T
+    span, tokens = bias_ref.shape
+    window = window_start(tokens, span, kt_ref.shape[1])
+    keys = kt_ref[:, window].T
+    values_t = vt_ref[:, window]
     for head in range(qt_ref.shape[0] // HEAD_SIZE):
         rows = slice(head * HEAD_SIZE, (head + 1) * HEAD_SIZE)
         scores = matmul(keys, qt_ref[rows, :]) + bias_ref[...]
@@ -508,12 +707,15 @@
         exp_scores = jnp.exp(scores - row_max)
         row_total = jnp.sum(exp_scores, 0, keepdims=True)
         probs = (exp_scores * (1.0 / row_total)).astype(bf16)
-        out_ref[rows, :] = matmul(vt_ref[...], probs)
+        out_ref[rows, :] = matmul(values_t, probs)
         lse_ref[0, head : head + 1, :] = row_max + jnp.log(row_total)
 
 
 def attn_bwd_body(qt_ref, kt_ref, vt_ref, dot_ref, lse_ref, bias_ref, dqt_ref, dkt_ref, dvt_ref):
-    keys, values = kt_ref[...].T, vt_ref[...].T
+    span, tokens = bias_ref.shape
+    window = window_start(tokens, span, kt_ref.shape[1])
+    keys_t = kt_ref[:, window]
+    keys, values = keys_t.T, vt_ref[:, window].T
     dk = jnp.zeros(keys.shape, f32)
     dv = jnp.zeros(values.shape, f32)
     for head in range(qt_ref.shape[0] // HEAD_SIZE):
@@ -524,61 +726,80 @@
         d_probs = matmul(values, do_t)
         inner = jnp.sum(probs * d_probs, 0, keepdims=True)
         d_scores = (probs * (d_probs - inner)).astype(bf16)
-        dqt_ref[rows, :] = (matmul(kt_ref[...], d_scores) * (HEAD_SIZE**-0.5)).astype(bf16)
+        dqt_ref[rows, :] = (matmul(keys_t, d_scores) * (HEAD_SIZE**-0.5)).astype(bf16)
         dk = dk + matmul(d_scores, q_t.T)
         dv = dv + matmul(probs.astype(bf16), do_t.T)
-    dkt_ref[...] = dk.T.astype(bf16)
-    dvt_ref[...] = dv.T.astype(bf16)
-
-
-def attn_specs(tokens, span, groups):
+    dkt_ref[...] = jnp.zeros_like(dkt_ref)
+    dvt_ref[...] = jnp.zeros_like(dvt_ref)
+    dkt_ref[:, window] = dk.T.astype(bf16)
+    dvt_ref[:, window] = dv.T.astype(bf16)
+
+
+def attn_specs(tokens, span, groups, length):
     heads = pl.BlockSpec((groups * HEAD_SIZE, tokens), lambda h: (h, 0))
-    key = pl.BlockSpec((HEAD_SIZE, span), lambda h: (h, 0))
-    value = pl.BlockSpec((HEAD_SIZE, span), lambda h: (KEY_VALUE_HEADS + h, 0))
+    key = pl.BlockSpec((HEAD_SIZE, length), lambda h: (h, 0))
+    value = pl.BlockSpec((HEAD_SIZE, length), lambda h: (KEY_VALUE_HEADS + h, 0))
     lse = pl.BlockSpec((1, 8, tokens), lambda h: (h, 0, 0))
     bias = pl.BlockSpec((span, tokens), lambda h: (0, 0))
     return heads, key, value, lse, bias
 
 
-def attention_forward(q_t, kv_t, bias):
+def attention_call(body, name, in_specs, out_specs, out_shape, arrays, moved, collective_id, cost):
+    count = len(moved)
+    params = comm_params(collective_id) if count else pltpu.CompilerParams(vmem_limit_bytes=48 << 20)
+    return pl.pallas_call(
+        with_exchange(body, count, len(in_specs), len(out_specs)),
+        grid=(KEY_VALUE_HEADS,),
+        in_specs=in_specs + [any_space] * count,
+        out_specs=out_specs + [any_space] * count,
+        out_shape=out_shape + [jax.ShapeDtypeStruct(x.shape, x.dtype) for x in moved],
+        scratch_shapes=direct_scratch({"seq": 8}, ("seq",) * count) if count else [],
+        compiler_params=params,
+        cost_estimate=cost,
+        name=name,
+    )(*arrays, *moved)
+
+
+def attention_forward(q_t, kv_t, bias, moved, collective_id):
     span, tokens = bias.shape
-    heads, key, value, lse, bias_spec = attn_specs(tokens, span, QUERY_HEADS // KEY_VALUE_HEADS)
-    return pl.pallas_call(
+    heads, key, value, lse, bias_spec = attn_specs(tokens, span, QUERY_HEADS // KEY_VALUE_HEADS, kv_t.shape[1])
+    return attention_call(
         attn_fwd_body,
-        grid=(KEY_VALUE_HEADS,),
-        in_specs=[heads, key, value, bias_spec],
-        out_specs=[heads, lse],
-        out_shape=[
+        "attention_forward",
+        [heads, key, value, bias_spec],
+        [heads, lse],
+        [
             jax.ShapeDtypeStruct(q_t.shape, f32),
             jax.ShapeDtypeStruct((KEY_VALUE_HEADS, 8, tokens), f32),
         ],
-        compiler_params=pltpu.CompilerParams(vmem_limit_bytes=40 << 20),
-        cost_estimate=pl.CostEstimate(
+        (q_t, kv_t, kv_t, bias),
+        moved,
+        collective_id,
+        pl.CostEstimate(
             flops=QUERY_HEADS * span * tokens * 512, bytes_accessed=8 << 20, transcendentals=QUERY_HEADS * span * tokens
         ),
-        name="attention_forward",
-    )(q_t, kv_t, kv_t, bias)
-
-
-def attention_backward(q_t, kv_t, do_t, lse, bias):
+    )
+
+
+def attention_backward(q_t, kv_t, do_t, lse, bias, moved, collective_id):
     span, tokens = bias.shape
-    heads, key, value, lse_spec, bias_spec = attn_specs(tokens, span, QUERY_HEADS // KEY_VALUE_HEADS)
-    return pl.pallas_call(
+    heads, key, value, lse_spec, bias_spec = attn_specs(
+        tokens, span, QUERY_HEADS // KEY_VALUE_HEADS, kv_t.shape[1]
+    )
+    grad = jax.ShapeDtypeStruct((KEY_VALUE_HEADS * HEAD_SIZE, kv_t.shape[1]), bf16)
+    return attention_call(
         attn_bwd_body,
-        grid=(KEY_VALUE_HEADS,),
-        in_specs=[heads, key, value, heads, lse_spec, bias_spec],
-        out_specs=[heads, key, key],
-        out_shape=[
-            jax.ShapeDtypeStruct(q_t.shape, bf16),
-            jax.ShapeDtypeStruct((KEY_VALUE_HEADS * HEAD_SIZE, span), bf16),
-            jax.ShapeDtypeStruct((KEY_VALUE_HEADS * HEAD_SIZE, span), bf16),
-        ],
-        compiler_params=pltpu.CompilerParams(vmem_limit_bytes=40 << 20),
-        cost_estimate=pl.CostEstimate(
+        "attention_backward",
+        [heads, key, value, heads, lse_spec, bias_spec],
+        [heads, key, key],
+        [jax.ShapeDtypeStruct(q_t.shape, bf16), grad, grad],
+        (q_t, kv_t, kv_t, do_t, lse, bias),
+        moved,
+        collective_id,
+        pl.CostEstimate(
             flops=QUERY_HEADS * span * tokens * 1280, bytes_accessed=16 << 20, transcendentals=QUERY_HEADS * span * tokens
         ),
-        name="attention_backward",
-    )(q_t, kv_t, kv_t, do_t, lse, bias)
+    )
 
 
 def layer(
@@ -604,6 +825,7 @@
     cotangent,
 ):
     fast = n == 8
+    sizes = {"seq": n, "fsdp": m}
     me = lax.axis_index("seq")
     query_w = QUERY_HEADS * HEAD_SIZE
     key_w = KEY_VALUE_HEADS * HEAD_SIZE
@@ -625,24 +847,35 @@
         in_blocks = exact(deal_in, in_weight, ((0,), (1,))).astype(bf16).reshape(n, p_own // n, z_rows)
         small_blocks = exact(deal_small, small_w, ((0,), (1,))).astype(bf16).reshape(n, c_own // n, -1)
         in_blocks, small_blocks, ids = direct(
-            "seq", n, [in_blocks, small_blocks, doc_ids.reshape(-1, 128)], ("exchange", "exchange", "gather"), 0
+            sizes,
+            [(in_blocks, "seq", "exchange"), (small_blocks, "seq", "exchange"), (doc_ids.reshape(-1, 128), "seq", "gather")],
+            0,
         )
         ids = ids.reshape(-1)
         in_cols = in_blocks.reshape(p_own, z_rows).T
         small_cols = small_blocks.reshape(c_own, -1).T
+        seq_x = tokens[0].astype(f32)
+        normed_one, scale_one = rms_norm(seq_x, first_gain)
+        normed_one = seq_gather(n, normed_one.astype(bf16), 3, (in_blocks,))
         gu_blocks = gate_up.T.reshape(n, -1, z_rows)
         out_blocks = exact(deal_out, out_weight, ((0,), (0,))).astype(bf16).reshape(n, -1, out_weight.shape[1])
         down_blocks = down_weight.reshape(n, -1, down_weight.shape[1])
-        gu_blocks, out_blocks, down_blocks = direct(
-            "seq", n, [gu_blocks, out_blocks, down_blocks], ("exchange",) * 3, 1
+        out_blocks, down_blocks, small_full = direct(
+            sizes,
+            [(x, "seq", "exchange") for x in (out_blocks, down_blocks)] + [(small_cols, "fsdp", "gather")],
+            1,
+            (normed_one,),
         )
-        gu_cols = gu_blocks.reshape(-1, z_rows).T
         out_rows = out_blocks.transpose(1, 0, 2).reshape(-1, width)
         down_rows = down_blocks.transpose(1, 0, 2).reshape(-1, width)
-        (small_full,) = direct("fsdp", m, [small_cols], ("gather",), 2)
+        in_full = lax.all_gather(in_cols, "fsdp", axis=0, tiled=True)
+        in_full, out_rows, down_rows = lax.optimization_barrier((in_full, out_rows, down_rows))
         out_full = lax.all_gather(out_rows, "fsdp", axis=0, tiled=True)
         down_full = lax.all_gather(down_rows, "fsdp", axis=0, tiled=True)
     else:
+        seq_x = tokens[0].astype(f32)
+        normed_one, scale_one = rms_norm(seq_x, first_gain)
+        normed_one = seq_gather(n, normed_one.astype(bf16), 3)
         ids = lax.all_gather(doc_ids[0], "seq", axis=0, tiled=True)
         in_cols = lax.all_gather(in_weight, "seq", axis=1, tiled=True)
         in_cols = jnp.concatenate(
@@ -665,8 +898,8 @@
         out_full = exchange(n, out_rows, None).transpose(1, 0, 2).reshape(q_own + c_own, -1)
         down_rows = lax.all_gather(down_weight, "fsdp", axis=0, tiled=True).reshape(n, f_own, -1)
         down_full = exchange(n, down_rows, None).transpose(1, 0, 2).reshape(f_own, -1)
-    in_full = lax.all_gather(in_cols, "fsdp", axis=0, tiled=True)
-    gu_full = lax.all_gather(gu_cols, "fsdp", axis=0, tiled=True)
+        in_full = lax.all_gather(in_cols, "fsdp", axis=0, tiled=True)
+        gu_full = lax.all_gather(gu_cols, "fsdp", axis=0, tiled=True)
     select_own = small_full[:, :sel_rows].reshape(-1, c_own)
     step_own = small_full[:, sel_rows:].reshape(-1, c_own)
 
@@ -691,9 +924,7 @@
             value = exact(deal(query_w, (query_w,), n), value, ((0,), (0,))).astype(bf16)
         return value.reshape(n, q_own, local)
 
-    seq_x = tokens[0].astype(f32)
-    normed_one, scale_one = rms_norm(seq_x, first_gain)
-    normed_one = seq_gather(n, normed_one.astype(bf16), 3).reshape(length, width)
+    normed_one = normed_one.reshape(length, width)
     qkv_w = q_own + 2 * k_own
     qkv_t = exact(in_full[:, :qkv_w], normed_one, ((0,), (1,))).astype(bf16)
     branch = matmul(normed_one, in_full[:, qkv_w:]).astype(bf16)
@@ -706,21 +937,22 @@
     reach = (WINDOW_TOKENS + local - 2) // local
     span = min((reach + 1) * local, length)
     first_key = jnp.clip((me - reach) * local, 0, length - span)
-    kv_win = lax.dynamic_slice_in_dim(kv_all, first_key, span, 2)
-    if fast:
-        deal_kv = deal(2 * key_w, (key_w, key_w), n)
-        kv_t = exact(deal_kv, kv_win.reshape(2 * key_w, span), ((1,), (0,))).astype(bf16)
-    else:
-        kv_t = jnp.concatenate(
-            [kv_win[:, :k_own].reshape(key_w, span), kv_win[:, k_own:].reshape(key_w, span)], 0
-        )
+    nat = jnp.arange(2 * key_w, dtype=jnp.int32)
+    inside = nat % key_w
+    block_order = inside // k_own * 2 * k_own + nat // key_w * k_own + inside % k_own
+    deal_kv = (
+        deal(2 * key_w, (key_w, key_w), n) if fast else (block_order[:, None] == nat[None, :]).astype(bf16)
+    )
+    kv_t = exact(deal_kv, kv_all.reshape(2 * key_w, length), ((1,), (0,))).astype(bf16)
     query_pos = me * local + jnp.arange(local, dtype=jnp.int32)
     key_pos = first_key + jnp.arange(span, dtype=jnp.int32)
     offset = query_pos[None, :] - key_pos[:, None]
     key_ids = lax.dynamic_slice_in_dim(ids, first_key, span, 0)
     allowed = (offset >= 0) & (offset < WINDOW_TOKENS) & (doc_ids[0][None, :] == key_ids[:, None])
     bias = jnp.where(allowed, 0.0, masked_score).astype(f32)
-    attended, lse = attention_forward(q_t, kv_t, bias)
+    attended, lse, *moved = attention_forward(q_t, kv_t, bias, [gu_blocks] if fast else [], 23)
+    if fast:
+        gu_full = lax.all_gather(moved[0].reshape(-1, z_rows).T, "fsdp", axis=0, tiled=True)
     attn_scale = lax.rsqrt(jnp.mean(attended * attended, axis=0, keepdims=True) + norm_eps)
     attn_normed = (attended * attn_scale * attn_gain[:, None]).astype(bf16)
     attn_c = exchange(n, heads_out(attn_normed), 6).transpose(0, 2, 1).reshape(length, q_own)
@@ -755,7 +987,7 @@
     mamba_scale = lax.rsqrt(square_sum / DI + norm_eps)[:, None]
     mamba_normed = mamba_out * mamba_scale * mamba_g
     joined = jnp.concatenate([attn_c, mamba_normed.astype(bf16)], 1)
-    mixed = seq_scatter(n, matmul(joined, out_full).astype(bf16).reshape(n, local, width), 9)
+    mixed = product_scatter(n, joined, out_full, False, 9)
     hidden = seq_x + 0.5 * mixed
     normed_two, scale_two = rms_norm(hidden, second_gain)
     normed_two = seq_gather(n, normed_two.astype(bf16), 10).reshape(length, width)
@@ -764,10 +996,10 @@
     up_part = gate_up_out[:, f_own:].astype(f32)
     gate_act = jax.nn.sigmoid(gate_part)
     inner = (gate_part * gate_act * up_part).astype(bf16)
-    ffn = seq_scatter(n, matmul(inner, down_full).astype(bf16).reshape(n, local, width), 11)
-    out_tokens = (hidden + ffn).astype(bf16)
-
-    d_ffn = seq_gather(n, cotangent[0], 12).reshape(length, width)
+    ffn = matmul(inner, down_full).astype(bf16)
+
+    own_d_out = cotangent[0] if fast else lax.optimization_barrier((cotangent[0], inner))[0]
+    d_ffn = lax.all_gather(own_d_out, "seq", axis=0, tiled=True)
     down_term = dot_tn(inner, d_ffn).astype(bf16)
     d_inner = dot_nt(d_ffn, down_full)
     d_gate_up = jnp.concatenate(
@@ -778,27 +1010,17 @@
         1,
     ).astype(bf16)
     gate_up_term = dot_tn(normed_two, d_gate_up).astype(bf16)
-    d_normed_two = seq_scatter(n, dot_nt(d_gate_up, gu_full).astype(bf16).reshape(n, local, width), 13)
+    gu_part = lax.psum_scatter(gate_up_term, "fsdp", scatter_dimension=0, tiled=True)
+    if fast:
+        down_part = lax.psum_scatter(down_term.reshape(m, -1, width), "fsdp", scatter_dimension=0, tiled=False)
+    d_normed_two = product_scatter(n, d_gate_up, gu_full, True, 13, (down_term, gate_up_term))
     d_hidden_part, second_grad = norm_back(hidden, scale_two, second_gain, d_normed_two)
     d_hidden = cotangent[0].astype(f32) + d_hidden_part
-    d_mixed = seq_gather(n, d_hidden.astype(bf16), 14).reshape(length, width)
+    d_mixed = seq_gather(n, d_hidden.astype(bf16), 14, (down_part,) if fast else ()).reshape(length, width)
     out_term = (0.5 * dot_tn(joined, d_mixed)).astype(bf16)
+    if fast:
+        out_part = lax.psum_scatter(out_term.reshape(m, -1, width), "fsdp", scatter_dimension=0, tiled=False)
     d_joined = 0.5 * dot_nt(d_mixed, out_full)
-
-    d_attn = d_joined[:, :q_own].astype(bf16).reshape(n, local, q_own).transpose(0, 2, 1)
-    d_attn = heads_in(exchange(n, d_attn, 15)).astype(f32)
-    weighted_a = d_attn * attn_gain[:, None]
-    attn_grad = jnp.sum(d_attn * attended * attn_scale, 1)
-    mean_a = jnp.mean(weighted_a * attended, axis=0, keepdims=True)
-    d_attended = attn_scale * weighted_a - attended * (attn_scale * attn_scale * attn_scale) * mean_a
-    dq_t, dk_t, dv_t = attention_backward(q_t, kv_t, d_attended.astype(bf16), lse, bias)
-    d_queries = exchange(n, heads_out(dq_t), 16).transpose(0, 2, 1).reshape(length, q_own)
-    if fast:
-        dkv = exact(deal_kv, jnp.concatenate([dk_t, dv_t], 0), ((0,), (0,))).astype(bf16).reshape(n, 2 * k_own, span)
-    else:
-        dkv = jnp.concatenate([dk_t.reshape(n, k_own, span), dv_t.reshape(n, k_own, span)], 1)
-    dkv = lax.dynamic_update_slice_in_dim(jnp.zeros((n, 2 * k_own, length), bf16), dkv, first_key, 2)
-    dkv = seq_scatter(n, dkv, 17).astype(bf16).T
 
     u = d_joined[:, q_own:]
     weighted = u * mamba_g
@@ -809,8 +1031,31 @@
     d_gate = d_mamba * mamba_pre * gate_sig * (1.0 + gate_z * (1.0 - gate_sig))
     skip_grad = jnp.sum(d_pre * activated, 0)
     by_rate, pushed, db_t, dc_t, decay_log_grad = scan_backward(
-        step_keep, push, d_pre, b_t, c_t, states, rate
-    )
+        step_keep, push, d_pre, b_t, c_t, states, rate, (out_part,) if fast else ()
+    )
+    ffn, db_t = lax.optimization_barrier((ffn, db_t))
+    ffn = lax.psum_scatter(ffn, "seq", scatter_dimension=0, tiled=True)
+    out_tokens = (hidden + ffn.astype(f32)).astype(bf16)
+
+    d_attn = d_joined[:, :q_own].astype(bf16).reshape(n, local, q_own).transpose(0, 2, 1)
+    d_attn = heads_in(exchange(n, d_attn, 15, (gu_part,))).astype(f32)
+    weighted_a = d_attn * attn_gain[:, None]
+    attn_grad = jnp.sum(d_attn * attended * attn_scale, 1)
+    mean_a = jnp.mean(weighted_a * attended, axis=0, keepdims=True)
+    d_attended = attn_scale * weighted_a - attended * (attn_scale * attn_scale * attn_scale) * mean_a
+    moved = []
+    if fast:
+        out_blocks = out_part.reshape(-1, n, width // n).transpose(1, 0, 2)
+        down_blocks = down_part.reshape(-1, n, width // n).transpose(1, 0, 2)
+        gu_blocks = gu_part.T.reshape(n, -1, z_rows)
+        moved = [gu_blocks, out_blocks, down_blocks]
+    dq_t, dk_t, dv_t, *moved = attention_backward(
+        q_t, kv_t, d_attended.astype(bf16), lse, bias, moved, 24
+    )
+    d_queries = exchange(n, heads_out(dq_t), 16, (out_tokens,)).transpose(0, 2, 1).reshape(length, q_own)
+    dkv = exact(deal_kv, jnp.concatenate([dk_t, dv_t], 0), ((0,), (0,))).astype(bf16).reshape(n, 2 * k_own, length)
+    dkv = seq_scatter(n, dkv, 17).astype(bf16).T
+
     step_grads = by_rate + pushed * activated
     d_step_pre = step_grads * jax.nn.sigmoid(step_pre)
     step_bias_grad = jnp.sum(d_step_pre, 0)
@@ -835,11 +1080,10 @@
     d_inputs = ext_grad[KC - 1 :]
     d_projected = jnp.concatenate([d_queries, dkv, d_inputs.astype(bf16), d_gate.astype(bf16)], 1)
     in_term = dot_tn(normed_one, d_projected).astype(bf16)
-    d_normed_one = seq_scatter(n, dot_nt(d_projected, in_full).astype(bf16).reshape(n, local, width), 20)
+    d_normed_one = product_scatter(n, d_projected, in_full, True, 20, (in_term,))
     d_x_part, first_grad = norm_back(seq_x, scale_one, first_gain, d_normed_one)
     tokens_grad = (d_hidden + d_x_part).astype(bf16)
 
-    gu_part = lax.psum_scatter(gate_up_term, "fsdp", scatter_dimension=0, tiled=True)
     in_part = lax.psum_scatter(in_term, "fsdp", scatter_dimension=0, tiled=True)
     small_term = jnp.concatenate(
         [select_term.reshape(m, sel_rows, c_own), step_term.reshape(m, -1, c_own)], 1
@@ -852,33 +1096,30 @@
         0,
     )
     wide_grads = jnp.stack([first_grad, second_grad, attn_grad])
-    small_z, channel_z, wide_z = direct(
-        "fsdp", m, [small_term, channel, wide_grads], ("exchange", "gather", "gather"), 21
-    )
+    small_specs = [(small_term, "fsdp", "exchange"), (channel, "fsdp", "gather"), (wide_grads, "fsdp", "gather")]
+    if fast:
+        gu_blocks, out_blocks, down_blocks = moved
+    small_z, channel_z, wide_z = direct(sizes, small_specs, 21)
     small_part = jnp.sum(small_z.astype(f32), 0)
     channel, wide_grads = jnp.sum(channel_z, 0), jnp.sum(wide_z, 0)
     if fast:
-        out_part = lax.psum_scatter(out_term.reshape(m, -1, width), "fsdp", scatter_dimension=0, tiled=False)
-        down_part = lax.psum_scatter(down_term.reshape(m, -1, width), "fsdp", scatter_dimension=0, tiled=False)
-        out_blocks = out_part.reshape(-1, n, width // n).transpose(1, 0, 2)
-        down_blocks = down_part.reshape(-1, n, width // n).transpose(1, 0, 2)
-        gu_blocks = gu_part.T.reshape(n, -1, z_rows)
-        gu_blocks, out_blocks, down_blocks = direct(
-            "seq", n, [gu_blocks, out_blocks, down_blocks], ("exchange",) * 3, 22
-        )
         gu_sum = gu_blocks.reshape(-1, z_rows).T.astype(f32)
         out_sum = exact(deal_out, out_blocks.reshape(-1, width // n), ((1,), (0,)))
         down_sum = down_blocks.reshape(-1, width // n).astype(f32)
         small_blocks = small_part.astype(bf16).T.reshape(n, c_own // n, -1)
-        small_blocks, channel_all, wide_all = direct(
-            "seq", n, [small_blocks, channel, wide_grads], ("exchange", "gather", "gather"), 23
+        in_blocks, small_blocks, channel_all, wide_all = direct(
+            sizes,
+            [
+                (in_part.T.reshape(n, -1, z_rows), "seq", "exchange"), (small_blocks, "seq", "exchange"),
+                (channel, "seq", "gather"), (wide_grads, "seq", "gather"),
+            ],
+            22,
         )
         small_sum = exact(small_blocks.reshape(c_own, -1), deal_small, ((0,), (1,)))
         channel_rows = channel.shape[0]
         channel = channel_all.reshape(n, channel_rows, n, c_own // n).transpose(1, 2, 0, 3).reshape(-1, c_own)
         channel = exact(channel, deal_small, ((1,), (1,)), highest).reshape(channel_rows, DI)
         wide_grads = jnp.sum(wide_all, 0)
-        (in_blocks,) = direct("seq", n, [in_part.T.reshape(n, -1, z_rows)], ("exchange",), 24)
         in_sum = exact(in_blocks.reshape(p_own, z_rows), deal_in, ((0,), (1,)))
     else:
         out_blocks = exchange(n, out_term.reshape(q_own + c_own, n, -1).transpose(1, 0, 2), None)

time: 1310 us -> 1020 us (0.78)
  Pallas kernels: 789 us -> 607 us
  local copies, waits for them, and re-layouts: 204 us -> 127 us
  waiting for transfers between devices: 36.5 us -> 11.1 us
    pallas_call x5 -> x1, Pallas kernels: 148 us -> 17.4 us  [seq_scatter(): pl.pallas_call(scatter_body, out_shape=jax.ShapeDtypeStruct((rows, width)...]
    pallas_call x15, Pallas kernels: 269 us -> 320 us  [the longest x10 133 us: direct(): pl.pallas_call(functools.partial(direct_body, sizes, axes, modes, len(aft...]
    pallas_call x1, Pallas kernels: 118 us -> 71.1 us  [scan_backward(): pl.pallas_call(scan_bwd_body, grid=(tokens // block,), in_specs=[rows, ro...]
    convert_element_type x4 -> x0, local copies, waits for them, and re-layouts: 38.5 us -> none  [the longest x1 9.72 us: layer(): matmul(joined, out_full).astype(bf16).reshape(n, local, width)]
    pallas_call x5 -> x4, Pallas kernels: 156 us -> 124 us  [seq_gather(): pl.pallas_call(gather_body, out_shape=jax.ShapeDtypeStruct((8,) + block.s...]
    all_gather x1, waiting for transfers between devices: 36.3 us -> 7.94 us  [layer(): in_full = lax.all_gather(in_cols, 'fsdp', axis=0, tiled=True)]
    pallas_call x1, Pallas kernels: 57.8 us -> 33.9 us  [scan_forward(): pl.pallas_call(scan_fwd_body, grid=(tokens // block,), in_specs=[rows, ro...]
    dynamic_update_slice x1 -> x0, local copies, waits for them, and re-layouts: 22.6 us -> none  [layer(): lax.dynamic_update_slice_in_dim(jnp.zeros((n, 2 * k_own, length), bf16),...]
  transfers between devices with their start and end apart: 8 -> 10, of which waited for: 1 -> 2; matrix products, arithmetic and copies ran while one was open for 22% -> 28% of each run, Pallas kernels for 48% -> 51%
where the time goes in v3:
time: 1020 us
  Pallas kernels  607 us (60%)
  matrix products  191 us (19%)
  local copies, waits for them, and re-layouts  127 us (12%)
  other arithmetic  61.3 us (6%)
  between operations  16.2 us (2%)
  waiting for transfers between devices  11.1 us (1%)
    pallas_call x10, Pallas kernels, direct(): pl.pallas_call(functools.partial(direct_body, sizes, axes, modes, len(aft...  133 us
    pallas_call x4, Pallas kernels, seq_gather(): pl.pallas_call(gather_body, out_shape=jax.ShapeDtypeStruct((8,) + block.s...  124 us
    pallas_call x3, Pallas kernels, product_scatter(): pl.pallas_call(functools.partial(product_scatter_body, transposed), out_s...  122 us
    dot_general x6, matrix products, dot_tn(): lax.dot_general(left, right, (((0,), (0,)), ((), ())), preferred_element_...  78.6 us
    pallas_call x1, Pallas kernels, scan_backward(): pl.pallas_call(scan_bwd_body, grid=(tokens // block,), in_specs=[rows, ro...  71.1 us
    pallas_call x2, Pallas kernels, attention_call(): pl.pallas_call(with_exchange(body, count, len(in_specs), len(out_specs)),...  65.6 us
    dot_general x5, matrix products, matmul(): return jnp.dot(left, right, preferred_element_type=f32)  45.2 us
    dot_general x15, matrix products, exact(): lax.dot_general(left, right, (contract, ((), ())), precision=precision, p...  42.8 us
  transfers between devices with their start and end apart: 10, of which 2 were waited for; matrix products, arithmetic and copies ran while one was open for 28% of the time, Pallas kernels for 51%

profile of v3, /device:TPU:0, one launch (start us, length us, event | category | flops | bytes accessed | tf_op | source)
XLA Modules:
  0.0 1015.5 jit_solution(5849690063760624874)
XLA Ops:
  11.7 19.4 %direct.10 = (bf16[8,135,400]{2,1,0:T(8,128)(2,1)S(1)}, bf16[8,50,58]{2,1,0:T(8,128)(2,1)S(1)}, s32[8,2,128]{2,1,0:T(2,128)S(1)}) custom-call(bf16[8,135,400]{2,1,0:T(8,128)(2,1)S(1)} %reshape.531.refs_0_, bf16[8,50,58]{2,1,0:T(8,128)(2,1)S(1)} %copy.147.refs_1_, s32[2,128]{1,0:T(2,128)S(1)} %bitcast.211), custom_call_target="tpu_custom_call" | custom-call | tf_op jit(solution)/shard_map/direct/pallas_call | solution.py:559
  46.0 35.8 %seq_gather.4.refs_3_ = bf16[8,256,1600]{2,1,0:T(8,128)(2,1)} custom-call(bf16[256,1600]{1,0:T(8,128)(2,1)S(1)} %fusion.60.x_ref, bf16[8,135,400]{2,1,0:T(8,128)(2,1)S(1)} %get-tuple-element.51.refs_0_), custom_call_target="tpu_custom_call" | custom-call | tf_op jit(solution)/shard_map/seq_gather/pallas_call | solution.py:573
  81.8 19.2 %direct.11 = (bf16[8,150,200]{2,1,0:T(8,128)(2,1)S(1)}, bf16[8,172,200]{2,1,0:T(8,128)(2,1)S(1)}, bf16[4,58,400]{2,1,0:T(8,128)(2,1)S(1)}) custom-call(bf16[8,150,200]{2,1,0:T(8,128)(2,1)S(1)} %reshape.535.refs_0_, bf16[8,172,200]{2,1,0:T(8,128)(2,1)S(1)} %copy.151.refs_1_, bf16[58,400]{1,0:T(8,128)(2,1)S(1)} %bitcast.205, ...), custom_call_target="tpu_custom_call" | custom-call | tf_op jit(solution)/shard_map/direct/pallas_call | solution.py:559
  141.3 18.9 %seq_gather.5 = bf16[8,80,2048]{2,1,0:T(8,128)(2,1)S(1)} custom-call(bf16[80,2048]{1,0:T(8,128)(2,1)S(1)} %slice.222.x_ref), custom_call_target="tpu_custom_call" | custom-call | tf_op jit(solution)/shard_map/seq_gather/pallas_call | solution.py:573
  166.2 29.3 %attention_forward.1 = (f32[1600,256]{1,0:T(8,128)}, f32[5,8,256]{2,1,0:T(8,128)S(1)}, bf16[8,172,400]{2,1,0:T(8,128)(2,1)S(1)}) custom-call(bf16[1600,256]{1,0:T(8,128)(2,1)S(1)} %fusion.55.refs_0_, bf16[640,2048]{1,0:T(8,128)(2,1)} %convolution_convert_fusion.6.refs_1_.refs_2_, bf16[640,2048]{1,0:T(8,128)(2,1)} %convolution_convert_fusion.6.refs_1_.refs_2_, ...), custom_call_target="tpu_custom_call" | custom-call | flops 4194304000 | bytes 8388608 | tf_op jit(solution)/shard_map/attention_forward/pallas_call | solution.py:750
  245.6 20.6 %seq_sum.2 = f32[136,2048]{1,0:T(8,128)S(1)} custom-call(f32[136,2048]{1,0:T(8,128)S(1)} %fusion.92.p_ref), custom_call_target="tpu_custom_call" | custom-call | tf_op jit(solution)/shard_map/seq_sum/pallas_call | solution.py:624
  274.5 33.9 %scan_forward.1 = (f32[2048,400]{1,0:T(8,128)S(1)}, bf16[2048,16,400]{2,1,0:T(8,128)(2,1)}) custom-call(f32[2048,400]{1,0:T(8,128)S(1)} %get-tuple-element.188.step_ref, f32[2048,400]{1,0:T(8,128)} %get-tuple-element.187.push_ref, f32[2048,32]{1,0:T(8,128)S(1)} %bitcast.185, f32[2048,32]{1,0:T(8,128)S(1)} %bitcast.187, f32[16,400]{1,0:T(8,128)S(1)} %neg.26.rate_ref, ...), custom_call_target="tpu_custom_call" | custom-call | flops 104857600 | bytes 52428800 | tf_op jit(solution)/shard_map/scan_forward/pallas_call | solution.py:202
  327.7 41.1 %product_scatter.3 = f32[256,1600]{1,0:T(8,128)S(1)} custom-call(bf16[2048,600]{1,0:T(8,128)(2,1)} %pad_maximum_fusion.1.a_ref, bf16[600,1600]{1,0:T(8,128)(2,1)S(1)} %copy-done.16), custom_call_target="tpu_custom_call" | custom-call | flops 3932160000 | bytes 104857600 | tf_op jit(solution)/shard_map/product_scatter/pallas_call | solution.py:604
  370.6 34.9 %seq_gather.6 = bf16[8,256,1600]{2,1,0:T(8,128)(2,1)} custom-call(bf16[256,1600]{1,0:T(8,128)(2,1)S(1)} %multiply_convert_fusion.3.x_ref), custom_call_target="tpu_custom_call" | custom-call | tf_op jit(solution)/shard_map/seq_gather/pallas_call | solution.py:573
  408.8 16.4 %convolution_convert_fusion.2 = bf16[2048,1376]{1,0:T(8,128)(2,1)} fusion(bf16[2048,1600]{1,0:T(8,128)(2,1)} %bitcast.218, bf16[1600,1376]{1,0:T(8,128)(2,1)} %all-gather.11.cloned.1.call-done.w_ref), kind=kOutput, calls=%fused_computation.14 | convolution fusion | flops 9020571648 | bytes 16592896 | tf_op jit(solution)/shard_map/dot_general | solution.py:30
  425.2 13.8 %fusion.39.refs_0_ = bf16[688,1600]{1,0:T(8,128)(2,1)} fusion(bf16[1,2048,1600]{1,2,0:T(8,128)(2,1)} %all-gather.13.cloned.1.call-done, bf16[2048,1376]{1,0:T(8,128)(2,1)} %convolution_convert_fusion.2), kind=kOutput, calls=%fused_computation.93 | convolution fusion | flops 4521249792 | bytes 15046656 | tf_op jit(solution)/shard_map/dot_general | solution.py:34
  442.1 14.4 %fusion.11 = (bf16[2048,688]{1,0:T(8,128)(2,1)S(1)}, bf16[2048,688]{1,0:T(8,128)(2,1)}) fusion(bf16[2048,1376]{1,0:T(8,128)(2,1)} %convolution_convert_fusion.2, bf16[688,1600]{1,0:T(8,128)(2,1)} %reshape.580, bf16[1,2048,1600]{1,2,0:T(8,128)(2,1)} %all-gather.13.cloned.1.call-done), kind=kOutput, calls=%fused_computation.31 | convolution fusion | flops 4530012160 | bytes 20027392 | tf_op jit(solution)/shard_map/dot_general | solution.py:38
  462.5 15.3 %convolution_convert_fusion.3.refs_1_ = bf16[1600,1376]{1,0:T(8,128)(2,1)} fusion(bf16[2048,1600]{1,0:T(8,128)(2,1)} %bitcast.219, bf16[2048,1376]{1,0:T(8,128)(2,1)S(1)} %pad_maximum_fusion.a_ref), kind=kOutput, calls=%fused_computation.15 | convolution fusion | flops 9019955200 | bytes 16592896 | tf_op jit(solution)/shard_map/dot_general | solution.py:34
  479.5 41.1 %product_scatter.4 = f32[256,1600]{1,0:T(8,128)S(1)} custom-call(bf16[2048,1376]{1,0:T(8,128)(2,1)} %copy-done.45, bf16[1600,1376]{1,0:T(8,128)(2,1)} %all-gather.11.cloned.1.call-done.w_ref, bf16[688,1600]{1,0:T(8,128)(2,1)S(1)} %copy-done.13, bf16[1600,1376]{1,0:T(8,128)(2,1)} %convolution_convert_fusion.3.refs_1_), custom_call_target="tpu_custom_call" | custom-call | flops 9017753600 | bytes 104857600 | tf_op jit(solution)/shard_map/product_scatter/pallas_call | solution.py:604
  524.0 34.3 %seq_gather.7 = bf16[8,256,1600]{2,1,0:T(8,128)(2,1)} custom-call(bf16[256,1600]{1,0:T(8,128)(2,1)S(1)} %get-tuple-element.173.x_ref, bf16[172,1600]{1,0:T(8,128)(2,1)S(1)} %bitcast.195), custom_call_target="tpu_custom_call" | custom-call | tf_op jit(solution)/shard_map/seq_gather/pallas_call | solution.py:573
  613.9 71.1 %scan_backward.1 = (f32[2048,400]{1,0:T(8,128)S(1)}, f32[2048,400]{1,0:T(8,128)S(1)}, f32[16,2048]{1,0:T(8,128)S(1)}, f32[16,2048]{1,0:T(8,128)S(1)}, f32[16,400]{1,0:T(8,128)S(1)}) custom-call(f32[2048,400]{1,0:T(8,128)} %copy-done.2, f32[2048,400]{1,0:T(8,128)} %get-tuple-element.187.push_ref, f32[2048,400]{1,0:T(8,128)} %get-tuple-element.170.dpre_ref, ...), custom_call_target="tpu_custom_call" | custom-call | flops 235929600 | bytes 52428800 | tf_op jit(solution)/shard_map/scan_backward/pallas_call | solution.py:235
  705.4 19.8 %seq_sum.3 = f32[136,2048]{1,0:T(8,128)S(1)} custom-call(f32[136,2048]{1,0:T(8,128)S(1)} %maximum_maximum_fusion.p_ref), custom_call_target="tpu_custom_call" | custom-call | tf_op jit(solution)/shard_map/seq_sum/pallas_call | solution.py:624
  725.4 19.4 %multiply_reduce_fusion = (f32[400]{0:T(512)S(1)}, f32[400]{0:T(512)S(1)}, f32[400]{0:T(512)S(1)}, f32[400]{0:T(512)S(1)}, f32[400]{0:T(512)S(1)}, /*index=5*/f3...) fusion(f32[2048,400]{1,0:T(8,128)} %copy-done.39, f32[2048]{0:T(1024)S(1)} %copy-done.62, ...), kind=kOutput, calls=%fused_computation.65 | convolution fusion | flops 245758000 | bytes 31870784 | tf_op jit(solution)/shard_map/dot_general | solution.py:34
  779.4 36.3 %attention_backward.1 = (bf16[1600,256]{1,0:T(8,128)(2,1)S(1)}, bf16[320,2048]{1,0:T(8,128)(2,1)}, bf16[320,2048]{1,0:T(8,128)(2,1)}, bf16[8,172,400]{2,1,0:T(8,...) custom-call(bf16[1600,256]{1,0:T(8,128)(2,1)S(1)} %copy-done.29, ...), custom_call_target="tpu_custom_call" | custom-call | flops 10485760000 | bytes 16777216 | tf_op jit(solution)/shard_map/attention_backward/pallas_call | solution.py:750
  820.8 17.4 %seq_scatter.1 = f32[80,2048]{1,0:T(8,128)S(1)} custom-call(bf16[8,80,2048]{2,1,0:T(8,128)(2,1)S(1)} %bitcast.194), custom_call_target="tpu_custom_call" | custom-call | tf_op jit(solution)/shard_map/seq_scatter/pallas_call | solution.py:588
  869.1 14.7 %convolution_convert_fusion.refs_0_ = bf16[1600,1080]{1,0:T(8,128)(2,1)} fusion(bf16[2048,1600]{1,0:T(8,128)(2,1)} %bitcast.215, bf16[2048,1080]{1,0:T(8,128)(2,1)} %concatenate.81.a_ref), kind=kOutput, calls=%fused_computation.12 | convolution fusion | flops 7079616000 | bytes 14433280 | tf_op jit(solution)/shard_map/dot_general | solution.py:34
  910.3 39.3 %product_scatter.5 = f32[256,1600]{1,0:T(8,128)S(1)} custom-call(bf16[2048,1080]{1,0:T(8,128)(2,1)} %concatenate.81.a_ref, bf16[1600,1080]{1,0:T(8,128)(2,1)S(1)} %copy-done.27, bf16[1600,1080]{1,0:T(8,128)(2,1)} %convolution_convert_fusion.refs_0_), custom_call_target="tpu_custom_call" | custom-call | flops 7077888000 | bytes 104857600 | tf_op jit(solution)/shard_map/product_scatter/pallas_call | solution.py:604
  952.1 15.6 %direct.18 = (bf16[4,58,400]{2,1,0:T(8,128)(2,1)S(1)}, f32[4,24,400]{2,1,0:T(8,128)S(1)}, f32[4,3,1600]{2,1,0:T(4,128)S(1)}) custom-call(bf16[4,58,400]{2,1,0:T(8,128)(2,1)S(1)} %pad_maximum_fusion.4.refs_0_, f32[24,400]{1,0:T(8,128)S(1)} %concatenate.83.refs_1_, f32[3,1600]{1,0:T(4,128)S(1)} %pad_maximum_fusion.5.refs_2_), custom_call_target="tpu_custom_call" | custom-call | tf_op jit(solution)/shard_map/direct/pallas_call | solution.py:559
  970.6 23.5 %direct.19 = (bf16[8,135,400]{2,1,0:T(8,128)(2,1)S(1)}, bf16[8,50,58]{2,1,0:T(8,128)(2,1)S(1)}, f32[8,24,400]{2,1,0:T(8,128)S(1)}, f32[8,3,1600]{2,1,0:T(4,128)S(1)}) custom-call(bf16[8,135,400]{2,1,0:T(8,128)(2,1)S(1)} %reshape.563.refs_0_, bf16[8,50,58]{2,1,0:T(8,128)(2,1)S(1)} %copy.177.refs_1_, f32[24,400]{1,0:T(8,128)S(1)} %reduce_sum.250.refs_2_, ...), custom_call_target="tpu_custom_call" | custom-call | tf_op jit(solution)/shard_map/direct/pallas_call | solution.py:559
  (418 shorter events, 353.8 us)
Async XLA Ops:
  7.2 105.2 %all-gather.9.cloned.1.call-start = ((), (), s32[]{:S(2)}) async-start(), calls=%async_computation.5 | async-start | bytes 4608000 | tf_op jit(solution)/shard_map/all_gather | solution.py:871
  7.3 200.6 %copy-start.67 = (s32[400]{0:T(512)}, s32[400]{0:T(512)S(1)}, u32[]{:S(2)}) copy-start(s32[400]{0:T(512)S(1)} %fusion.206) | copy-start | bytes 4804
  33.3 289.0 %all-gather.15.cloned.1.call-start = ((), (), s32[]{:S(2)}) async-start(), calls=%async_computation.12 | async-start | bytes 2529280 | tf_op jit(solution)/shard_map/all_gather | solution.py:873
  112.4 293.1 %all-gather.17.cloned.1.call-start = ((), (), s32[]{:S(2)}) async-start(), calls=%async_computation.13 | async-start | bytes 2928640 | tf_op jit(solution)/shard_map/all_gather | solution.py:874
  113.2 295.6 %all-gather.11.cloned.1.call-start = ((), (), s32[]{:S(2)}) async-start(), calls=%async_computation.6 | async-start | bytes 5632000 | tf_op jit(solution)/shard_map/all_gather | solution.py:955
  121.8 40.5 %copy-start.91 = (s32[640]{0:T(1024)}, s32[640]{0:T(1024)S(1)}, u32[]{:S(2)}) copy-start(s32[640]{0:T(1024)S(1)} %fusion.193) | copy-start | bytes 7684
  121.9 89.8 %copy-start.81 = (s32[1600]{0:T(1024)}, s32[1600]{0:T(1024)S(1)}, u32[]{:S(2)}) copy-start(s32[1600]{0:T(1024)S(1)} %fusion.136) | copy-start | bytes 19204
  122.3 43.9 %copy-start.18 = (f32[1280,256]{1,0:T(8,128)}, f32[1280,256]{1,0:T(8,128)S(1)}, u32[]{:S(2)}) copy-start(f32[1280,256]{1,0:T(8,128)S(1)} %fusion.70.refs_3_.refs_5_) | copy-start | bytes 3932164
  200.0 225.2 %all-gather.13.cloned.1.call-start = ((), (), s32[]{:S(2)}) async-start(), calls=%async_computation.11 | async-start | bytes 7372800 | tf_op jit(solution)/shard_map/all_gather | solution.py:1002
  200.6 322.4 %reduce-scatter.8.cloned.1.call-start = ((), (), s32[]{:S(2)}) async-start(), calls=%async_computation.7 | async-start | bytes 2928640 | tf_op jit(solution)/shard_map/reduce_scatter | solution.py:1015
  210.2 57.8 %copy-start.65 = (f32[400]{0:T(512)}, f32[400]{0:T(512)S(1)}, u32[]{:S(2)}) copy-start(f32[400]{0:T(512)S(1)} %add.570) | copy-start | bytes 4804
  210.8 57.2 %copy-start.50 = (bf16[100,400]{1,0:T(8,128)(2,1)}, bf16[100,400]{1,0:T(8,128)(2,1)S(1)}, u32[]{:S(2)}) copy-start(bf16[100,400]{1,0:T(8,128)(2,1)S(1)} %reshape.549) | copy-start | bytes 240004
  327.7 41.2 %copy-start.35 = (bf16[1,256,1600]{2,1,0:T(8,128)(2,1)S(1)}, bf16[1,256,1600]{2,1,0:T(8,128)(2,1)}, u32[]{:S(2)}) copy-start(bf16[1,256,1600]{2,1,0:T(8,128)(2,1)} %copy.145) | copy-start | bytes 2457604
  442.0 170.9 %reduce-scatter.16.cloned.1.call-start = ((), (), s32[]{:S(2)}) async-start(), calls=%async_computation.14 | async-start | bytes 2529280
  479.5 41.1 %copy-start.34 = (f32[256,1600]{1,0:T(8,128)S(1)}, f32[256,1600]{1,0:T(8,128)}, u32[]{:S(2)}) copy-start(f32[256,1600]{1,0:T(8,128)} %copy-done.33) | copy-start | bytes 4915204
  479.5 41.7 %copy-start.47 = (bf16[1,256,1600]{2,1,0:T(8,128)(2,1)S(1)}, bf16[1,256,1600]{2,1,0:T(8,128)(2,1)}, u32[]{:S(2)}) copy-start(bf16[1,256,1600]{2,1,0:T(8,128)(2,1)} %copy.164) | copy-start | bytes 2457604
  570.8 183.6 %reduce-scatter.12.cloned.1.call-start = ((), (), s32[]{:S(2)}) async-start(), calls=%async_computation.9 | async-start | bytes 5632000 | tf_op jit(solution)/shard_map/reduce_scatter | solution.py:1013
  571.5 272.9 %reduce-scatter.10.cloned.1.call-start = ((), (), s32[]{:S(2)}) async-start(), calls=%async_computation.8 | async-start | bytes 7667712 | tf_op jit(solution)/shard_map/reduce_scatter | solution.py:1037
  689.0 279.2 %reduce-scatter.14.cloned.1.call-start = ((), (), s32[]{:S(2)}) async-start(), calls=%async_computation.10 | async-start | bytes 4608000 | tf_op jit(solution)/shard_map/reduce_scatter | solution.py:1087
  910.3 39.4 %copy-start.57 = (f32[1600]{0:T(1024)S(1)}, f32[1600]{0:T(1024)}, u32[]{:S(2)}) copy-start(f32[1600]{0:T(1024)} %param.26) | copy-start | bytes 19204
  910.3 39.4 %copy-start.74 = (f32[256]{0:T(256)S(1)}, f32[256]{0:T(256)}, u32[]{:S(2)}) copy-start(f32[256]{0:T(256)} %copy-done.73) | copy-start | bytes 3076
  910.3 40.0 %copy-start.42 = (f32[256,1600]{1,0:T(8,128)S(1)}, f32[256,1600]{1,0:T(8,128)}, u32[]{:S(2)}) copy-start(f32[256,1600]{1,0:T(8,128)} %get-tuple-element.174) | copy-start | bytes 4915204
  910.3 40.0 %copy-start.93 = (f32[256]{0:T(256)S(1)}, f32[256]{0:T(256)}, u32[]{:S(2)}) copy-start(f32[256]{0:T(256)} %get-tuple-element.209) | copy-start | bytes 3076
  950.8 43.3 %copy-start.68 = (s32[400]{0:T(512)S(1)}, s32[400]{0:T(512)}, u32[]{:S(2)}) copy-start(s32[400]{0:T(512)} %copy-done.67) | copy-start | bytes 4804
  (83 other events, 1022.0 us)
Sparse Core Ops, SparseCore 0:
  33.4 78.9 all-gather.8
  114.0 43.0 all-gather.14
  159.2 49.0 all-gather.16
  210.3 84.7 all-gather.10
  296.8 50.5 all-gather.12
  442.1 48.0 reduce-scatter.7
  570.9 41.9 reduce-scatter.15
  615.2 82.2 reduce-scatter.11
  701.3 64.7 reduce-scatter.9
  883.9 69.2 reduce-scatter.13

commit v4 on v3

--- a/solution.py
+++ b/solution.py
@@ -304,7 +304,7 @@
     return ref.at[pl.ds(0, top)], ref.at[pl.ds(top, rows - top)]
 
 
-def gather_steps(out, sems, base, tile):
+def gather_steps(out, sems, base, tile, early=None, late=None, use=None):
     me, core, sib, step_x, step_y = places()
     at_x, at_y = me + step_x, me + step_y
     diag = me + step_x + step_y
@@ -316,19 +316,40 @@
 
     mine, from_x, from_y, far = (block_at(out, d) for d in (me, at_x, at_y, diag))
     own_x, own_y, own_s = send(mine, 0, at_x), send(mine, 1, at_y), send(mine, 2, sib)
+    if early is not None:
+        early()
+    if use is not None:
+        use(me)
+        own_s.wait_recv()
+        use(sib)
     own_x.wait_recv()
     on_y = send(halves(from_x, tile)[0], 3, at_y)
     pass_x = send(from_x, 5, sib)
     own_y.wait_recv()
     on_x = send(halves(from_y, tile)[1], 4, at_x)
     pass_y = send(from_y, 6, sib)
+    if late is not None:
+        late()
+    if use is not None:
+        use(at_x)
+        use(at_y)
+        pass_x.wait_recv()
+        use(sib + step_x)
+        pass_y.wait_recv()
+        use(sib + step_y)
     on_y.wait_recv()
     pass_top = send(halves(far, tile)[0], 7, sib)
     on_x.wait_recv()
     pass_low = send(halves(far, tile)[1], 8, sib)
-    for copy in (own_s, pass_x, pass_y, pass_top, pass_low):
-        copy.wait()
-    for copy in (own_x, own_y, on_x, on_y):
+    if use is None:
+        for copy in (own_s, pass_x, pass_y, pass_top, pass_low):
+            copy.wait_recv()
+    else:
+        use(diag)
+        pass_top.wait_recv()
+        pass_low.wait_recv()
+        use(sib + step_x + step_y)
+    for copy in (own_s, pass_x, pass_y, pass_top, pass_low, own_x, own_y, on_x, on_y):
         copy.wait_send()
 
 
@@ -340,6 +361,63 @@
     greet([sib, me + step_x, me + step_y])
     mine.wait()
     gather_steps(out_ref, sems, 0, 16)
+
+
+def gather_product_body(x_ref, w_ref, out_ref, y_ref, sems, local_sem):
+    me, core, sib, step_x, step_y = places()
+    rows, width = x_ref.shape[0], w_ref.shape[1]
+    mine = pltpu.make_async_copy(x_ref, out_ref.at[me], local_sem)
+    mine.start()
+    greet([sib, me + step_x, me + step_y])
+    mine.wait()
+
+    def use(d):
+        left = out_ref[d]
+        at = pl.ds(pl.multiple_of(d * rows, rows), rows)
+        for first in range(0, width, 512):
+            cols = slice(first, min(first + 512, width))
+            y_ref[at, cols] = matmul(left, w_ref[:, cols]).astype(bf16)
+
+    gather_steps(out_ref, sems, 0, 16, use=use)
+
+
+def column_products(out_ref, a_ref, b_ref):
+    count = a_ref.shape[1]
+
+    def step(i, _):
+        at = pl.ds(pl.multiple_of(i * 256, 256), 256)
+        out_ref[at, :] = dot_tn(a_ref[:, at], b_ref[...]).astype(bf16)
+        return 0
+
+    lax.fori_loop(0, count // 256, step, 0)
+    if count % 256:
+        at = pl.ds(count // 256 * 256, count % 256)
+        out_ref[at, :] = dot_tn(a_ref[:, at], b_ref[...]).astype(bf16)
+
+
+def gather_beside_body(x_ref, a1_ref, b1_ref, a2_ref, b2_ref, out_ref, p1_ref, p2_ref, *refs):
+    a1, b1, a2, b2, sems, local_sems = refs
+    me, core, sib, step_x, step_y = places()
+    mine = pltpu.make_async_copy(x_ref, out_ref.at[me], local_sems.at[4])
+    mine.start()
+    pairs = ((a1_ref, a1), (b1_ref, b1), (a2_ref, a2), (b2_ref, b2))
+    loads = [pltpu.make_async_copy(src, dst, local_sems.at[k]) for k, (src, dst) in enumerate(pairs)]
+    greet([sib, me + step_x, me + step_y])
+    mine.wait()
+
+    def early():
+        for load in loads:
+            load.start()
+        loads[0].wait()
+        loads[1].wait()
+        column_products(p1_ref, a1, b1)
+
+    def late():
+        loads[2].wait()
+        loads[3].wait()
+        column_products(p2_ref, a2, b2)
+
+    gather_steps(out_ref, sems, 0, 16, early, late)
 
 
 def add_rows(out, parts, rows):
@@ -394,11 +472,22 @@
         copy.wait_send()
 
 
-def product_scatter_body(transposed, a_ref, w_ref, *refs):
-    out_ref, stage, from_sib, acc, got_x, got_y, last_x, last_y, sems = refs[-9:]
+def product_scatter_body(transposed, axes, modes, sizes, a_ref, w_ref, *refs):
+    count = len(modes)
+    moved, out_ref, arrived, refs = refs[:count], refs[count], refs[count + 1 : 2 * count + 1], refs[2 * count + 1 :]
+    stage, from_sib, acc, got_x, got_y, last_x, last_y, sems = refs[:8]
+    plan = direct_copies(sizes, axes, modes, moved, arrived, *refs[8:]) if count else None
+    others = [(axis, d) for axis, devices in plan[0].items() for d in devices] if count else []
     me, core, sib, step_x, step_y = places()
     rows, width = out_ref.shape
-    greet([sib, me + step_x, me + step_y])
+    barrier = pltpu.get_barrier_semaphore()
+    others += [("seq", sib), ("seq", me + step_x), ("seq", me + step_y)]
+    for axis, d in others:
+        pl.semaphore_signal(barrier, inc=1, device_id={axis: d}, device_id_type=MESH)
+    pl.semaphore_wait(barrier, len(others))
+    if count:
+        for copy in plan[1] + plan[2]:
+            copy.start()
     dests = (me + step_x + step_y, me + step_x, me + step_y, me)
 
     def multiply(d, store):
@@ -465,6 +554,8 @@
     add_rows(out_low, [got_y.at[1], low, last_x], 16)
     for copy in pairs + out_x + out_y + [last_a, last_b]:
         copy.wait_send()
+    if count:
+        direct_wait(plan)
 
 
 def scatter_body(p_ref, *refs):
@@ -474,7 +565,8 @@
     scatter_steps(p_ref, out_ref, from_sib, acc, got_x, got_y, last_x, last_y, sems, 16)
 
 
-def sum_body(p_ref, out_ref, from_sib, acc, got_x, got_y, last_x, last_y, sems):
+def sum_body(p_ref, *refs):
+    out_ref, from_sib, acc, got_x, got_y, last_x, last_y, sems = refs[-8:]
     me, core, sib, step_x, step_y = places()
     greet([sib, me + step_x, me + step_y])
     scatter_steps(p_ref, block_at(out_ref, me), from_sib, acc, got_x, got_y, last_x, last_y, sems, 8)
@@ -538,6 +630,32 @@
     plan = direct_copies(sizes, axes, modes, ins, refs[:count], *refs[count:])
     direct_start(plan)
     direct_wait(plan)
+
+
+def gather_exchange_body(x_ref, e_ref, out_ref, e_out, sems, local_sem, *e_sems):
+    mine = pltpu.make_async_copy(x_ref, out_ref.at[lax.axis_index("seq")], local_sem)
+    mine.start()
+    others, own, copies = direct_copies({"seq": 8}, ("seq",), ("exchange",), [e_ref], [e_out], *e_sems)
+    greet(others["seq"])
+    mine.wait()
+
+    def early():
+        for copy in own + copies:
+            copy.start()
+
+    gather_steps(out_ref, sems, 0, 16, early)
+    for copy in own + copies:
+        copy.wait()
+
+
+def scatter_exchange_body(p_ref, e_ref, out_ref, e_out, *refs):
+    others, own, copies = direct_copies({"seq": 8}, ("seq",), ("exchange",), [e_ref], [e_out], *refs[7:])
+    greet(others["seq"])
+    for copy in own + copies:
+        copy.start()
+    scatter_steps(p_ref, out_ref, *refs[:7], 16)
+    for copy in own + copies:
+        copy.wait()
 
 
 any_space = pl.BlockSpec(memory_space=pl.ANY)
@@ -581,6 +699,88 @@
     )(block, *after)
 
 
+def gather_exchange(n, block, blocks, collective_id):
+    if n != 8:
+        return seq_gather(n, block, None), exchange(n, blocks, None)
+    return pl.pallas_call(
+        gather_exchange_body,
+        out_shape=[
+            jax.ShapeDtypeStruct((8,) + block.shape, block.dtype),
+            jax.ShapeDtypeStruct(blocks.shape, blocks.dtype),
+        ],
+        in_specs=[any_space, any_space],
+        out_specs=[any_space, any_space],
+        scratch_shapes=[pltpu.SemaphoreType.DMA((2, 9)), pltpu.SemaphoreType.DMA]
+        + direct_scratch({"seq": 8}, ("seq",)),
+        compiler_params=comm_params(collective_id),
+        name="gather_exchange",
+    )(block, blocks)
+
+
+def scatter_exchange(n, parts, blocks, collective_id):
+    if n != 8:
+        return seq_scatter(n, parts, None), exchange(n, blocks, None)
+    _, rows, width = parts.shape
+    return pl.pallas_call(
+        scatter_exchange_body,
+        out_shape=[jax.ShapeDtypeStruct((rows, width), f32), jax.ShapeDtypeStruct(blocks.shape, blocks.dtype)],
+        in_specs=[vmem_space, any_space],
+        out_specs=[vmem_space, any_space],
+        scratch_shapes=scatter_scratch(rows, width, parts.dtype, 16)
+        + [pltpu.SemaphoreType.DMA((2, 10))]
+        + direct_scratch({"seq": 8}, ("seq",)),
+        compiler_params=comm_params(collective_id),
+        name="scatter_exchange",
+    )(parts, blocks)
+
+
+def exchange_token_sum(n, blocks, value, collective_id, after=()):
+    if n != 8:
+        return exchange(n, blocks, None), lax.psum(value, "seq")
+    arrays = [(blocks, "seq", "exchange"), (value.reshape(-1, 128), "seq", "gather")]
+    moved, got = direct({"seq": n}, arrays, collective_id, after)
+    return moved, jnp.sum(got, 0).reshape(-1)
+
+
+def gather_product(n, block, w, collective_id):
+    if n != 8:
+        full = lax.all_gather(block, "seq", axis=0, tiled=True)
+        return full, matmul(full, w).astype(bf16)
+    rows = 8 * block.shape[0]
+    full, product = pl.pallas_call(
+        gather_product_body,
+        out_shape=[
+            jax.ShapeDtypeStruct((8,) + block.shape, bf16),
+            jax.ShapeDtypeStruct((rows, w.shape[1]), bf16),
+        ],
+        in_specs=[vmem_space, vmem_space],
+        out_specs=[vmem_space, vmem_space],
+        scratch_shapes=[pltpu.SemaphoreType.DMA((2, 9)), pltpu.SemaphoreType.DMA],
+        compiler_params=comm_params(collective_id),
+        name="gather_product",
+    )(block, w)
+    return full.reshape(rows, -1), product
+
+
+def gather_beside(n, block, first, second, collective_id):
+    if n != 8:
+        full = lax.all_gather(block, "seq", axis=0, tiled=True)
+        return full, dot_tn(*first).astype(bf16), dot_tn(*second).astype(bf16)
+    operands = first + second
+    full, one, two = pl.pallas_call(
+        gather_beside_body,
+        out_shape=[jax.ShapeDtypeStruct((8,) + block.shape, bf16)]
+        + [jax.ShapeDtypeStruct((a.shape[1], b.shape[1]), bf16) for a, b in (first, second)],
+        in_specs=[any_space] * 5,
+        out_specs=[any_space, vmem_space, vmem_space],
+        scratch_shapes=[pltpu.VMEM(x.shape, bf16) for x in operands]
+        + [pltpu.SemaphoreType.DMA((2, 9)), pltpu.SemaphoreType.DMA((5,))],
+        compiler_params=comm_params(collective_id),
+        name="gather_beside",
+    )(block, *operands)
+    return full.reshape(8 * block.shape[0], -1), one, two
+
+
 def seq_scatter(n, parts, collective_id, after=()):
     if n != 8:
         return lax.psum_scatter(parts, "seq", scatter_dimension=0, tiled=False).astype(f32)
@@ -596,47 +796,48 @@
     )(parts, *after)
 
 
-def product_scatter(n, a, w, transposed, collective_id, after=()):
+def product_scatter(n, a, w, transposed, collective_id, sizes=None, arrays=()):
     if n != 8:
         product = (dot_nt if transposed else matmul)(a, w).astype(bf16)
-        return lax.psum_scatter(product, "seq", scatter_dimension=0, tiled=True).astype(f32)
+        product = lax.psum_scatter(product, "seq", scatter_dimension=0, tiled=True).astype(f32)
+        return [product] + (list(direct(sizes, arrays, collective_id)) if arrays else [])
     rows, width = a.shape[0] // 8, w.shape[0 if transposed else 1]
+    moved = [x for x, _, _ in arrays]
+    axes = [axis for _, axis, _ in arrays]
+    modes = [mode for _, _, mode in arrays]
+    sizes = {axis: sizes[axis] for axis in sorted(set(axes))}
+    shapes = [x.shape if mode == "exchange" else (sizes[axis],) + x.shape for x, axis, mode in arrays]
     return pl.pallas_call(
-        functools.partial(product_scatter_body, transposed),
-        out_shape=jax.ShapeDtypeStruct((rows, width), f32),
-        in_specs=[vmem_space, vmem_space] + [any_space] * len(after),
-        out_specs=vmem_space,
+        functools.partial(product_scatter_body, transposed, axes, modes, sizes),
+        out_shape=[jax.ShapeDtypeStruct((rows, width), f32)]
+        + [jax.ShapeDtypeStruct(shape, x.dtype) for shape, x in zip(shapes, moved)],
+        in_specs=[vmem_space, vmem_space] + [any_space] * len(moved),
+        out_specs=[vmem_space] + [any_space] * len(moved),
         scratch_shapes=[pltpu.VMEM((4, rows, width), bf16)]
         + scatter_scratch(rows, width, bf16, 16)
-        + [pltpu.SemaphoreType.DMA((2, 10))],
+        + [pltpu.SemaphoreType.DMA((2, 10))]
+        + (direct_scratch(sizes, axes) if moved else []),
         compiler_params=comm_params(collective_id),
         cost_estimate=pl.CostEstimate(
             flops=2 * a.shape[0] * a.shape[1] * width, bytes_accessed=100 << 20, transcendentals=0
         ),
         name="product_scatter",
-    )(a, w, *after)
-
-
-def seq_sum(n, parts, collective_id):
+    )(a, w, *moved)
+
+
+def seq_sum(n, parts, collective_id, after=()):
     if n != 8:
         return lax.psum(parts, "seq")
     rows, length = parts.shape
     return pl.pallas_call(
         sum_body,
         out_shape=jax.ShapeDtypeStruct(parts.shape, f32),
-        in_specs=[vmem_space],
+        in_specs=[vmem_space] + [any_space] * len(after),
         out_specs=vmem_space,
         scratch_shapes=scatter_scratch(rows, length // 8, f32, 8) + [pltpu.SemaphoreType.DMA((2, 19))],
         compiler_params=comm_params(collective_id),
         name="seq_sum",
-    )(parts)
-
-
-def seq_token_sum(n, value, collective_id):
-    if n != 8:
-        return lax.psum(value, "seq")
-    (got,) = direct({"seq": n}, [(value.reshape(-1, 128), "seq", "gather")], collective_id)
-    return jnp.sum(got, 0).reshape(-1)
+    )(parts, *after)
 
 
 def exchange(n, blocks, collective_id, after=()):
@@ -932,8 +1133,8 @@
     gate_z = branch[:, c_own:].astype(f32)
 
     q_blocks = qkv_t[:q_own].reshape(q_own, n, local).transpose(1, 0, 2)
-    q_t = heads_in(exchange(n, q_blocks, 4)) * bf16(HEAD_SIZE**-0.5)
-    kv_all = seq_gather(n, qkv_t[q_own:], 5)
+    kv_all, q_blocks = gather_exchange(n, qkv_t[q_own:], q_blocks, 4)
+    q_t = heads_in(q_blocks) * bf16(HEAD_SIZE**-0.5)
     reach = (WINDOW_TOKENS + local - 2) // local
     span = min((reach + 1) * local, length)
     first_key = jnp.clip((me - reach) * local, 0, length - span)
@@ -955,7 +1156,6 @@
         gu_full = lax.all_gather(moved[0].reshape(-1, z_rows).T, "fsdp", axis=0, tiled=True)
     attn_scale = lax.rsqrt(jnp.mean(attended * attended, axis=0, keepdims=True) + norm_eps)
     attn_normed = (attended * attn_scale * attn_gain[:, None]).astype(bf16)
-    attn_c = exchange(n, heads_out(attn_normed), 6).transpose(0, 2, 1).reshape(length, q_own)
 
     padded_inputs = jnp.pad(inputs, ((KC - 1, 0), (0, 0)))
     padded_ids = jnp.pad(ids, (KC - 1, 0), constant_values=-1)
@@ -983,15 +1183,15 @@
     mamba_pre = scan_out + skip_g * activated
     gate_sig = jax.nn.sigmoid(gate_z)
     mamba_out = mamba_pre * gate_z * gate_sig
-    square_sum = seq_token_sum(n, jnp.sum(mamba_out * mamba_out, -1), 8)
+    attn_c, square_sum = exchange_token_sum(n, heads_out(attn_normed), jnp.sum(mamba_out * mamba_out, -1), 6)
+    attn_c = attn_c.transpose(0, 2, 1).reshape(length, q_own)
     mamba_scale = lax.rsqrt(square_sum / DI + norm_eps)[:, None]
     mamba_normed = mamba_out * mamba_scale * mamba_g
     joined = jnp.concatenate([attn_c, mamba_normed.astype(bf16)], 1)
-    mixed = product_scatter(n, joined, out_full, False, 9)
+    (mixed,) = product_scatter(n, joined, out_full, False, 9)
     hidden = seq_x + 0.5 * mixed
     normed_two, scale_two = rms_norm(hidden, second_gain)
-    normed_two = seq_gather(n, normed_two.astype(bf16), 10).reshape(length, width)
-    gate_up_out = matmul(normed_two, gu_full).astype(bf16)
+    normed_two, gate_up_out = gather_product(n, normed_two.astype(bf16), gu_full, 10)
     gate_part = gate_up_out[:, :f_own].astype(f32)
     up_part = gate_up_out[:, f_own:].astype(f32)
     gate_act = jax.nn.sigmoid(gate_part)
@@ -1000,7 +1200,6 @@
 
     own_d_out = cotangent[0] if fast else lax.optimization_barrier((cotangent[0], inner))[0]
     d_ffn = lax.all_gather(own_d_out, "seq", axis=0, tiled=True)
-    down_term = dot_tn(inner, d_ffn).astype(bf16)
     d_inner = dot_nt(d_ffn, down_full)
     d_gate_up = jnp.concatenate(
         [
@@ -1009,14 +1208,15 @@
         ],
         1,
     ).astype(bf16)
-    gate_up_term = dot_tn(normed_two, d_gate_up).astype(bf16)
+    (d_normed_two,) = product_scatter(n, d_gate_up, gu_full, True, 13)
+    d_hidden_part, second_grad = norm_back(hidden, scale_two, second_gain, d_normed_two)
+    d_hidden = cotangent[0].astype(f32) + d_hidden_part
+    d_mixed, down_term, gate_up_term = gather_beside(
+        n, d_hidden.astype(bf16), (inner, d_ffn), (normed_two, d_gate_up), 14
+    )
     gu_part = lax.psum_scatter(gate_up_term, "fsdp", scatter_dimension=0, tiled=True)
     if fast:
         down_part = lax.psum_scatter(down_term.reshape(m, -1, width), "fsdp", scatter_dimension=0, tiled=False)
-    d_normed_two = product_scatter(n, d_gate_up, gu_full, True, 13, (down_term, gate_up_term))
-    d_hidden_part, second_grad = norm_back(hidden, scale_two, second_gain, d_normed_two)
-    d_hidden = cotangent[0].astype(f32) + d_hidden_part
-    d_mixed = seq_gather(n, d_hidden.astype(bf16), 14, (down_part,) if fast else ()).reshape(length, width)
     out_term = (0.5 * dot_tn(joined, d_mixed)).astype(bf16)
     if fast:
         out_part = lax.psum_scatter(out_term.reshape(m, -1, width), "fsdp", scatter_dimension=0, tiled=False)
@@ -1024,37 +1224,19 @@
 
     u = d_joined[:, q_own:]
     weighted = u * mamba_g
-    inner_mean = seq_token_sum(n, jnp.sum(weighted * mamba_out, -1), 18)[:, None] / DI
+    d_attn = d_joined[:, :q_own].astype(bf16).reshape(n, local, q_own).transpose(0, 2, 1)
+    d_attn, inner_mean = exchange_token_sum(n, d_attn, jnp.sum(weighted * mamba_out, -1), 15)
+    inner_mean = inner_mean[:, None] / DI
     mamba_grad = jnp.sum(u * mamba_out * mamba_scale, 0)
     d_mamba = mamba_scale * weighted - mamba_out * (mamba_scale * mamba_scale * mamba_scale) * inner_mean
     d_pre = d_mamba * gate_z * gate_sig
     d_gate = d_mamba * mamba_pre * gate_sig * (1.0 + gate_z * (1.0 - gate_sig))
     skip_grad = jnp.sum(d_pre * activated, 0)
+    ffn, d_pre = lax.optimization_barrier((ffn, d_pre))
+    ffn = lax.psum_scatter(ffn, "seq", scatter_dimension=0, tiled=True)
     by_rate, pushed, db_t, dc_t, decay_log_grad = scan_backward(
-        step_keep, push, d_pre, b_t, c_t, states, rate, (out_part,) if fast else ()
-    )
-    ffn, db_t = lax.optimization_barrier((ffn, db_t))
-    ffn = lax.psum_scatter(ffn, "seq", scatter_dimension=0, tiled=True)
-    out_tokens = (hidden + ffn.astype(f32)).astype(bf16)
-
-    d_attn = d_joined[:, :q_own].astype(bf16).reshape(n, local, q_own).transpose(0, 2, 1)
-    d_attn = heads_in(exchange(n, d_attn, 15, (gu_part,))).astype(f32)
-    weighted_a = d_attn * attn_gain[:, None]
-    attn_grad = jnp.sum(d_attn * attended * attn_scale, 1)
-    mean_a = jnp.mean(weighted_a * attended, axis=0, keepdims=True)
-    d_attended = attn_scale * weighted_a - attended * (attn_scale * attn_scale * attn_scale) * mean_a
-    moved = []
-    if fast:
-        out_blocks = out_part.reshape(-1, n, width // n).transpose(1, 0, 2)
-        down_blocks = down_part.reshape(-1, n, width // n).transpose(1, 0, 2)
-        gu_blocks = gu_part.T.reshape(n, -1, z_rows)
-        moved = [gu_blocks, out_blocks, down_blocks]
-    dq_t, dk_t, dv_t, *moved = attention_backward(
-        q_t, kv_t, d_attended.astype(bf16), lse, bias, moved, 24
-    )
-    d_queries = exchange(n, heads_out(dq_t), 16, (out_tokens,)).transpose(0, 2, 1).reshape(length, q_own)
-    dkv = exact(deal_kv, jnp.concatenate([dk_t, dv_t], 0), ((0,), (0,))).astype(bf16).reshape(n, 2 * k_own, length)
-    dkv = seq_scatter(n, dkv, 17).astype(bf16).T
+        step_keep, push, d_pre, b_t, c_t, states, rate
+    )
 
     step_grads = by_rate + pushed * activated
     d_step_pre = step_grads * jax.nn.sigmoid(step_pre)
@@ -1077,13 +1259,29 @@
         masked_grad = d_conv * same_masks[tap]
         conv_rows.append(jnp.sum(masked_grad * padded_inputs[begin : begin + length], 0))
         ext_grad = ext_grad + jnp.pad(conv_w[tap] * masked_grad, ((begin, tap), (0, 0)))
-    d_inputs = ext_grad[KC - 1 :]
-    d_projected = jnp.concatenate([d_queries, dkv, d_inputs.astype(bf16), d_gate.astype(bf16)], 1)
+    d_inputs = ext_grad[KC - 1 :].astype(bf16)
+    d_attn, d_inputs, ffn = lax.optimization_barrier((d_attn, d_inputs, ffn))
+    out_tokens = (hidden + ffn.astype(f32)).astype(bf16)
+    d_attn = heads_in(d_attn).astype(f32)
+    weighted_a = d_attn * attn_gain[:, None]
+    attn_grad = jnp.sum(d_attn * attended * attn_scale, 1)
+    mean_a = jnp.mean(weighted_a * attended, axis=0, keepdims=True)
+    d_attended = attn_scale * weighted_a - attended * (attn_scale * attn_scale * attn_scale) * mean_a
+    moved = []
+    if fast:
+        down_blocks = down_part.reshape(-1, n, width // n).transpose(1, 0, 2)
+        gu_blocks = gu_part.T.reshape(n, -1, z_rows)
+        moved = [gu_blocks, down_blocks]
+    dq_t, dk_t, dv_t, *moved = attention_backward(
+        q_t, kv_t, d_attended.astype(bf16), lse, bias, moved, 24
+    )
+    dkv = exact(deal_kv, jnp.concatenate([dk_t, dv_t], 0), ((0,), (0,))).astype(bf16).reshape(n, 2 * k_own, length)
+    dkv, d_queries = scatter_exchange(n, dkv, heads_out(dq_t), 16)
+    dkv = dkv.astype(bf16).T
+    d_queries = d_queries.transpose(0, 2, 1).reshape(length, q_own)
+
+    d_projected = jnp.concatenate([d_queries, dkv, d_inputs, d_gate.astype(bf16)], 1)
     in_term = dot_tn(normed_one, d_projected).astype(bf16)
-    d_normed_one = product_scatter(n, d_projected, in_full, True, 20, (in_term,))
-    d_x_part, first_grad = norm_back(seq_x, scale_one, first_gain, d_normed_one)
-    tokens_grad = (d_hidden + d_x_part).astype(bf16)
-
     in_part = lax.psum_scatter(in_term, "fsdp", scatter_dimension=0, tiled=True)
     small_term = jnp.concatenate(
         [select_term.reshape(m, sel_rows, c_own), step_term.reshape(m, -1, c_own)], 1
@@ -1095,26 +1293,34 @@
         ],
         0,
     )
-    wide_grads = jnp.stack([first_grad, second_grad, attn_grad])
+    wide_grads = jnp.stack([second_grad, attn_grad])
     small_specs = [(small_term, "fsdp", "exchange"), (channel, "fsdp", "gather"), (wide_grads, "fsdp", "gather")]
     if fast:
-        gu_blocks, out_blocks, down_blocks = moved
-    small_z, channel_z, wide_z = direct(sizes, small_specs, 21)
+        gu_blocks, down_blocks = moved
+        out_blocks = out_part.reshape(-1, n, width // n).transpose(1, 0, 2)
+        small_specs.append((out_blocks, "seq", "exchange"))
+    d_normed_one, small_z, channel_z, wide_z, *moved = product_scatter(
+        n, d_projected, in_full, True, 20, sizes, small_specs
+    )
+    if fast:
+        (out_blocks,) = moved
+    d_x_part, first_grad = norm_back(seq_x, scale_one, first_gain, d_normed_one)
+    (first_z,) = direct(sizes, [(first_grad[None], "fsdp", "gather")], 25)
+    tokens_grad = (d_hidden + d_x_part).astype(bf16)
+
     small_part = jnp.sum(small_z.astype(f32), 0)
-    channel, wide_grads = jnp.sum(channel_z, 0), jnp.sum(wide_z, 0)
+    channel, wide_grads = jnp.sum(channel_z, 0), jnp.concatenate([jnp.sum(first_z, 0), jnp.sum(wide_z, 0)], 0)
     if fast:
         gu_sum = gu_blocks.reshape(-1, z_rows).T.astype(f32)
         out_sum = exact(deal_out, out_blocks.reshape(-1, width // n), ((1,), (0,)))
         down_sum = down_blocks.reshape(-1, width // n).astype(f32)
         small_blocks = small_part.astype(bf16).T.reshape(n, c_own // n, -1)
-        in_blocks, small_blocks, channel_all, wide_all = direct(
+        small_blocks, channel_all, wide_all = direct(
             sizes,
-            [
-                (in_part.T.reshape(n, -1, z_rows), "seq", "exchange"), (small_blocks, "seq", "exchange"),
-                (channel, "seq", "gather"), (wide_grads, "seq", "gather"),
-            ],
+            [(small_blocks, "seq", "exchange"), (channel, "seq", "gather"), (wide_grads, "seq", "gather")],
             22,
         )
+        (in_blocks,) = direct(sizes, [(in_part.T.reshape(n, -1, z_rows), "seq", "exchange")], 21, (wide_all,))
         small_sum = exact(small_blocks.reshape(c_own, -1), deal_small, ((0,), (1,)))
         channel_rows = channel.shape[0]
         channel = channel_all.reshape(n, channel_rows, n, c_own // n).transpose(1, 2, 0, 3).reshape(-1, c_own)

time: 1020 us -> 961 us (0.942)
  matrix products: 191 us -> 141 us
  local copies, waits for them, and re-layouts: 127 us -> 114 us
    pallas_call x4 -> x7, Pallas kernels: 139 us -> 265 us  [the longest x3 138 us: product_scatter(): pl.pallas_call(functools.partial(product_scatter_body, transposed, axes,...]
    pallas_call x4 -> x1, Pallas kernels: 124 us -> 35.7 us  [seq_gather(): pl.pallas_call(gather_body, out_shape=jax.ShapeDtypeStruct((8,) + block.s...]
    pallas_call x10 -> x7, Pallas kernels: 133 us -> 99.3 us  [direct(): pl.pallas_call(functools.partial(direct_body, sizes, axes, modes, len(aft...]
    dot_general x6 -> x4, matrix products: 78.6 us -> 50.3 us  [dot_tn(): lax.dot_general(left, right, (((0,), (0,)), ((), ())), preferred_element_...]
    dot_general x5 -> x4, matrix products: 45.2 us -> 25.7 us  [matmul(): return jnp.dot(left, right, preferred_element_type=f32)]
    unnamed x205 -> x191, local copies, waits for them, and re-layouts: 36.6 us -> 30.5 us
  transfers between devices with their start and end apart: 10 -> 10, of which waited for: 2 -> 1; matrix products, arithmetic and copies ran while one was open for 28% -> 28% of each run, Pallas kernels for 51% -> 52%
where the time goes in v4:
time: 961 us; the launch traced here: 951 us
  Pallas kernels  608 us (63%)
  matrix products  141 us (15%)
  local copies, waits for them, and re-layouts  114 us (12%)
  other arithmetic  62.7 us (7%)
  between operations  16.3 us (2%)
    pallas_call x3, Pallas kernels, product_scatter(): pl.pallas_call(functools.partial(product_scatter_body, transposed, axes,...  138 us
    pallas_call x7, Pallas kernels, direct(): pl.pallas_call(functools.partial(direct_body, sizes, axes, modes, len(aft...  99.3 us
    pallas_call x1, Pallas kernels, scan_backward(): pl.pallas_call(scan_bwd_body, grid=(tokens // block,), in_specs=[rows, ro...  71.3 us
    pallas_call x2, Pallas kernels, attention_call(): pl.pallas_call(with_exchange(body, count, len(in_specs), len(out_specs)),...  63.9 us
    dot_general x4, matrix products, dot_tn(): lax.dot_general(left, right, (((0,), (0,)), ((), ())), preferred_element_...  50.3 us
    dot_general x15, matrix products, exact(): lax.dot_general(left, right, (contract, ((), ())), precision=precision, p...  40.6 us
    pallas_call x1, Pallas kernels, gather_product(): pl.pallas_call(gather_product_body, out_shape=[jax.ShapeDtypeStruct((8,)...  39.5 us
    pallas_call x2, Pallas kernels, seq_sum(): pl.pallas_call(sum_body, out_shape=jax.ShapeDtypeStruct(parts.shape, f32)...  39 us
  transfers between devices with their start and end apart: 10, of which 1 were waited for; matrix products, arithmetic and copies ran while one was open for 28% of the time, Pallas kernels for 52%

profile of v4, /device:TPU:0, one launch (start us, length us, event | category | flops | bytes accessed | tf_op | source)
XLA Modules:
  0.0 950.9 jit_solution(8418639615978603888)
XLA Ops:
  11.7 19.4 %direct.7 = (bf16[8,135,400]{2,1,0:T(8,128)(2,1)S(1)}, bf16[8,50,58]{2,1,0:T(8,128)(2,1)S(1)}, s32[8,2,128]{2,1,0:T(2,128)S(1)}) custom-call(bf16[8,135,400]{2,1,0:T(8,128)(2,1)S(1)} %reshape.532.refs_0_, bf16[8,50,58]{2,1,0:T(8,128)(2,1)S(1)} %copy.143.refs_1_, s32[2,128]{1,0:T(2,128)S(1)} %bitcast.198), custom_call_target="tpu_custom_call" | custom-call | tf_op jit(solution)/shard_map/direct/pallas_call | solution.py:677
  47.2 35.7 %seq_gather.1.refs_3_ = bf16[8,256,1600]{2,1,0:T(8,128)(2,1)} custom-call(bf16[256,1600]{1,0:T(8,128)(2,1)S(1)} %fusion.53.x_ref, bf16[8,135,400]{2,1,0:T(8,128)(2,1)S(1)} %get-tuple-element.67.refs_0_), custom_call_target="tpu_custom_call" | custom-call | tf_op jit(solution)/shard_map/seq_gather/pallas_call | solution.py:691
  82.9 19.2 %direct.8 = (bf16[8,150,200]{2,1,0:T(8,128)(2,1)S(1)}, bf16[8,172,200]{2,1,0:T(8,128)(2,1)S(1)}, bf16[4,58,400]{2,1,0:T(8,128)(2,1)S(1)}) custom-call(bf16[8,150,200]{2,1,0:T(8,128)(2,1)S(1)} %reshape.536.refs_0_, bf16[8,172,200]{2,1,0:T(8,128)(2,1)S(1)} %copy.147.refs_1_, bf16[58,400]{1,0:T(8,128)(2,1)S(1)} %bitcast.192, ...), custom_call_target="tpu_custom_call" | custom-call | tf_op jit(solution)/shard_map/direct/pallas_call | solution.py:677
  128.0 25.8 %gather_exchange.1 = (bf16[8,80,2048]{2,1,0:T(8,128)(2,1)S(1)}, bf16[8,200,256]{2,1,0:T(8,128)(2,1)S(1)}) custom-call(bf16[80,2048]{1,0:T(8,128)(2,1)S(1)} %slice.221.x_ref, bf16[8,200,256]{2,1,0:T(8,128)(2,1)S(1)} %bitcast.182), custom_call_target="tpu_custom_call" | custom-call | tf_op jit(solution)/shard_map/gather_exchange/pallas_call | solution.py:705
  159.7 29.5 %attention_forward.1 = (f32[1600,256]{1,0:T(8,128)}, f32[5,8,256]{2,1,0:T(8,128)S(1)}, bf16[8,172,400]{2,1,0:T(8,128)(2,1)S(1)}) custom-call(bf16[1600,256]{1,0:T(8,128)(2,1)S(1)} %fusion.48.refs_0_, bf16[640,2048]{1,0:T(8,128)(2,1)} %convolution_convert_fusion.4.refs_1_.refs_2_, bf16[640,2048]{1,0:T(8,128)(2,1)} %convolution_convert_fusion.4.refs_1_.refs_2_, ...), custom_call_target="tpu_custom_call" | custom-call | flops 4194304000 | bytes 8388608 | tf_op jit(solution)/shard_map/attention_forward/pallas_call | solution.py:951
  216.1 19.5 %seq_sum.2 = f32[136,2048]{1,0:T(8,128)S(1)} custom-call(f32[136,2048]{1,0:T(8,128)S(1)} %fusion.86.p_ref), custom_call_target="tpu_custom_call" | custom-call | tf_op jit(solution)/shard_map/seq_sum/pallas_call | solution.py:832
  243.8 33.8 %scan_forward.1 = (f32[2048,400]{1,0:T(8,128)S(1)}, bf16[2048,16,400]{2,1,0:T(8,128)(2,1)}) custom-call(f32[2048,400]{1,0:T(8,128)S(1)} %get-tuple-element.221.step_ref, f32[2048,400]{1,0:T(8,128)} %get-tuple-element.220.push_ref, f32[2048,32]{1,0:T(8,128)S(1)} %bitcast.177, f32[2048,32]{1,0:T(8,128)S(1)} %bitcast.179, f32[16,400]{1,0:T(8,128)S(1)} %neg.26.rate_ref, ...), custom_call_target="tpu_custom_call" | custom-call | flops 104857600 | bytes 52428800 | tf_op jit(solution)/shard_map/scan_forward/pallas_call | solution.py:202
  286.4 13.6 %direct.9 = (bf16[8,200,256]{2,1,0:T(8,128)(2,1)S(1)}, f32[8,16,128]{2,1,0:T(8,128)S(1)}) custom-call(bf16[8,200,256]{2,1,0:T(8,128)(2,1)S(1)} %bitcast.186, f32[16,128]{1,0:T(8,128)S(1)} %bitcast.196), custom_call_target="tpu_custom_call" | custom-call | tf_op jit(solution)/shard_map/direct/pallas_call | solution.py:677
  312.5 55.0 %product_scatter.3 = f32[256,1600]{1,0:T(8,128)S(1)} custom-call(bf16[2048,600]{1,0:T(8,128)(2,1)} %pad_maximum_fusion.1.a_ref, bf16[600,1600]{1,0:T(8,128)(2,1)S(1)} %copy-done.11), custom_call_target="tpu_custom_call" | custom-call | flops 3932160000 | bytes 104857600 | tf_op jit(solution)/shard_map/product_scatter/pallas_call | solution.py:810
  374.8 39.5 %gather_product.1 = (bf16[8,256,1600]{2,1,0:T(8,128)(2,1)}, bf16[2048,1376]{1,0:T(8,128)(2,1)}) custom-call(bf16[256,1600]{1,0:T(8,128)(2,1)S(1)} %multiply_convert_fusion.3.x_ref, bf16[1600,1376]{1,0:T(8,128)(2,1)S(1)} %copy-done.6), custom_call_target="tpu_custom_call" | custom-call | tf_op jit(solution)/shard_map/gather_product/pallas_call | solution.py:750
  414.4 13.9 %fusion.6 = (bf16[2048,688]{1,0:T(8,128)(2,1)S(1)}, bf16[2048,688]{1,0:T(8,128)(2,1)S(1)}, bf16[2048,688]{1,0:T(8,128)(2,1)}) fusion(bf16[2048,1376]{1,0:T(8,128)(2,1)} %get-tuple-element.83, bf16[688,1600]{1,0:T(8,128)(2,1)} %reshape.581, bf16[1,2048,1600]{2,1,0:T(8,128)(2,1)} %all-gather.13.cloned.1.call-done), kind=kOutput, calls=%fused_computation.24 | convolution fusion | flops 4534239232 | bytes 22845440 | tf_op jit(solution)/shard_map/dot_general | solution.py:38
  432.7 39.8 %product_scatter.4 = f32[256,1600]{1,0:T(8,128)S(1)} custom-call(bf16[2048,1376]{1,0:T(8,128)(2,1)} %pad_maximum_fusion.a_ref.b2_ref, bf16[1600,1376]{1,0:T(8,128)(2,1)S(1)} %bitcast.176), custom_call_target="tpu_custom_call" | custom-call | flops 9017753600 | bytes 104857600 | tf_op jit(solution)/shard_map/product_scatter/pallas_call | solution.py:810
  475.4 37.7 %gather_beside.1 = (bf16[8,256,1600]{2,1,0:T(8,128)(2,1)}, bf16[688,1600]{1,0:T(8,128)(2,1)S(1)}, bf16[1600,1376]{1,0:T(8,128)(2,1)}) custom-call(bf16[256,1600]{1,0:T(8,128)(2,1)S(1)} %get-tuple-element.205.x_ref, bf16[2048,688]{1,0:T(8,128)(2,1)} %get-tuple-element.216.a1_ref, bf16[2048,1600]{1,0:T(8,128)(2,1)} %bitcast.206, bf16[2048,1600]{1,0:T(8,128)(2,1)} %bitcast.207, ...), custom_call_target="tpu_custom_call" | custom-call | tf_op jit(solution)/shard_map/gather_beside/pallas_call | solution.py:770
  534.5 13.7 %direct.10 = (bf16[8,200,256]{2,1,0:T(8,128)(2,1)S(1)}, f32[8,16,128]{2,1,0:T(8,128)S(1)}) custom-call(bf16[8,200,256]{2,1,0:T(8,128)(2,1)S(1)} %bitcast.181, f32[16,128]{1,0:T(8,128)S(1)} %bitcast.197), custom_call_target="tpu_custom_call" | custom-call | tf_op jit(solution)/shard_map/direct/pallas_call | solution.py:677
  559.1 11.5 %fusion.25 = (f32[400]{0:T(512)S(1)}, f32[2048,400]{1,0:T(8,128)}, bf16[2048,400]{1,0:T(8,128)(2,1)}) fusion(bf16[2048,400]{1,0:T(8,128)(2,1)} %copy-done.24, bf16[2048,800]{1,0:T(8,128)(2,1)} %copy-done.35, f32[2048]{0:T(1024)S(1)} %multiply_bitcast_fusion, f32[2048,400]{1,0:T(8,128)} %get-tuple-element.210, f32[2048]{0:T(1024)S(1)} %multiply_multiply_fusion.3, ...), kind=kLoop, calls=%fused_computation.46 | loop fusion | flops 18841200 | bytes 18051776 | tf_op jit(solution)/shard_map/reduce_sum | solution.py:1234
  584.7 71.3 %scan_backward.1 = (f32[2048,400]{1,0:T(8,128)S(1)}, f32[2048,400]{1,0:T(8,128)S(1)}, f32[16,2048]{1,0:T(8,128)S(1)}, f32[16,2048]{1,0:T(8,128)S(1)}, f32[16,400]{1,0:T(8,128)S(1)}) custom-call(f32[2048,400]{1,0:T(8,128)} %copy-done.2, f32[2048,400]{1,0:T(8,128)} %get-tuple-element.220.push_ref, f32[2048,400]{1,0:T(8,128)} %get-tuple-element.88.dpre_ref, ...), custom_call_target="tpu_custom_call" | custom-call | flops 235929600 | bytes 52428800 | tf_op jit(solution)/shard_map/scan_backward/pallas_call | solution.py:235
  659.3 19.5 %seq_sum.3 = f32[136,2048]{1,0:T(8,128)S(1)} custom-call(f32[136,2048]{1,0:T(8,128)S(1)} %maximum_maximum_fusion.p_ref), custom_call_target="tpu_custom_call" | custom-call | tf_op jit(solution)/shard_map/seq_sum/pallas_call | solution.py:832
  679.1 19.3 %multiply_reduce_fusion = (f32[400]{0:T(512)S(1)}, f32[400]{0:T(512)S(1)}, f32[400]{0:T(512)S(1)}, f32[400]{0:T(512)S(1)}, f32[400]{0:T(512)S(1)}, /*index=5*/f3...) fusion(f32[2048,400]{1,0:T(8,128)} %copy-done.34, f32[2048]{0:T(1024)S(1)} %copy-done.55, ...), kind=kOutput, calls=%fused_computation.59 | convolution fusion | flops 245758000 | bytes 31870784 | tf_op jit(solution)/shard_map/dot_general | solution.py:34
  726.8 34.4 %attention_backward.1 = (bf16[1600,256]{1,0:T(8,128)(2,1)S(1)}, bf16[320,2048]{1,0:T(8,128)(2,1)S(1)}, bf16[320,2048]{1,0:T(8,128)(2,1)}, bf16[8,172,400]{2,1,0:T(8,128)(2,1)}, bf16[8,172,200]{2,1,0:T(8,128)(2,1)S(1)}) custom-call(bf16[1600,256]{1,0:T(8,128)(2,1)S(1)} %copy-done.23, bf16[640,2048]{1,0:T(8,128)(2,1)} %convolution_convert_fusion.4.refs_1_.refs_2_, ...), custom_call_target="tpu_custom_call" | custom-call | flops 10485760000 | bytes 16777216 | tf_op jit(solution)/shard_map/attention_backward/pallas_call | solution.py:951
  768.5 24.2 %scatter_exchange.1 = (f32[80,2048]{1,0:T(8,128)S(1)}, bf16[8,200,256]{2,1,0:T(8,128)(2,1)S(1)}) custom-call(bf16[8,80,2048]{2,1,0:T(8,128)(2,1)S(1)} %bitcast.183, bf16[8,200,256]{2,1,0:T(8,128)(2,1)S(1)} %bitcast.187), custom_call_target="tpu_custom_call" | custom-call | tf_op jit(solution)/shard_map/scatter_exchange/pallas_call | solution.py:724
  804.5 14.7 %convolution_convert_fusion = bf16[1600,1080]{1,0:T(8,128)(2,1)} fusion(bf16[2048,1600]{1,0:T(8,128)(2,1)} %bitcast.205, bf16[2048,1080]{1,0:T(8,128)(2,1)} %concatenate.84.a_ref), kind=kOutput, calls=%fused_computation.12 | convolution fusion | flops 7079616000 | bytes 14433280 | tf_op jit(solution)/shard_map/dot_general | solution.py:34
  828.1 42.8 %product_scatter.5 = (f32[256,1600]{1,0:T(8,128)S(1)}, bf16[4,58,400]{2,1,0:T(8,128)(2,1)S(1)}, f32[4,24,400]{2,1,0:T(8,128)S(1)}, f32[4,2,1600]{2,1,0:T(2,128)S(1)}, bf16[8,150,200]{2,1,0:T(8,128)(2,1)S(1)}) custom-call(bf16[2048,1080]{1,0:T(8,128)(2,1)} %concatenate.84.a_ref, bf16[1600,1080]{1,0:T(8,128)(2,1)} %all-gather.9.cloned.1.call-done.w_ref, ...), custom_call_target="tpu_custom_call" | custom-call | flops 7077888000 | bytes 104857600 | tf_op jit(solution)/shard_map/product_scatter/pallas_call | solution.py:810
  879.0 11.9 %direct.12 = (bf16[8,50,58]{2,1,0:T(8,128)(2,1)S(1)}, f32[8,24,400]{2,1,0:T(8,128)S(1)}, f32[8,3,1600]{2,1,0:T(4,128)S(1)}) custom-call(bf16[8,50,58]{2,1,0:T(8,128)(2,1)S(1)} %copy.172.refs_0_, f32[24,400]{1,0:T(8,128)S(1)} %reduce_sum.260.refs_1_, f32[3,1600]{1,0:T(4,128)S(1)} %pad_maximum_fusion.5.refs_2_), custom_call_target="tpu_custom_call" | custom-call | tf_op jit(solution)/shard_map/direct/pallas_call | solution.py:677
  924.7 15.3 %direct.13 = bf16[8,135,400]{2,1,0:T(8,128)(2,1)S(1)} custom-call(bf16[8,135,400]{2,1,0:T(8,128)(2,1)S(1)} %reshape.566.refs_0_, f32[8,3,1600]{2,1,0:T(4,128)S(1)} %get-tuple-element.111.refs_1_), custom_call_target="tpu_custom_call" | custom-call | tf_op jit(solution)/shard_map/direct/pallas_call | solution.py:677
  (402 shorter events, 273.6 us)
Async XLA Ops:
  7.2 105.2 %all-gather.9.cloned.1.call-start = ((), (), s32[]{:S(2)}) async-start(), calls=%async_computation.5 | async-start | bytes 4608000 | tf_op jit(solution)/shard_map/all_gather | solution.py:1072
  7.3 188.8 %copy-start.58 = (s32[400]{0:T(512)}, s32[400]{0:T(512)S(1)}, u32[]{:S(2)}) copy-start(s32[400]{0:T(512)S(1)} %fusion.200) | copy-start | bytes 4804
  33.3 273.9 %all-gather.15.cloned.1.call-start = ((), (), s32[]{:S(2)}) async-start(), calls=%async_computation.12 | async-start | bytes 2529280 | tf_op jit(solution)/shard_map/all_gather | solution.py:1074
  112.4 256.9 %all-gather.17.cloned.1.call-start = ((), (), s32[]{:S(2)}) async-start(), calls=%async_computation.13 | async-start | bytes 2928640 | tf_op jit(solution)/shard_map/all_gather | solution.py:1075
  113.2 259.4 %all-gather.11.cloned.1.call-start = ((), (), s32[]{:S(2)}) async-start(), calls=%async_computation.6 | async-start | bytes 5632000 | tf_op jit(solution)/shard_map/all_gather | solution.py:1156
  120.6 35.3 %copy-start.82 = (s32[640]{0:T(1024)}, s32[640]{0:T(1024)S(1)}, u32[]{:S(2)}) copy-start(s32[640]{0:T(1024)S(1)} %fusion.187) | copy-start | bytes 7684
  120.6 158.1 %copy-start.72 = (s32[1600]{0:T(1024)}, s32[1600]{0:T(1024)S(1)}, u32[]{:S(2)}) copy-start(s32[1600]{0:T(1024)S(1)} %fusion.130) | copy-start | bytes 19204
  121.0 38.6 %copy-start.13 = (f32[1280,256]{1,0:T(8,128)}, f32[1280,256]{1,0:T(8,128)S(1)}, u32[]{:S(2)}) copy-start(f32[1280,256]{1,0:T(8,128)S(1)} %fusion.63.refs_3_.refs_5_) | copy-start | bytes 3932164
  193.6 220.7 %all-gather.13.cloned.1.call-start = ((), (), s32[]{:S(2)}) async-start(), calls=%async_computation.11 | async-start | bytes 7667712 | tf_op jit(solution)/shard_map/all_gather | solution.py:1202
  195.1 513.3 %reduce-scatter.12.cloned.1.call-start = ((), (), s32[]{:S(2)}) async-start(), calls=%async_computation.9 | async-start | bytes 2928640 | tf_op jit(solution)/shard_map/reduce_scatter | solution.py:1219
  243.8 34.9 %copy-start.66 = (f32[1600]{0:T(1024)S(1)}, f32[1600]{0:T(1024)}, u32[]{:S(2)}) copy-start(f32[1600]{0:T(1024)} %param.28) | copy-start | bytes 19204
  312.5 55.0 %copy-start.29 = (bf16[1,256,1600]{2,1,0:T(8,128)(2,1)S(1)}, bf16[1,256,1600]{2,1,0:T(8,128)(2,1)}, u32[]{:S(2)}) copy-start(bf16[1,256,1600]{2,1,0:T(8,128)(2,1)} %copy.141) | copy-start | bytes 2457604
  374.8 57.9 %slice-start = ((s8[4505600]{0:T(1024)(128)(4,1)}), s8[311296]{0:T(1024)(128)(4,1)S(1)}, s32[]{:S(2)}) async-start(s8[4505600]{0:T(1024)(128)(4,1)} %bitcast.175), calls=%async_computation.15 | async-start | bytes 622592
  432.7 39.8 %copy-start.28 = (f32[256,1600]{1,0:T(8,128)S(1)}, f32[256,1600]{1,0:T(8,128)}, u32[]{:S(2)}) copy-start(f32[256,1600]{1,0:T(8,128)} %copy-done.27) | copy-start | bytes 4915204
  517.4 195.3 %reduce-scatter.10.cloned.1.call-start = ((), (), s32[]{:S(2)}) async-start(), calls=%async_computation.8 | async-start | bytes 5632000 | tf_op jit(solution)/shard_map/reduce_scatter | solution.py:1217
  518.2 203.4 %reduce-scatter.8.cloned.1.call-start = ((), (), s32[]{:S(2)}) async-start(), calls=%async_computation.7 | async-start | bytes 7667712 | tf_op jit(solution)/shard_map/reduce_scatter | solution.py:1236
  570.6 255.1 %reduce-scatter.16.cloned.1.call-start = ((), (), s32[]{:S(2)}) async-start(), calls=%async_computation.14 | async-start | bytes 2529280
  584.7 71.3 %copy-start.26 = (bf16[2048,400]{1,0:T(8,128)(2,1)S(1)}, bf16[2048,400]{1,0:T(8,128)(2,1)}, u32[]{:S(2)}) copy-start(bf16[2048,400]{1,0:T(8,128)(2,1)} %copy-done.24) | copy-start | bytes 4915204
  584.7 71.3 %copy-start.33 = (f32[2048,400]{1,0:T(8,128)S(1)}, f32[2048,400]{1,0:T(8,128)}, u32[]{:S(2)}) copy-start(f32[2048,400]{1,0:T(8,128)} %get-tuple-element.248) | copy-start | bytes 9830404
  678.8 243.7 %reduce-scatter.14.cloned.1.call-start = ((), (), s32[]{:S(2)}) async-start(), calls=%async_computation.10 | async-start | bytes 4608000 | tf_op jit(solution)/shard_map/reduce_scatter | solution.py:1285
  726.8 34.5 %copy-start.83 = (s32[640]{0:T(1024)S(1)}, s32[640]{0:T(1024)}, u32[]{:S(2)}) copy-start(s32[640]{0:T(1024)} %copy-done.82) | copy-start | bytes 7684
  828.1 43.6 %copy-start.30 = (bf16[1,256,1600]{2,1,0:T(8,128)(2,1)S(1)}, bf16[1,256,1600]{2,1,0:T(8,128)(2,1)}, u32[]{:S(2)}) copy-start(bf16[1,256,1600]{2,1,0:T(8,128)(2,1)} %copy.141) | copy-start | bytes 2457604
  828.1 43.6 %copy-start.50 = (f32[1600]{0:T(1024)S(1)}, f32[1600]{0:T(1024)}, u32[]{:S(2)}) copy-start(f32[1600]{0:T(1024)} %param.26) | copy-start | bytes 19204
  828.1 43.6 %copy-start.65 = (f32[256]{0:T(256)S(1)}, f32[256]{0:T(256)}, u32[]{:S(2)}) copy-start(f32[256]{0:T(256)} %copy-done.64) | copy-start | bytes 3076
  (76 other events, 639.3 us)
Sparse Core Ops, SparseCore 0:
  33.4 78.9 all-gather.8
  114.0 43.0 all-gather.14
  159.2 49.0 all-gather.16
  210.3 84.7 all-gather.10
  297.3 64.5 all-gather.12
  517.5 45.5 reduce-scatter.11
  565.4 81.4 reduce-scatter.9
  650.8 64.7 reduce-scatter.7
  717.9 41.9 reduce-scatter.15
  819.3 75.2 reduce-scatter.13
